TPU v7x, 256 devices: a whole 4x4x8 slice. The times are simulated.
256 devices in a mesh: seq: 16 (over z_hi, x), tp: 4 (over y), batch: 4 (over z_lo, core).
Axes of the slice: x: 4, y: 4, z: 8 (z_hi: 4, z_lo: 2; z = z_hi * 2 + z_lo), core: 2. Of those that a mesh axis runs over, the one named last changes fastest.
Arguments:
- tokens: bfloat16 [8192, 3072], P(('batch', 'seq')), parts along dimension 0, may hold values from -6 to 6
- tangents: bfloat16 [8192, 3072], P(('batch', 'seq')), parts along dimension 0, may hold values from -6 to 6
- qkv_weight: bfloat16 [3072, 16, 3, 128], P('seq', 'tp'), may hold values from -0.109375 to 0.109375
- out_weight: bfloat16 [3072, 16, 128], P('seq', 'tp'), may hold values from -0.5 to 0.5
- mod_shift: float32 [12288], P('batch'), parts along dimension 0, may hold values from -3 to 3
- mod_scale: float32 [12288], P('batch'), parts along dimension 0, may hold values from -3 to 3
- mod_gate: float32 [12288], P('batch'), parts along dimension 0, may hold values from -8 to 8
- query_gain: float32 [128], replicated, may hold values from 0.5 to 2
- key_gain: float32 [128], replicated, may hold values from 0.5 to 2
Outputs:
- result: bfloat16 [8192, 3072], P(('batch', 'seq'), 'tp'), parts along dimension 0
- result_tangent: bfloat16 [8192, 3072], P(('batch', 'seq'), 'tp'), parts along dimension 0
There are 4 independent parts, one for each index of `batch`. A program takes and returns all parts, laid end to end along the dimension named above; an argument that names none is the same for every part. Nothing has to cross between parts.
All inputs are finite; a program needn't handle non-finite values.
Results may differ from a plain program's by a relative error of at most 0.017.
Values may be sent and summed in bfloat16 or wider, within the bound.
No kernel may reach another device: no remote copies, remote signals or barrier semaphores. Data moves between devices by JAX's collectives and lax.ppermute only.
A program may use at most 64 MiB of HBM per device.

v0:
```python
import functools

import jax
import jax.numpy as jnp
from jax import lax
from jax.experimental import pallas as pl
from jax.experimental.pallas import tpu as pltpu
from jax.sharding import Mesh, PartitionSpec as P

epsilon = 1e-06
MIB = 1 << 20
f32 = jnp.float32
bf16 = jnp.bfloat16


def dot_nt(a, b):
    return lax.dot_general(a, b, (((1,), (1,)), ((), ())), preferred_element_type=f32)


def modulate_kernel(y_ref, tok_ref, tan_ref, shift_ref, scale_ref, out_ref, quarter_ref):
    groups, _, _, width = out_ref.shape
    part = width // groups
    gain = 1.0 + scale_ref[...]
    values = tok_ref[...].astype(f32)
    dots = tan_ref[...].astype(f32)
    center = values - jnp.mean(values, axis=-1, keepdims=True)
    center_dot = dots - jnp.mean(dots, axis=-1, keepdims=True)
    spread = jnp.mean(center * center, axis=-1, keepdims=True)
    spread_dot = 2.0 * jnp.mean(center * center_dot, axis=-1, keepdims=True)
    root = lax.rsqrt(spread + epsilon)
    root_dot = -0.5 * root * root * root * spread_dot
    normed = (center * root * gain + shift_ref[...]).astype(bf16)
    normed_dot = ((center_dot * root + center * root_dot) * gain).astype(bf16)
    for high in range(groups):
        for low in range(groups):
            start = (high * groups + low) * part
            out_ref[low, 0, :, high * part : (high + 1) * part] = normed[:, start : start + part]
            out_ref[low, 1, :, high * part : (high + 1) * part] = normed_dot[:, start : start + part]
    quarter_ref[...] = out_ref[y_ref[0]]


def modulate(y, tokens, tangents, shift, scale):
    rows, width = tokens.shape
    step = 32
    token_spec = pl.BlockSpec((step, width), lambda i, s: (i, 0))
    whole_spec = pl.BlockSpec((1, width), lambda i, s: (0, 0))
    return pl.pallas_call(
        modulate_kernel,
        grid_spec=pltpu.PrefetchScalarGridSpec(
            num_scalar_prefetch=1,
            grid=(rows // step,),
            in_specs=[token_spec, token_spec, whole_spec, whole_spec],
            out_specs=[
                pl.BlockSpec((4, 2, step, width // 4), lambda i, s: (0, 0, i, 0)),
                pl.BlockSpec((2, step, width // 4), lambda i, s: (0, i, 0)),
            ],
        ),
        out_shape=[
            jax.ShapeDtypeStruct((4, 2, rows, width // 4), bf16),
            jax.ShapeDtypeStruct((2, rows, width // 4), bf16),
        ],
        compiler_params=pltpu.CompilerParams(vmem_limit_bytes=56 * MIB),
        cost_estimate=pl.CostEstimate(flops=20 * rows * width, bytes_accessed=8 * rows * width, transcendentals=0),
    )(y.reshape(1).astype(jnp.int32), tokens, tangents, shift.reshape(1, width), scale.reshape(1, width))


smem = pl.BlockSpec(memory_space=pltpu.SMEM)
vmem = pl.BlockSpec(memory_space=pltpu.VMEM)


def three_kernel(spot_ref, n0_ref, n1_ref, w0_ref, w1_ref, w3_ref, out_ref):
    x, s = spot_ref[0], spot_ref[1]
    for r, ref in enumerate((n0_ref, n1_ref)):
        total = None
        for n, w_ref in enumerate((w0_ref, w1_ref, w3_ref)):
            term = jnp.dot(ref[(x + (0, s, 4 - s)[n]) % 4], w_ref[...], preferred_element_type=f32)
            total = term if total is None else total + term
        out_ref[r] = total


def project_three(spot, parts, weights):
    shape = (2, parts[0].shape[1], weights[0].shape[1])
    return pl.pallas_call(
        three_kernel,
        in_specs=[smem] + [vmem] * 5,
        out_specs=vmem,
        out_shape=jax.ShapeDtypeStruct(shape, f32),
        compiler_params=pltpu.CompilerParams(vmem_limit_bytes=24 * MIB),
        cost_estimate=pl.CostEstimate(flops=2 * 3 * 768 * 512 * 384, bytes_accessed=6 * MIB, transcendentals=0),
    )(spot, *parts, *weights)


def last_kernel(spot_ref, n0_ref, n1_ref, n2_ref, n3_ref, w_ref, near_ref, far_ref, gain_ref, *refs):
    *out_refs, own_ref, held_ref = refs
    rows = n0_ref.shape[1] // 2
    for r, ref in enumerate((n0_ref, n1_ref, n2_ref, n3_ref)):
        before = near_ref[r] if r < 2 else far_ref[r - 2]
        total = before + jnp.dot(ref[0], w_ref[...], preferred_element_type=f32)
        for kind in range(3):
            part = total[:rows, kind * 128 : (kind + 1) * 128]
            part_dot = total[rows:, kind * 128 : (kind + 1) * 128]
            if kind < 2:
                root = lax.rsqrt(jnp.mean(part * part, axis=-1, keepdims=True) + epsilon)
                root_dot = -root * root * root * jnp.mean(part * part_dot, axis=-1, keepdims=True)
                gain = gain_ref[kind : kind + 1, :]
                part, part_dot = part * root * gain, (part_dot * root + part * root_dot) * gain
            at = (4, 0, 2)[kind]
            held_ref[r, at] = part.astype(bf16)
            held_ref[r, at + 1] = part_dot.astype(bf16)
    for k, ref in enumerate(out_refs):
        ref[...] = held_ref[spot_ref[1 + k], : ref.shape[0]]
    own_ref[...] = held_ref[spot_ref[1], 4:]


def project_last(spot, parts, weight, near, far, gains):
    groups, rows, depth = parts[0].shape
    whole = lambda shape: pl.BlockSpec(shape, lambda n, s: (0,) * len(shape))
    part_spec = pl.BlockSpec((1, rows, depth), lambda n, s: (s[0], 0, 0))
    extra = [weight, near, far, gains]
    shapes = [(4, rows // 2, 128)] + [(6, rows // 2, 128)] * 3 + [(2, rows // 2, 128)]
    return pl.pallas_call(
        last_kernel,
        grid_spec=pltpu.PrefetchScalarGridSpec(
            num_scalar_prefetch=1,
            grid=(1,),
            in_specs=[part_spec] * 4 + [whole(a.shape) for a in extra],
            out_specs=[whole(shape) for shape in shapes],
            scratch_shapes=[pltpu.VMEM((4, 6, rows // 2, 128), bf16)],
        ),
        out_shape=[jax.ShapeDtypeStruct(shape, bf16) for shape in shapes],
        compiler_params=pltpu.CompilerParams(vmem_limit_bytes=24 * MIB),
        cost_estimate=pl.CostEstimate(flops=8 * rows * depth * 384, bytes_accessed=5 * MIB, transcendentals=0),
    )(spot, *parts, *extra)


def attend_kernel(counts, spot_ref, *refs):
    kv_refs = refs[: len(counts)]
    own_refs = refs[len(counts) : len(counts) + 3]
    first_ref, *out_refs, q_cat, k_cat, v_cat, e_ref, sd_ref, held_ref = refs[len(counts) + 3 :]
    rows = 128
    for i, ref in enumerate((first_ref,) + own_refs):
        at = 0 if i == 0 else 4
        q_cat[i * rows : (i + 1) * rows, :128] = ref[at + 1]
        q_cat[i * rows : (i + 1) * rows, 128:] = ref[at]
    at = 0
    for count, ref in zip(counts + (1,) * 3, kv_refs + own_refs):
        for n in range(count):
            k_cat[at : at + rows, :128] = ref[4 * n]
            k_cat[at : at + rows, 128:] = ref[4 * n + 1]
            v_cat[at : at + rows, :128] = ref[4 * n + 2]
            v_cat[at : at + rows, 128:] = ref[4 * n + 3]
            at += rows
    inverse = 128.0 ** -0.5
    chunk = 256
    total_rows = q_cat.shape[0]
    weight_sum = jnp.zeros((total_rows, 128), f32)
    dot_sum = jnp.zeros((total_rows, 128), f32)
    for at in range(0, k_cat.shape[0], chunk):
        keys = k_cat[at : at + chunk, :]
        scores = dot_nt(q_cat[:, 128:], keys[:, :128])
        scores_dot = dot_nt(q_cat[...], keys)
        weights = jnp.exp2(scores * (inverse * 1.4426950408889634))
        e_ref[:, at : at + chunk] = weights
        sd_ref[:, at : at + chunk] = scores_dot
        both = weights * scores_dot
        weight_sum += weights[:, :128] + weights[:, 128:]
        dot_sum += both[:, :128] + both[:, 128:]
    scale = 1.0 / jnp.sum(weight_sum, axis=-1, keepdims=True)
    center = jnp.sum(dot_sum, axis=-1, keepdims=True) * scale
    summed = jnp.zeros((total_rows, 256), f32)
    summed_dot = jnp.zeros((total_rows, 128), f32)
    for at in range(0, k_cat.shape[0], chunk):
        weights = e_ref[:, at : at + chunk]
        weights_dot = (weights * (sd_ref[:, at : at + chunk] - center)).astype(bf16)
        values = v_cat[at : at + chunk, :]
        summed += jnp.dot(weights.astype(bf16), values, preferred_element_type=f32)
        summed_dot += jnp.dot(weights_dot, values[:, :128], preferred_element_type=f32)
    primal = (summed[:, :128] * scale).astype(bf16)
    tangent = ((summed[:, 128:] + summed_dot * inverse) * scale).astype(bf16)
    for i in range(4):
        held_ref[i, :rows] = primal[i * rows : (i + 1) * rows]
        held_ref[i, rows:] = tangent[i * rows : (i + 1) * rows]
    for i, ref in enumerate(out_refs):
        ref[...] = held_ref[spot_ref[i]]


def attend(spot, key_parts, own_parts, first_queries):
    counts = tuple(part.shape[0] // 4 for part in key_parts)
    keys = 128 * (sum(counts) + 3)
    return pl.pallas_call(
        functools.partial(attend_kernel, counts),
        in_specs=[smem] + [vmem] * (len(counts) + 4),
        out_specs=[vmem] * 4,
        out_shape=[jax.ShapeDtypeStruct((256, 128), bf16)] * 4,
        scratch_shapes=[
            pltpu.VMEM((512, 256), bf16),
            pltpu.VMEM((keys, 256), bf16),
            pltpu.VMEM((keys, 256), bf16),
            pltpu.VMEM((512, keys), f32),
            pltpu.VMEM((512, keys), f32),
            pltpu.VMEM((4, 256, 128), bf16),
        ],
        compiler_params=pltpu.CompilerParams(vmem_limit_bytes=24 * MIB),
        cost_estimate=pl.CostEstimate(
            flops=2 * 512 * keys * 128 * 6, bytes_accessed=3 * MIB, transcendentals=512 * keys
        ),
    )(spot, *key_parts, *own_parts, first_queries)


def terms_kernel(spot_ref, h0, h1, h2, h3, own_ref, other_ref, *out_refs):
    y, zh, c = (spot_ref[i] for i in range(3))
    *out_refs, held_ref = out_refs
    for i, ref in enumerate((h0, h1, h2, h3)):
        held_ref[i] = ref[...]
    lefts = []
    for first, w_ref in ((2 * c, own_ref), (2 - 2 * c, other_ref)):
        left = jnp.concatenate([held_ref[(zh - first + 4) % 4], held_ref[(zh - first + 3) % 4]], axis=1)
        lefts.append((left, w_ref))
    for k, ref in enumerate(out_refs):
        total = None
        for left, w_ref in lefts:
            weight = w_ref[(y + k) % 4].reshape(-1, left.shape[1])
            term = dot_nt(left, weight)
            total = term if total is None else total + term
        ref[...] = total.astype(ref.dtype)


def terms(spot, heads, own, other):
    rows, cols = heads[0].shape[0], own.shape[1] * own.shape[2]
    kinds = [f32, bf16, bf16, bf16]
    return pl.pallas_call(
        terms_kernel,
        in_specs=[smem] + [vmem] * 6,
        out_specs=[vmem] * 4,
        out_shape=[jax.ShapeDtypeStruct((rows, cols), kind) for kind in kinds],
        scratch_shapes=[pltpu.VMEM((4,) + heads[0].shape, bf16)],
        compiler_params=pltpu.CompilerParams(vmem_limit_bytes=24 * MIB),
        cost_estimate=pl.CostEstimate(flops=2 * rows * 4 * cols * 512, bytes_accessed=6 * MIB, transcendentals=0),
    )(spot, *heads, own, other)


def finish_kernel(t0, t1, t2, t3, tok_ref, tan_ref, gate_ref, out_ref, out_dot_ref):
    rows = tok_ref.shape[0]
    total = t0[...] + t1[...].astype(f32) + t2[...].astype(f32) + t3[...].astype(f32)
    gate = gate_ref[...]
    out_ref[...] = (tok_ref[...].astype(f32) + gate * total[:rows]).astype(bf16)
    out_dot_ref[...] = (tan_ref[...].astype(f32) + gate * total[rows:]).astype(bf16)


def finish(parts, tokens, tangents, gate):
    rows, cols = tokens.shape
    return pl.pallas_call(
        finish_kernel,
        in_specs=[vmem] * 7,
        out_specs=[vmem] * 2,
        out_shape=[jax.ShapeDtypeStruct((rows, cols), bf16)] * 2,
        compiler_params=pltpu.CompilerParams(vmem_limit_bytes=24 * MIB),
        cost_estimate=pl.CostEstimate(flops=8 * rows * cols, bytes_accessed=3 * MIB, transcendentals=0),
    )(*parts, tokens, tangents, gate)


def from_ahead(array, axis, k):
    if k % 4 == 0:
        return array
    return lax.ppermute(array, axis, [(i, (i - k) % 4) for i in range(4)])


def swap(array, axis):
    return lax.ppermute(array, axis, [(0, 1), (1, 0)])


def beside(array, axis, sign):
    perm = [(2 * i + core, 2 * ((i - sign * (1 - 2 * core)) % 4) + core) for i in range(4) for core in range(2)]
    return lax.ppermute(array, (axis, "c"), perm)


def pick(array, index, axis=0):
    return lax.dynamic_index_in_dim(array, index, axis, keepdims=False)


def place(pieces, positions):
    out = jnp.zeros((len(pieces),) + pieces[0].shape, pieces[0].dtype)
    for piece, position in zip(pieces, positions):
        out = lax.dynamic_update_index_in_dim(out, piece, position, 0)
    return out


def after(array, *others):
    return lax.optimization_barrier((array,) + others)[0]


def per_device(tokens, tangents, qkv_weight, out_weight, mod_shift, mod_scale, mod_gate, query_gain, key_gain):
    zh, x, y = (lax.axis_index(name) for name in ("zh", "x", "y"))
    zl, c = lax.axis_index("zl"), lax.axis_index("c")
    clip = 2 * zl + c
    rows, features = tokens.shape
    share = features // 4
    ahead = lambda base, k: (base + k) % 4

    side = 1 - 2 * c
    ring = lambda base: [base, (base + side) % 4, (base + 2) % 4, (base - side) % 4]

    normed, quarter = modulate(y, tokens, tangents, mod_shift, mod_scale)
    normed = normed.reshape(4, 2 * rows, share)
    own_weight = pick(qkv_weight, clip, 1).reshape(qkv_weight.shape[0], 384)
    half = lax.dynamic_slice_in_dim(out_weight, 2 * c, 2, 1).reshape(-1, 256)
    near = swap(normed, "c")
    quarter = swap(quarter.reshape(2 * rows, share), "zl")
    near, quarter, own_weight = lax.optimization_barrier((near, quarter, own_weight))

    far_own = lax.all_gather(quarter, "y")
    columns = place([from_ahead(own_weight, "zh", k) for k in range(4)], [ahead(zh, k) for k in range(4)])
    columns = columns.reshape(-1, 384)
    up, down = beside(columns, "x", 1), beside(columns, "x", -1)
    up, down = lax.optimization_barrier((up, down))
    opposite = beside(up, "x", 1)
    far_other = swap(after(far_own, up, down), "c")

    spot = jnp.stack([x, (side + 4) % 4]).astype(jnp.int32)
    three = [columns, up, down]
    near_total = project_three(spot, [normed, near], three)
    far_total = project_three(spot, [far_own, far_other], three)
    gains = jnp.stack([query_gain, key_gain])
    spot = jnp.stack([ahead(x, 2)] + [ahead(zh, k) ^ clip for k in range(4)]).astype(jnp.int32)
    first, *blocks, first_queries = project_last(
        spot, [normed, near, far_own, far_other], opposite, near_total, far_total, gains
    )

    own = lax.all_gather(after(half, up, down), ("zh", "x"))

    def along_x(group):
        return [from_ahead(group, "x", m) for m in range(1, 4)]

    got = {k: from_ahead(blocks[k - 1], "zh", -k) for k in (1, 3)}
    second = along_x(first)
    wave = lax.optimization_barrier((got[1], got[3], *second))
    got[1], got[3], second = wave[0], wave[1], wave[2:]
    got[2] = from_ahead(after(blocks[1], *wave), "zh", -2)
    third = along_x(jnp.concatenate([got[1][:4], got[3][:4]]))
    got[2], third[0] = lax.optimization_barrier((got[2], third[0]))
    fourth = along_x(got[2][:4])
    spot = jnp.stack([ahead(zh, -clip - i) for i in range(4)]).astype(jnp.int32)
    own = own.reshape(4, 4, -1, 256)
    attended = attend(spot, [first, *second, *third, *fourth], [got[k] for k in (1, 2, 3)], first_queries)
    other = swap(after(own, attended[0]), "c")

    heads = []
    for i in range(4):
        perm = [(a * 4 + j, ((j + i) % 4) * 4 + a) for a in range(4) for j in range(4)]
        heads.append(lax.ppermute(attended[i], ("zh", "zl", "c"), perm))
    spot = jnp.stack([y, zh, c]).astype(jnp.int32)
    sums = terms(spot, heads, own, other)
    sums = [from_ahead(part, "y", -k) for k, part in enumerate(sums)]

    offset = y * share
    tokens_part = lax.dynamic_slice_in_dim(tokens, offset, share, 1)
    tangents_part = lax.dynamic_slice_in_dim(tangents, offset, share, 1)
    gate_part = lax.dynamic_slice_in_dim(mod_gate, offset, share, 0).reshape(1, share)
    result, result_tangent = finish(sums, tokens_part, tangents_part, gate_part)
    return (result, result_tangent)


def solution(mesh):
    split = Mesh(mesh.devices.reshape(4, 4, 4, 2, 2), ("zh", "x", "y", "zl", "c"))
    rows = P(("zl", "c", "zh", "x"), None)
    clip = P(("zl", "c"))
    return jax.shard_map(
        per_device,
        mesh=split,
        in_specs=(
            rows,
            rows,
            P(("zh", "x"), "y", None, None),
            P(("zh", "x"), "y", None),
            clip,
            clip,
            clip,
            P(),
            P(),
        ),
        out_specs=(P(("zl", "c", "zh", "x"), "y"), P(("zl", "c", "zh", "x"), "y")),
        check_vma=False,
    )
```

profile of v0, /device:TPU:1, one launch (start us, length us, event | category | flops | bytes accessed | tf_op | source)
XLA Modules:
  0.0 172.5 jit_solution(1616446440973257220)
XLA Ops:
  7.2 4.7 %shard_map.104 = (bf16[4,2,128,768]{3,2,1,0:T(8,128)(2,1)}, bf16[2,128,768]{2,1,0:T(8,128)(2,1)}) custom-call(s32[1]{0:T(128)} %bitcast.y_ref, bf16[128,3072]{1,0:T(8,128)(2,1)} %tok_ref.1, bf16[128,3072]{1,0:T(8,128)(2,1)} %tan_ref.1, f32[1,3072]{1,0:T(1,128)} %bitcast.58, f32[1,3072]{1,0:T(1,128)} %bitcast.59), custom_call_target="tpu_custom_call" | custom-call | flops 7864320 | bytes 3145728 | tf_op jit(solution)/shard_map/pallas_call | solution.py:47
  11.9 3.2 %collective-permute-start = (bf16[4,256,768]{2,1,0:T(8,128)(2,1)}, bf16[4,256,768]{2,1,0:T(8,128)(2,1)}, u32[]{:S(2)}, u32[]{:S(2)}) collective-permute-start(bf16[4,256,768]{2,1,0:T(8,128)(2,1)} %bitcast.39), channel_id=1, source_target_pairs={{0,1},{1,0},{2,3},{3,2},{4,5},{5,4},{6,7},{7,6},{8,9},{9,8},{10,11... | collective-permute-start | bytes 4718600 | tf_op jit(solution)/shard_map/ppermute | solution.py:269
  15.2 1.0 dynamic-slice_reduce_fusion
  16.2 9.9 %collective-permute-done.1 = bf16[256,768]{1,0:T(8,128)(2,1)S(1)} collective-permute-done((bf16[256,768]{1,0:T(8,128)(2,1)}, bf16[256,768]{1,0:T(8,128)(2,1)S(1)}, u32[]{:S(2)}, u32[]{:S(2)}) %collective-permute-start.1) | collective-permute-done | bytes 393248 | tf_op jit(solution)/shard_map/ppermute | solution.py:269
  26.1 0.8 copy-done.4
  26.9 4.4 %collective-permute-start.2 = (bf16[192,384]{1,0:T(8,128)(2,1)S(1)}, bf16[192,384]{1,0:T(8,128)(2,1)S(1)}, u32[]{:S(2)}, u32[]{:S(2)}) collective-permute-start(bf16[192,384]{1,0:T(8,128)(2,1)S(1)} %bitcast.52), channel_id=1, source_target_pairs={{0,192},{64,0},{128,64},{192,128},{1,193},{65,1},{129,65},{193,129... | collective-permute-start | bytes 442376 | tf_op jit(solution)/shard_map/ppermute | solution.py:265
  31.3 1.0 collective-permute-start.3
  32.3 2.3 %collective-permute-start.4 = (bf16[192,384]{1,0:T(8,128)(2,1)S(1)}, bf16[192,384]{1,0:T(8,128)(2,1)S(1)}, u32[]{:S(2)}, u32[]{:S(2)}) collective-permute-start(bf16[192,384]{1,0:T(8,128)(2,1)S(1)} %bitcast.54), channel_id=1, source_target_pairs={{0,64},{64,128},{128,192},{192,0},{1,65},{65,129},{129,193},{193,1... | collective-permute-start | bytes 442376 | tf_op jit(solution)/shard_map/ppermute | solution.py:265
  34.7 3.5 %collective-permute-done.2 = bf16[192,384]{1,0:T(8,128)(2,1)S(1)} collective-permute-done((bf16[192,384]{1,0:T(8,128)(2,1)S(1)}, bf16[192,384]{1,0:T(8,128)(2,1)S(1)}, u32[]{:S(2)}, u32[]{:S(2)}) %collective-permute-start.2) | collective-permute-done | bytes 147488 | tf_op jit(solution)/shard_map/ppermute | solution.py:265
  38.2 5.1 %collective-permute-done.3 = bf16[192,384]{1,0:T(8,128)(2,1)S(1)} collective-permute-done((bf16[192,384]{1,0:T(8,128)(2,1)S(1)}, bf16[192,384]{1,0:T(8,128)(2,1)S(1)}, u32[]{:S(2)}, u32[]{:S(2)}) %collective-permute-start.3) | collective-permute-done | bytes 147488 | tf_op jit(solution)/shard_map/ppermute | solution.py:265
  43.3 1.6 collective-permute-start.5
  44.9 1.4 collective-permute-start.6
  47.1 7.4 %collective-permute-done.5.w1_ref = bf16[768,384]{1,0:T(8,128)(2,1)S(1)} collective-permute-done((bf16[768,384]{1,0:T(8,128)(2,1)S(1)}, bf16[768,384]{1,0:T(8,128)(2,1)S(1)}, u32[]{:S(2)}, u32[]{:S(2)}) %collective-permute-start.5) | collective-permute-done | bytes 589856 | tf_op jit(solution)/shard_map/ppermute | solution.py:274
  54.5 4.3 %collective-permute-done.6.w3_ref = bf16[768,384]{1,0:T(8,128)(2,1)} collective-permute-done((bf16[768,384]{1,0:T(8,128)(2,1)S(1)}, bf16[768,384]{1,0:T(8,128)(2,1)}, u32[]{:S(2)}, u32[]{:S(2)}) %collective-permute-start.6) | collective-permute-done | bytes 589856 | tf_op jit(solution)/shard_map/ppermute | solution.py:274
  58.9 1.9 %collective-permute-start.7 = (bf16[4,256,768]{2,1,0:T(8,128)(2,1)}, bf16[4,256,768]{2,1,0:T(8,128)(2,1)}, u32[]{:S(2)}, u32[]{:S(2)}) collective-permute-start(bf16[4,256,768]{2,1,0:T(8,128)(2,1)} %bitcast.42), channel_id=1, source_target_pairs={{0,1},{1,0},{2,3},{3,2},{4,5},{5,4},{6,7},{7,6},{8,9},{9,8},{10,11... | collective-permute-start | bytes 4718600 | tf_op jit(solution)/shard_map/ppermute | solution.py:269
  60.8 1.2 collective-permute-start.8
  62.2 3.0 %shard_map.105.near_ref = f32[2,256,384]{2,1,0:T(8,128)S(1)} custom-call(s32[2]{0:T(128)S(1)} %pad_add_fusion.2.spot_ref, bf16[4,256,768]{2,1,0:T(8,128)(2,1)S(1)} %bitcast.40, bf16[4,256,768]{2,1,0:T(8,128)(2,1)} %collective-permute-done.n1_ref, bf16[768,384]{1,0:T(8,128)(2,1)S(1)} %bitcast.47, bf16[768,384]{1,0:T(8,128)(2,1)S(1)} %collective-permute-done.5.w1_ref, ...), custom_call_target="tpu_custom_call" | custom-call | flops 905969664 | bytes 6291456 | tf_op jit(solution)/shard_map/pallas_call | solution.py:83
  65.3 2.9 %shard_map.106.far_ref = f32[2,256,384]{2,1,0:T(8,128)S(1)} custom-call(s32[2]{0:T(128)S(1)} %pad_add_fusion.2.spot_ref, bf16[4,256,768]{2,1,0:T(8,128)(2,1)S(1)} %bitcast.43, bf16[4,256,768]{2,1,0:T(8,128)(2,1)} %collective-permute-done.7.n1_ref.n3_ref, bf16[768,384]{1,0:T(8,128)(2,1)S(1)} %bitcast.48, bf16[768,384]{1,0:T(8,128)(2,1)S(1)} %collective-permute-done.5.w1_ref, ...), custom_call_target="tpu_custom_call" | custom-call | flops 905969664 | bytes 6291456 | tf_op jit(solution)/shard_map/pallas_call | solution.py:83
  68.3 2.6 %collective-permute-done.8.w_ref = bf16[768,384]{1,0:T(8,128)(2,1)} collective-permute-done((bf16[768,384]{1,0:T(8,128)(2,1)S(1)}, bf16[768,384]{1,0:T(8,128)(2,1)}, u32[]{:S(2)}, u32[]{:S(2)}) %collective-permute-start.8) | collective-permute-done | bytes 589856 | tf_op jit(solution)/shard_map/ppermute | solution.py:274
  70.9 3.0 %shard_map.107 = (bf16[4,128,128]{2,1,0:T(8,128)(2,1)S(1)}, bf16[6,128,128]{2,1,0:T(8,128)(2,1)S(1)}, bf16[6,128,128]{2,1,0:T(8,128)(2,1)S(1)}, bf16[6,128,128]{2,1,0:T(8,128)(2,1)S(1)}, bf16[2,128,128]{2,1,0:T(8,128)(2,1)S(1)}) custom-call(s32[5]{0:T(128)S(1)} %stack.77.spot_ref, bf16[4,256,768]{2,1,0:T(8,128)(2,1)S(1)} %bitcast.41, ...), custom_call_target="tpu_custom_call" | custom-call | flops 603979776 | bytes 5242880 | tf_op jit(solution)/shard_map/pallas_call | solution.py:121
  73.9 3.6 %collective-permute-start.9 = (bf16[6,128,128]{2,1,0:T(8,128)(2,1)S(1)}, bf16[6,128,128]{2,1,0:T(8,128)(2,1)S(1)}, u32[]{:S(2)}, u32[]{:S(2)}) collective-permute-start(bf16[6,128,128]{2,1,0:T(8,128)(2,1)S(1)} %get-tuple-element.42), channel_id=1, source_target_pairs={{0,64},{64,128},{128,192},{192,0},{1,65},{65,129},{129,193},{193,1... | collective-permute-start | bytes 589832 | tf_op jit(solution)/shard_map/ppermute | solution.py:265
  77.7 1.7 collective-permute-start.11
  80.1 1.9 %collective-permute-done.11.refs_1_ = bf16[4,128,128]{2,1,0:T(8,128)(2,1)S(1)} collective-permute-done((bf16[4,128,128]{2,1,0:T(8,128)(2,1)S(1)}, bf16[4,128,128]{2,1,0:T(8,128)(2,1)S(1)}, u32[]{:S(2)}, u32[]{:S(2)}) %collective-permute-start.11) | collective-permute-done | bytes 131104 | tf_op jit(solution)/shard_map/ppermute | solution.py:265
  82.0 2.8 %collective-permute-done.12.refs_2_ = bf16[4,128,128]{2,1,0:T(8,128)(2,1)S(1)} collective-permute-done((bf16[4,128,128]{2,1,0:T(8,128)(2,1)S(1)}, bf16[4,128,128]{2,1,0:T(8,128)(2,1)S(1)}, u32[]{:S(2)}, u32[]{:S(2)}) %collective-permute-start.12) | collective-permute-done | bytes 131104 | tf_op jit(solution)/shard_map/ppermute | solution.py:265
  84.8 1.6 collective-permute-done.13.refs_3_
  86.5 0.9 collective-permute-start.15
  87.4 5.7 %collective-permute-start.14 = (bf16[6,128,128]{2,1,0:T(8,128)(2,1)S(1)}, bf16[6,128,128]{2,1,0:T(8,128)(2,1)S(1)}, u32[]{:S(2)}, u32[]{:S(2)}) collective-permute-start(bf16[6,128,128]{2,1,0:T(8,128)(2,1)S(1)} %get-tuple-element.50), channel_id=1, source_target_pairs={{0,128},{64,192},{128,0},{192,64},{1,129},{65,193},{129,1},{193,65... | collective-permute-start | bytes 589832 | tf_op jit(solution)/shard_map/ppermute | solution.py:265
  93.9 2.8 %collective-permute-done.14.refs_11_ = bf16[6,128,128]{2,1,0:T(8,128)(2,1)S(1)} collective-permute-done((bf16[6,128,128]{2,1,0:T(8,128)(2,1)S(1)}, bf16[6,128,128]{2,1,0:T(8,128)(2,1)S(1)}, u32[]{:S(2)}, u32[]{:S(2)}) %collective-permute-start.14) | collective-permute-done | bytes 196640 | tf_op jit(solution)/shard_map/ppermute | solution.py:265
  96.7 3.6 %collective-permute-start.18 = (bf16[4,128,128]{2,1,0:T(8,128)(2,1)S(1)}, bf16[4,128,128]{2,1,0:T(8,128)(2,1)S(1)}, u32[]{:S(2)}, u32[]{:S(2)}) collective-permute-start(bf16[4,128,128]{2,1,0:T(8,128)(2,1)S(1)} %slice.11), channel_id=1, source_target_pairs={{0,48},{16,0},{32,16},{48,32},{1,49},{17,1},{33,17},{49,33},{2,50}... | collective-permute-start | bytes 393224 | tf_op jit(solution)/shard_map/ppermute | solution.py:265
  101.1 6.3 %collective-permute-done.17.refs_6_ = bf16[8,128,128]{2,1,0:T(8,128)(2,1)S(1)} collective-permute-done((bf16[8,128,128]{2,1,0:T(8,128)(2,1)S(1)}, bf16[8,128,128]{2,1,0:T(8,128)(2,1)S(1)}, u32[]{:S(2)}, u32[]{:S(2)}) %collective-permute-start.17) | collective-permute-done | bytes 262176 | tf_op jit(solution)/shard_map/ppermute | solution.py:265
  107.4 4.8 %collective-permute-done.20.refs_9_ = bf16[4,128,128]{2,1,0:T(8,128)(2,1)S(1)} collective-permute-done((bf16[4,128,128]{2,1,0:T(8,128)(2,1)S(1)}, bf16[4,128,128]{2,1,0:T(8,128)(2,1)S(1)}, u32[]{:S(2)}, u32[]{:S(2)}) %collective-permute-start.20) | collective-permute-done | bytes 131104 | tf_op jit(solution)/shard_map/ppermute | solution.py:265
  112.2 3.5 %shard_map.108 = (bf16[256,128]{1,0:T(8,128)(2,1)S(1)}, bf16[256,128]{1,0:T(8,128)(2,1)S(1)}, bf16[256,128]{1,0:T(8,128)(2,1)S(1)}, bf16[256,128]{1,0:T(8,128)(2,1)S(1)}) custom-call(s32[4]{0:T(128)S(1)} %pad_add_fusion.1.spot_ref, bf16[4,128,128]{2,1,0:T(8,128)(2,1)S(1)} %get-tuple-element.41.refs_0_, ...), custom_call_target="tpu_custom_call" | custom-call | flops 1610612736 | bytes 3145728 | tf_op jit(solution)/shard_map/pallas_call | solution.py:190
  115.7 7.5 %all-gather.7.cloned.1.call-done = bf16[3072,256]{1,0:T(8,128)(2,1)} async-done(((bf16[192,256]{1,0:T(8,128)(2,1)}), bf16[3072,256]{1,0:T(8,128)(2,1)}) %all-gather.7.cloned.1.call-update) | async-done | bytes 1572880 | tf_op jit(solution)/shard_map/all_gather | solution.py:329
  123.2 1.9 %collective-permute-start.25 = (bf16[4,4,192,256]{3,2,1,0:T(8,128)(2,1)}, bf16[4,4,192,256]{3,2,1,0:T(8,128)(2,1)S(1)}, u32[]{:S(2)}, u32[]{:S(2)}) collective-permute-start(bf16[4,4,192,256]{3,2,1,0:T(8,128)(2,1)} %bitcast.49), channel_id=1, source_target_pairs={{0,1},{1,0},{2,3},{3,2},{4,5},{5,4},{6,7},{7,6},{8,9},{9,8},{10,11... | collective-permute-start | bytes 4718600 | tf_op jit(solution)/shard_map/ppermute | solution.py:269
  125.1 3.1 %collective-permute-start.21 = (bf16[256,128]{1,0:T(8,128)(2,1)S(1)}, bf16[256,128]{1,0:T(8,128)(2,1)S(1)}, u32[]{:S(2)}, u32[]{:S(2)}) collective-permute-start(bf16[256,128]{1,0:T(8,128)(2,1)S(1)} %get-tuple-element.54), channel_id=1, source_target_pairs={{0,0},{1,64},{2,128},{3,192},{64,1},{65,65},{66,129},{67,193},{128... | collective-permute-start | bytes 196616 | tf_op jit(solution)/shard_map/ppermute | solution.py:350
  128.3 7.0 %collective-permute-start.22 = (bf16[256,128]{1,0:T(8,128)(2,1)S(1)}, bf16[256,128]{1,0:T(8,128)(2,1)S(1)}, u32[]{:S(2)}, u32[]{:S(2)}) collective-permute-start(bf16[256,128]{1,0:T(8,128)(2,1)S(1)} %get-tuple-element.55), channel_id=1, source_target_pairs={{0,64},{1,128},{2,192},{3,0},{64,65},{65,129},{66,193},{67,1},{128... | collective-permute-start | bytes 196616 | tf_op jit(solution)/shard_map/ppermute | solution.py:350
  135.9 1.2 collective-permute-done.22.h1
  137.1 3.7 %collective-permute-done.23.h2 = bf16[256,128]{1,0:T(8,128)(2,1)S(1)} collective-permute-done((bf16[256,128]{1,0:T(8,128)(2,1)S(1)}, bf16[256,128]{1,0:T(8,128)(2,1)S(1)}, u32[]{:S(2)}, u32[]{:S(2)}) %collective-permute-start.23) | collective-permute-done | bytes 65568 | tf_op jit(solution)/shard_map/ppermute | solution.py:350
  140.8 1.4 copy-done.3
  142.2 2.2 %shard_map.109 = (f32[256,768]{1,0:T(8,128)S(1)}, bf16[256,768]{1,0:T(8,128)(2,1)}, bf16[256,768]{1,0:T(8,128)(2,1)S(1)}, bf16[256,768]{1,0:T(8,128)(2,1)S(1)}) custom-call(s32[3]{0:T(128)S(1)} %pad_add_fusion.spot_ref, bf16[256,128]{1,0:T(8,128)(2,1)S(1)} %collective-permute-done.21.h0, bf16[256,128]{1,0:T(8,128)(2,1)S(1)} %collective-permute-done.22.h1, ...), custom_call_target="tpu_custom_call" | custom-call | flops 805306368 | bytes 6291456 | tf_op jit(solution)/shard_map/pallas_call | solution.py:231
  144.4 1.2 collective-permute-start.26
  145.6 2.1 %collective-permute-start.27 = (bf16[256,768]{1,0:T(8,128)(2,1)S(1)}, bf16[256,768]{1,0:T(8,128)(2,1)S(1)}, u32[]{:S(2)}, u32[]{:S(2)}) collective-permute-start(bf16[256,768]{1,0:T(8,128)(2,1)S(1)} %get-tuple-element.62), channel_id=1, source_target_pairs={{0,8},{4,12},{8,0},{12,4},{1,9},{5,13},{9,1},{13,5},{2,10},{6,14},... | collective-permute-start | bytes 1179656 | tf_op jit(solution)/shard_map/ppermute | solution.py:265
  147.7 1.3 collective-permute-start.28
  149.0 0.8 dynamic_slice.20
  149.8 1.0 constant_dynamic-slice_fusion
  150.8 5.4 %collective-permute-done.26.t1 = bf16[256,768]{1,0:T(8,128)(2,1)S(1)} collective-permute-done((bf16[256,768]{1,0:T(8,128)(2,1)}, bf16[256,768]{1,0:T(8,128)(2,1)S(1)}, u32[]{:S(2)}, u32[]{:S(2)}) %collective-permute-start.26) | collective-permute-done | bytes 393248 | tf_op jit(solution)/shard_map/ppermute | solution.py:265
  156.3 8.4 %collective-permute-done.27.t2 = bf16[256,768]{1,0:T(8,128)(2,1)S(1)} collective-permute-done((bf16[256,768]{1,0:T(8,128)(2,1)S(1)}, bf16[256,768]{1,0:T(8,128)(2,1)S(1)}, u32[]{:S(2)}, u32[]{:S(2)}) %collective-permute-start.27) | collective-permute-done | bytes 393248 | tf_op jit(solution)/shard_map/ppermute | solution.py:265
  164.7 0.9 shard_map.110
  (60 shorter events, 4.6 us)
Async XLA Ops:
  7.2 8.0 %copy-start = (bf16[192,4,3,128]{3,1,2,0:T(4,128)(2,1)S(1)}, bf16[192,4,3,128]{3,1,2,0:T(4,128)(2,1)}, u32[]{:S(2)}) copy-start(bf16[192,4,3,128]{3,1,2,0:T(4,128)(2,1)} %param.11) | copy-start | bytes 1769476
  7.2 51.7 %all-gather.5.cloned.1.call-start = ((), (), s32[]{:S(2)}) async-start(), calls=%async_computation | async-start | bytes 1966080 | tf_op jit(solution)/shard_map/all_gather | solution.py:311
  11.9 14.1 %collective-permute-start = (bf16[4,256,768]{2,1,0:T(8,128)(2,1)}, bf16[4,256,768]{2,1,0:T(8,128)(2,1)}, u32[]{:S(2)}, u32[]{:S(2)}) collective-permute-start(bf16[4,256,768]{2,1,0:T(8,128)(2,1)} %bitcast.39), channel_id=1, source_target_pairs={{0,1},{1,0},{2,3},{3,2},{4,5},{5,4},{6,7},{7,6},{8,9},{9,8},{10,11... | collective-permute-start | bytes 4718600 | tf_op jit(solution)/shard_map/ppermute | solution.py:269
  15.2 10.9 %collective-permute-start.1 = (bf16[256,768]{1,0:T(8,128)(2,1)}, bf16[256,768]{1,0:T(8,128)(2,1)S(1)}, u32[]{:S(2)}, u32[]{:S(2)}) collective-permute-start(bf16[256,768]{1,0:T(8,128)(2,1)} %bitcast.62), channel_id=1, source_target_pairs={{0,2},{2,0},{1,3},{3,1},{4,6},{6,4},{5,7},{7,5},{8,10},{10,8},{9,1... | collective-permute-start | bytes 1179656 | tf_op jit(solution)/shard_map/ppermute | solution.py:269
  15.2 31.1 %copy-start.5 = (bf16[192,4,128]{2,1,0:T(4,128)(2,1)S(1)}, bf16[192,4,128]{2,1,0:T(4,128)(2,1)}, u32[]{:S(2)}) copy-start(bf16[192,4,128]{2,1,0:T(4,128)(2,1)} %param.12) | copy-start | bytes 589828
  16.1 46.1 %copy-start.6 = (f32[128]{0:T(128)S(1)}, f32[128]{0:T(128)}, u32[]{:S(2)}) copy-start(f32[128]{0:T(128)} %param.17) | copy-start | bytes 1540
  16.1 46.1 %copy-start.7 = (f32[128]{0:T(128)S(1)}, f32[128]{0:T(128)}, u32[]{:S(2)}) copy-start(f32[128]{0:T(128)} %param.16) | copy-start | bytes 1540
  16.1 46.1 %copy-start.1 = (bf16[4,2,128,768]{3,2,1,0:T(8,128)(2,1)S(1)}, bf16[4,2,128,768]{3,2,1,0:T(8,128)(2,1)}, u32[]{:S(2)}) copy-start(bf16[4,2,128,768]{3,2,1,0:T(8,128)(2,1)} %get-tuple-element.33) | copy-start | bytes 4718596
  26.0 0.8 copy-start.4
  26.8 96.4 %all-gather.7.cloned.1.call-start = ((), (), s32[]{:S(2)}) async-start(), calls=%async_computation.1 | async-start | bytes 1671168 | tf_op jit(solution)/shard_map/all_gather | solution.py:329
  26.9 11.2 %collective-permute-start.2 = (bf16[192,384]{1,0:T(8,128)(2,1)S(1)}, bf16[192,384]{1,0:T(8,128)(2,1)S(1)}, u32[]{:S(2)}, u32[]{:S(2)}) collective-permute-start(bf16[192,384]{1,0:T(8,128)(2,1)S(1)} %bitcast.52), channel_id=1, source_target_pairs={{0,192},{64,0},{128,64},{192,128},{1,193},{65,1},{129,65},{193,129... | collective-permute-start | bytes 442376 | tf_op jit(solution)/shard_map/ppermute | solution.py:265
  31.3 12.0 %collective-permute-start.3 = (bf16[192,384]{1,0:T(8,128)(2,1)S(1)}, bf16[192,384]{1,0:T(8,128)(2,1)S(1)}, u32[]{:S(2)}, u32[]{:S(2)}) collective-permute-start(bf16[192,384]{1,0:T(8,128)(2,1)S(1)} %bitcast.53), channel_id=1, source_target_pairs={{0,128},{64,192},{128,0},{192,64},{1,129},{65,193},{129,1},{193,65... | collective-permute-start | bytes 442376 | tf_op jit(solution)/shard_map/ppermute | solution.py:265
  32.3 11.0 %collective-permute-start.4 = (bf16[192,384]{1,0:T(8,128)(2,1)S(1)}, bf16[192,384]{1,0:T(8,128)(2,1)S(1)}, u32[]{:S(2)}, u32[]{:S(2)}) collective-permute-start(bf16[192,384]{1,0:T(8,128)(2,1)S(1)} %bitcast.54), channel_id=1, source_target_pairs={{0,64},{64,128},{128,192},{192,0},{1,65},{65,129},{129,193},{193,1... | collective-permute-start | bytes 442376 | tf_op jit(solution)/shard_map/ppermute | solution.py:265
  43.3 11.1 %collective-permute-start.5 = (bf16[768,384]{1,0:T(8,128)(2,1)S(1)}, bf16[768,384]{1,0:T(8,128)(2,1)S(1)}, u32[]{:S(2)}, u32[]{:S(2)}) collective-permute-start(bf16[768,384]{1,0:T(8,128)(2,1)S(1)} %bitcast.45), channel_id=1, source_target_pairs={{0,48},{1,17},{16,0},{17,33},{32,16},{33,49},{48,32},{49,1},{2,50}... | collective-permute-start | bytes 1769480 | tf_op jit(solution)/shard_map/ppermute | solution.py:274
  44.9 13.9 %collective-permute-start.6 = (bf16[768,384]{1,0:T(8,128)(2,1)S(1)}, bf16[768,384]{1,0:T(8,128)(2,1)}, u32[]{:S(2)}, u32[]{:S(2)}) collective-permute-start(bf16[768,384]{1,0:T(8,128)(2,1)S(1)} %bitcast.46), channel_id=1, source_target_pairs={{0,16},{1,49},{16,32},{17,1},{32,48},{33,17},{48,0},{49,33},{2,18}... | collective-permute-start | bytes 1769480 | tf_op jit(solution)/shard_map/ppermute | solution.py:274
  58.9 6.4 %collective-permute-start.7 = (bf16[4,256,768]{2,1,0:T(8,128)(2,1)}, bf16[4,256,768]{2,1,0:T(8,128)(2,1)}, u32[]{:S(2)}, u32[]{:S(2)}) collective-permute-start(bf16[4,256,768]{2,1,0:T(8,128)(2,1)} %bitcast.42), channel_id=1, source_target_pairs={{0,1},{1,0},{2,3},{3,2},{4,5},{5,4},{6,7},{7,6},{8,9},{9,8},{10,11... | collective-permute-start | bytes 4718600 | tf_op jit(solution)/shard_map/ppermute | solution.py:269
  60.8 10.1 %collective-permute-start.8 = (bf16[768,384]{1,0:T(8,128)(2,1)S(1)}, bf16[768,384]{1,0:T(8,128)(2,1)}, u32[]{:S(2)}, u32[]{:S(2)}) collective-permute-start(bf16[768,384]{1,0:T(8,128)(2,1)S(1)} %collective-permute-done.5.w1_ref), channel_id=1, source_target_pairs={{0,48},{1,17},{16,0},{17,33},{32,16},{33,49},{48,32},{49,1},{2,50}... | collective-permute-start | bytes 1769480 | tf_op jit(solution)/shard_map/ppermute | solution.py:274
  62.2 3.1 %copy-start.2 = (bf16[1024,768]{1,0:T(8,128)(2,1)S(1)}, bf16[1024,768]{1,0:T(8,128)(2,1)}, u32[]{:S(2)}) copy-start(bf16[1024,768]{1,0:T(8,128)(2,1)} %all-gather.5.cloned.1.call-done) | copy-start | bytes 4718596
  73.9 12.6 %collective-permute-start.9 = (bf16[6,128,128]{2,1,0:T(8,128)(2,1)S(1)}, bf16[6,128,128]{2,1,0:T(8,128)(2,1)S(1)}, u32[]{:S(2)}, u32[]{:S(2)}) collective-permute-start(bf16[6,128,128]{2,1,0:T(8,128)(2,1)S(1)} %get-tuple-element.42), channel_id=1, source_target_pairs={{0,64},{64,128},{128,192},{192,0},{1,65},{65,129},{129,193},{193,1... | collective-permute-start | bytes 589832 | tf_op jit(solution)/shard_map/ppermute | solution.py:265
  77.4 9.0 %collective-permute-start.10 = (bf16[6,128,128]{2,1,0:T(8,128)(2,1)S(1)}, bf16[6,128,128]{2,1,0:T(8,128)(2,1)S(1)}, u32[]{:S(2)}, u32[]{:S(2)}) collective-permute-start(bf16[6,128,128]{2,1,0:T(8,128)(2,1)S(1)} %get-tuple-element.43), channel_id=1, source_target_pairs={{0,192},{64,0},{128,64},{192,128},{1,193},{65,1},{129,65},{193,129... | collective-permute-start | bytes 589832 | tf_op jit(solution)/shard_map/ppermute | solution.py:265
  77.7 4.3 %collective-permute-start.11 = (bf16[4,128,128]{2,1,0:T(8,128)(2,1)S(1)}, bf16[4,128,128]{2,1,0:T(8,128)(2,1)S(1)}, u32[]{:S(2)}, u32[]{:S(2)}) collective-permute-start(bf16[4,128,128]{2,1,0:T(8,128)(2,1)S(1)} %get-tuple-element.41.refs_0_), channel_id=1, source_target_pairs={{0,48},{16,0},{32,16},{48,32},{1,49},{17,1},{33,17},{49,33},{2,50}... | collective-permute-start | bytes 393224 | tf_op jit(solution)/shard_map/ppermute | solution.py:265
  79.4 5.4 %collective-permute-start.12 = (bf16[4,128,128]{2,1,0:T(8,128)(2,1)S(1)}, bf16[4,128,128]{2,1,0:T(8,128)(2,1)S(1)}, u32[]{:S(2)}, u32[]{:S(2)}) collective-permute-start(bf16[4,128,128]{2,1,0:T(8,128)(2,1)S(1)} %get-tuple-element.41.refs_0_), channel_id=1, source_target_pairs={{0,32},{16,48},{32,0},{48,16},{1,33},{17,49},{33,1},{49,17},{2,34}... | collective-permute-start | bytes 393224 | tf_op jit(solution)/shard_map/ppermute | solution.py:265
  79.8 6.6 %collective-permute-start.13 = (bf16[4,128,128]{2,1,0:T(8,128)(2,1)S(1)}, bf16[4,128,128]{2,1,0:T(8,128)(2,1)S(1)}, u32[]{:S(2)}, u32[]{:S(2)}) collective-permute-start(bf16[4,128,128]{2,1,0:T(8,128)(2,1)S(1)} %get-tuple-element.41.refs_0_), channel_id=1, source_target_pairs={{0,16},{16,32},{32,48},{48,0},{1,17},{17,33},{33,49},{49,1},{2,18}... | collective-permute-start | bytes 393224 | tf_op jit(solution)/shard_map/ppermute | solution.py:265
  86.5 10.2 %collective-permute-start.15 = (bf16[8,128,128]{2,1,0:T(8,128)(2,1)S(1)}, bf16[8,128,128]{2,1,0:T(8,128)(2,1)S(1)}, u32[]{:S(2)}, u32[]{:S(2)}) collective-permute-start(bf16[8,128,128]{2,1,0:T(8,128)(2,1)S(1)} %pad_maximum_fusion), channel_id=1, source_target_pairs={{0,48},{16,0},{32,16},{48,32},{1,49},{17,1},{33,17},{49,33},{2,50}... | collective-permute-start | bytes 786440 | tf_op jit(solution)/shard_map/ppermute | solution.py:265
  87.4 9.3 %collective-permute-start.14 = (bf16[6,128,128]{2,1,0:T(8,128)(2,1)S(1)}, bf16[6,128,128]{2,1,0:T(8,128)(2,1)S(1)}, u32[]{:S(2)}, u32[]{:S(2)}) collective-permute-start(bf16[6,128,128]{2,1,0:T(8,128)(2,1)S(1)} %get-tuple-element.50), channel_id=1, source_target_pairs={{0,128},{64,192},{128,0},{192,64},{1,129},{65,193},{129,1},{193,65... | collective-permute-start | bytes 589832 | tf_op jit(solution)/shard_map/ppermute | solution.py:265
  93.1 8.0 %collective-permute-start.16 = (bf16[8,128,128]{2,1,0:T(8,128)(2,1)S(1)}, bf16[8,128,128]{2,1,0:T(8,128)(2,1)S(1)}, u32[]{:S(2)}, u32[]{:S(2)}) collective-permute-start(bf16[8,128,128]{2,1,0:T(8,128)(2,1)S(1)} %pad_maximum_fusion), channel_id=1, source_target_pairs={{0,32},{16,48},{32,0},{48,16},{1,33},{17,49},{33,1},{49,17},{2,34}... | collective-permute-start | bytes 786440 | tf_op jit(solution)/shard_map/ppermute | solution.py:265
  93.4 14.0 %collective-permute-start.17 = (bf16[8,128,128]{2,1,0:T(8,128)(2,1)S(1)}, bf16[8,128,128]{2,1,0:T(8,128)(2,1)S(1)}, u32[]{:S(2)}, u32[]{:S(2)}) collective-permute-start(bf16[8,128,128]{2,1,0:T(8,128)(2,1)S(1)} %pad_maximum_fusion), channel_id=1, source_target_pairs={{0,16},{16,32},{32,48},{48,0},{1,17},{17,33},{33,49},{49,1},{2,18}... | collective-permute-start | bytes 786440 | tf_op jit(solution)/shard_map/ppermute | solution.py:265
  96.7 10.7 %collective-permute-start.18 = (bf16[4,128,128]{2,1,0:T(8,128)(2,1)S(1)}, bf16[4,128,128]{2,1,0:T(8,128)(2,1)S(1)}, u32[]{:S(2)}, u32[]{:S(2)}) collective-permute-start(bf16[4,128,128]{2,1,0:T(8,128)(2,1)S(1)} %slice.11), channel_id=1, source_target_pairs={{0,48},{16,0},{32,16},{48,32},{1,49},{17,1},{33,17},{49,33},{2,50}... | collective-permute-start | bytes 393224 | tf_op jit(solution)/shard_map/ppermute | solution.py:265
  100.3 7.1 %collective-permute-start.19 = (bf16[4,128,128]{2,1,0:T(8,128)(2,1)S(1)}, bf16[4,128,128]{2,1,0:T(8,128)(2,1)S(1)}, u32[]{:S(2)}, u32[]{:S(2)}) collective-permute-start(bf16[4,128,128]{2,1,0:T(8,128)(2,1)S(1)} %slice.11), channel_id=1, source_target_pairs={{0,32},{16,48},{32,0},{48,16},{1,33},{17,49},{33,1},{49,17},{2,34}... | collective-permute-start | bytes 393224 | tf_op jit(solution)/shard_map/ppermute | solution.py:265
  100.3 11.9 %collective-permute-start.20 = (bf16[4,128,128]{2,1,0:T(8,128)(2,1)S(1)}, bf16[4,128,128]{2,1,0:T(8,128)(2,1)S(1)}, u32[]{:S(2)}, u32[]{:S(2)}) collective-permute-start(bf16[4,128,128]{2,1,0:T(8,128)(2,1)S(1)} %slice.11), channel_id=1, source_target_pairs={{0,16},{16,32},{32,48},{48,0},{1,17},{17,33},{33,49},{49,1},{2,18}... | collective-permute-start | bytes 393224 | tf_op jit(solution)/shard_map/ppermute | solution.py:265
  123.2 17.6 %collective-permute-start.25 = (bf16[4,4,192,256]{3,2,1,0:T(8,128)(2,1)}, bf16[4,4,192,256]{3,2,1,0:T(8,128)(2,1)S(1)}, u32[]{:S(2)}, u32[]{:S(2)}) collective-permute-start(bf16[4,4,192,256]{3,2,1,0:T(8,128)(2,1)} %bitcast.49), channel_id=1, source_target_pairs={{0,1},{1,0},{2,3},{3,2},{4,5},{5,4},{6,7},{7,6},{8,9},{9,8},{10,11... | collective-permute-start | bytes 4718600 | tf_op jit(solution)/shard_map/ppermute | solution.py:269
  125.1 10.7 %collective-permute-start.21 = (bf16[256,128]{1,0:T(8,128)(2,1)S(1)}, bf16[256,128]{1,0:T(8,128)(2,1)S(1)}, u32[]{:S(2)}, u32[]{:S(2)}) collective-permute-start(bf16[256,128]{1,0:T(8,128)(2,1)S(1)} %get-tuple-element.54), channel_id=1, source_target_pairs={{0,0},{1,64},{2,128},{3,192},{64,1},{65,65},{66,129},{67,193},{128... | collective-permute-start | bytes 196616 | tf_op jit(solution)/shard_map/ppermute | solution.py:350
  128.3 8.8 %collective-permute-start.22 = (bf16[256,128]{1,0:T(8,128)(2,1)S(1)}, bf16[256,128]{1,0:T(8,128)(2,1)S(1)}, u32[]{:S(2)}, u32[]{:S(2)}) collective-permute-start(bf16[256,128]{1,0:T(8,128)(2,1)S(1)} %get-tuple-element.55), channel_id=1, source_target_pairs={{0,64},{1,128},{2,192},{3,0},{64,65},{65,129},{66,193},{67,1},{128... | collective-permute-start | bytes 196616 | tf_op jit(solution)/shard_map/ppermute | solution.py:350
  135.3 5.5 %collective-permute-start.23 = (bf16[256,128]{1,0:T(8,128)(2,1)S(1)}, bf16[256,128]{1,0:T(8,128)(2,1)S(1)}, u32[]{:S(2)}, u32[]{:S(2)}) collective-permute-start(bf16[256,128]{1,0:T(8,128)(2,1)S(1)} %get-tuple-element.56), channel_id=1, source_target_pairs={{0,128},{1,192},{2,0},{3,64},{64,129},{65,193},{66,1},{67,65},{128... | collective-permute-start | bytes 196616 | tf_op jit(solution)/shard_map/ppermute | solution.py:350
  135.3 5.5 %collective-permute-start.24 = (bf16[256,128]{1,0:T(8,128)(2,1)S(1)}, bf16[256,128]{1,0:T(8,128)(2,1)S(1)}, u32[]{:S(2)}, u32[]{:S(2)}) collective-permute-start(bf16[256,128]{1,0:T(8,128)(2,1)S(1)} %get-tuple-element.57), channel_id=1, source_target_pairs={{0,192},{1,0},{2,64},{3,128},{64,193},{65,1},{66,65},{67,129},{128... | collective-permute-start | bytes 196616 | tf_op jit(solution)/shard_map/ppermute | solution.py:350
  140.8 1.4 copy-start.3
  144.4 11.9 %collective-permute-start.26 = (bf16[256,768]{1,0:T(8,128)(2,1)}, bf16[256,768]{1,0:T(8,128)(2,1)S(1)}, u32[]{:S(2)}, u32[]{:S(2)}) collective-permute-start(bf16[256,768]{1,0:T(8,128)(2,1)} %get-tuple-element.61), channel_id=1, source_target_pairs={{0,4},{4,8},{8,12},{12,0},{1,5},{5,9},{9,13},{13,1},{2,6},{6,10},{... | collective-permute-start | bytes 1179656 | tf_op jit(solution)/shard_map/ppermute | solution.py:265
  145.6 19.1 %collective-permute-start.27 = (bf16[256,768]{1,0:T(8,128)(2,1)S(1)}, bf16[256,768]{1,0:T(8,128)(2,1)S(1)}, u32[]{:S(2)}, u32[]{:S(2)}) collective-permute-start(bf16[256,768]{1,0:T(8,128)(2,1)S(1)} %get-tuple-element.62), channel_id=1, source_target_pairs={{0,8},{4,12},{8,0},{12,4},{1,9},{5,13},{9,1},{13,5},{2,10},{6,14},... | collective-permute-start | bytes 1179656 | tf_op jit(solution)/shard_map/ppermute | solution.py:265
  147.7 17.0 %collective-permute-start.28 = (bf16[256,768]{1,0:T(8,128)(2,1)S(1)}, bf16[256,768]{1,0:T(8,128)(2,1)S(1)}, u32[]{:S(2)}, u32[]{:S(2)}) collective-permute-start(bf16[256,768]{1,0:T(8,128)(2,1)S(1)} %get-tuple-element.63), channel_id=1, source_target_pairs={{0,12},{4,0},{8,4},{12,8},{1,13},{5,1},{9,5},{13,9},{2,14},{6,2},{... | collective-permute-start | bytes 1179656 | tf_op jit(solution)/shard_map/ppermute | solution.py:265
Sparse Core Ops, SparseCore 0:
  27.0 30.5 all-gather.4
  60.5 62.6 all-gather.6
where the time goes:
time: 173 us; the launch traced here: 172 us
  waiting for transfers between devices  79.5 us (46%)
  starting transfers between devices  52.2 us (30%)
  Pallas kernels  20.2 us (12%)
  between operations  14.3 us (8%)
  local copies, waits for them, and re-layouts  6.04 us (3%)
    ppermute x18, waiting for transfers between devices, from_ahead(): return lax.ppermute(array, axis, [(i, (i - k) % 4) for i in range(4)])  42.7 us
    ppermute x18, starting transfers between devices, from_ahead(): return lax.ppermute(array, axis, [(i, (i - k) % 4) for i in range(4)])  30.2 us
    ppermute x3, waiting for transfers between devices, beside(): return lax.ppermute(array, (axis, 'c'), perm)  14.4 us
    ppermute x4, starting transfers between devices, per_device(): heads.append(lax.ppermute(attended[i], ('zh', 'zl', 'c'), perm))  10.6 us
    ppermute x4, waiting for transfers between devices, swap(): return lax.ppermute(array, axis, [(0, 1), (1, 0)])  9.86 us
    all_gather x1, waiting for transfers between devices, per_device(): own = lax.all_gather(after(half, up, down), ('zh', 'x'))  7.54 us
    ppermute x4, starting transfers between devices, swap(): return lax.ppermute(array, axis, [(0, 1), (1, 0)])  7.1 us
    pallas_call x2, Pallas kernels, project_three(): pl.pallas_call(three_kernel, in_specs=[smem] + [vmem] * 5, out_specs=vmem...  5.98 us
  transfers between devices with their start and end apart: 31, of which 17 were waited for; matrix products, arithmetic and copies ran while one was open for 2% of the time, Pallas kernels for 7%

commit v1 on v0

--- a/solution.py
+++ b/solution.py
@@ -207,56 +207,41 @@
     )(spot, *key_parts, *own_parts, first_queries)
 
 
-def terms_kernel(spot_ref, h0, h1, h2, h3, own_ref, other_ref, *out_refs):
-    y, zh, c = (spot_ref[i] for i in range(3))
-    *out_refs, held_ref = out_refs
-    for i, ref in enumerate((h0, h1, h2, h3)):
-        held_ref[i] = ref[...]
-    lefts = []
-    for first, w_ref in ((2 * c, own_ref), (2 - 2 * c, other_ref)):
-        left = jnp.concatenate([held_ref[(zh - first + 4) % 4], held_ref[(zh - first + 3) % 4]], axis=1)
-        lefts.append((left, w_ref))
-    for k, ref in enumerate(out_refs):
-        total = None
-        for left, w_ref in lefts:
-            weight = w_ref[(y + k) % 4].reshape(-1, left.shape[1])
-            term = dot_nt(left, weight)
-            total = term if total is None else total + term
-        ref[...] = total.astype(ref.dtype)
-
-
-def terms(spot, heads, own, other):
-    rows, cols = heads[0].shape[0], own.shape[1] * own.shape[2]
-    kinds = [f32, bf16, bf16, bf16]
-    return pl.pallas_call(
-        terms_kernel,
-        in_specs=[smem] + [vmem] * 6,
-        out_specs=[vmem] * 4,
-        out_shape=[jax.ShapeDtypeStruct((rows, cols), kind) for kind in kinds],
-        scratch_shapes=[pltpu.VMEM((4,) + heads[0].shape, bf16)],
-        compiler_params=pltpu.CompilerParams(vmem_limit_bytes=24 * MIB),
-        cost_estimate=pl.CostEstimate(flops=2 * rows * 4 * cols * 512, bytes_accessed=6 * MIB, transcendentals=0),
-    )(spot, *heads, own, other)
-
-
-def finish_kernel(t0, t1, t2, t3, tok_ref, tan_ref, gate_ref, out_ref, out_dot_ref):
+def finish_kernel(place_ref, h0, h1, h2, h3, own_ref, other_ref, tok_ref, tan_ref, gate_ref, out_ref, out_dot_ref):
     rows = tok_ref.shape[0]
-    total = t0[...] + t1[...].astype(f32) + t2[...].astype(f32) + t3[...].astype(f32)
+    y, zh, c = (place_ref[i] for i in range(3))
+    totals = [None] * own_ref.shape[1]
+    for m, ref in enumerate((h0, h1, h2, h3)):
+        for first, w_ref in ((2 * c, own_ref), (2 - 2 * c, other_ref)):
+            left = jnp.concatenate([ref[(zh - first + 4) % 4], ref[(zh - first + 3) % 4]], axis=1)
+            for b in range(len(totals)):
+                term = dot_nt(left, w_ref[(y + m) % 4, b])
+                totals[b] = term if totals[b] is None else totals[b] + term
+    total = jnp.concatenate(totals, axis=1)
     gate = gate_ref[...]
     out_ref[...] = (tok_ref[...].astype(f32) + gate * total[:rows]).astype(bf16)
     out_dot_ref[...] = (tan_ref[...].astype(f32) + gate * total[rows:]).astype(bf16)
 
 
-def finish(parts, tokens, tangents, gate):
+def finish(place, parts, own, other, tokens, tangents, gate):
     rows, cols = tokens.shape
+    step = cols // 2
+    part_spec = pl.BlockSpec(parts[0].shape, lambda n, s: (0, 0, 0))
+    col_spec = pl.BlockSpec((rows, step), lambda n, s: (0, n))
+    weight_spec = pl.BlockSpec((4, 2) + own.shape[2:], lambda n, s: (0, n, 0, 0))
     return pl.pallas_call(
         finish_kernel,
-        in_specs=[vmem] * 7,
-        out_specs=[vmem] * 2,
+        grid_spec=pltpu.PrefetchScalarGridSpec(
+            num_scalar_prefetch=1,
+            grid=(2,),
+            in_specs=[part_spec] * 4
+            + [weight_spec, weight_spec, col_spec, col_spec, pl.BlockSpec((1, step), lambda n, s: (0, n))],
+            out_specs=[col_spec, col_spec],
+        ),
         out_shape=[jax.ShapeDtypeStruct((rows, cols), bf16)] * 2,
-        compiler_params=pltpu.CompilerParams(vmem_limit_bytes=24 * MIB),
-        cost_estimate=pl.CostEstimate(flops=8 * rows * cols, bytes_accessed=3 * MIB, transcendentals=0),
-    )(*parts, tokens, tangents, gate)
+        compiler_params=pltpu.CompilerParams(vmem_limit_bytes=56 * MIB),
+        cost_estimate=pl.CostEstimate(flops=4 * rows * cols * 2048, bytes_accessed=6 * MIB, transcendentals=0),
+    )(place, *parts, own, other, tokens, tangents, gate)
 
 
 def from_ahead(array, axis, k):
@@ -312,7 +297,9 @@
     columns = place([from_ahead(own_weight, "zh", k) for k in range(4)], [ahead(zh, k) for k in range(4)])
     columns = columns.reshape(-1, 384)
     up, down = beside(columns, "x", 1), beside(columns, "x", -1)
-    up, down = lax.optimization_barrier((up, down))
+    half = after(half, columns)
+    half = lax.ppermute(half, ("zh", "y"), [(a * 4 + b, b * 4 + a) for a in range(4) for b in range(4)])
+    up, down, half = lax.optimization_barrier((up, down, half))
     opposite = beside(up, "x", 1)
     far_other = swap(after(far_own, up, down), "c")
 
@@ -326,7 +313,7 @@
         spot, [normed, near, far_own, far_other], opposite, near_total, far_total, gains
     )
 
-    own = lax.all_gather(after(half, up, down), ("zh", "x"))
+    half_rows = lax.all_gather(half, ("zh", "x"))
 
     def along_x(group):
         return [from_ahead(group, "x", m) for m in range(1, 4)]
@@ -340,23 +327,23 @@
     got[2], third[0] = lax.optimization_barrier((got[2], third[0]))
     fourth = along_x(got[2][:4])
     spot = jnp.stack([ahead(zh, -clip - i) for i in range(4)]).astype(jnp.int32)
-    own = own.reshape(4, 4, -1, 256)
     attended = attend(spot, [first, *second, *third, *fourth], [got[k] for k in (1, 2, 3)], first_queries)
-    other = swap(after(own, attended[0]), "c")
 
     heads = []
     for i in range(4):
         perm = [(a * 4 + j, ((j + i) % 4) * 4 + a) for a in range(4) for j in range(4)]
         heads.append(lax.ppermute(attended[i], ("zh", "zl", "c"), perm))
-    spot = jnp.stack([y, zh, c]).astype(jnp.int32)
-    sums = terms(spot, heads, own, other)
-    sums = [from_ahead(part, "y", -k) for k, part in enumerate(sums)]
+    heads = jnp.stack(heads)
+    all_heads = [from_ahead(heads, "y", m) for m in range(4)]
+    own = half_rows.reshape(4, 4, -1, 256)
+    other = swap(after(own, heads), "c")
 
     offset = y * share
     tokens_part = lax.dynamic_slice_in_dim(tokens, offset, share, 1)
     tangents_part = lax.dynamic_slice_in_dim(tangents, offset, share, 1)
     gate_part = lax.dynamic_slice_in_dim(mod_gate, offset, share, 0).reshape(1, share)
-    result, result_tangent = finish(sums, tokens_part, tangents_part, gate_part)
+    spot = jnp.stack([y, zh, c]).astype(jnp.int32)
+    result, result_tangent = finish(spot, all_heads, own, other, tokens_part, tangents_part, gate_part)
     return (result, result_tangent)
 
 

time: 173 us -> 171 us (0.988)
  starting transfers between devices: 52.2 us -> 41.7 us
  waiting for transfers between devices: 79.5 us -> 84.9 us
    ppermute x18, waiting for transfers between devices: 42.7 us -> 55.9 us  [from_ahead(): return lax.ppermute(array, axis, [(i, (i - k) % 4) for i in range(4)])]
    ppermute x18, starting transfers between devices: 30.2 us -> 22.1 us  [from_ahead(): return lax.ppermute(array, axis, [(i, (i - k) % 4) for i in range(4)])]
    all_gather x1, waiting for transfers between devices: 7.54 us -> 0.02 us  [per_device(): half_rows = lax.all_gather(half, ('zh', 'x'))]
    ppermute x4, starting transfers between devices: 10.6 us -> 7.84 us  [per_device(): heads.append(lax.ppermute(attended[i], ('zh', 'zl', 'c'), perm))]
    pallas_call x2 -> x1, Pallas kernels: 3.12 us -> 4.69 us  [finish(): pl.pallas_call(finish_kernel, grid_spec=pltpu.PrefetchScalarGridSpec(num_...]
  transfers between devices with their start and end apart: 31 -> 32, of which waited for: 17 -> 20; matrix products, arithmetic and copies ran while one was open for 2% -> 3% of each run, Pallas kernels for 7% -> 7%
where the time goes in v1:
time: 171 us; the launch traced here: 170 us
  waiting for transfers between devices  84.9 us (50%)
  starting transfers between devices  41.7 us (24%)
  Pallas kernels  21.7 us (13%)
  between operations  14.4 us (8%)
  local copies, waits for them, and re-layouts  6.55 us (4%)
    ppermute x18, waiting for transfers between devices, from_ahead(): return lax.ppermute(array, axis, [(i, (i - k) % 4) for i in range(4)])  55.9 us
    ppermute x18, starting transfers between devices, from_ahead(): return lax.ppermute(array, axis, [(i, (i - k) % 4) for i in range(4)])  22.1 us
    ppermute x3, waiting for transfers between devices, beside(): return lax.ppermute(array, (axis, 'c'), perm)  14.3 us
    ppermute x4, waiting for transfers between devices, swap(): return lax.ppermute(array, axis, [(0, 1), (1, 0)])  9.86 us
    ppermute x4, starting transfers between devices, per_device(): heads.append(lax.ppermute(attended[i], ('zh', 'zl', 'c'), perm))  7.84 us
    ppermute x4, starting transfers between devices, swap(): return lax.ppermute(array, axis, [(0, 1), (1, 0)])  6.94 us
    pallas_call x2, Pallas kernels, project_three(): pl.pallas_call(three_kernel, in_specs=[smem] + [vmem] * 5, out_specs=vmem...  5.99 us
    ppermute x4, waiting for transfers between devices, per_device(): heads.append(lax.ppermute(attended[i], ('zh', 'zl', 'c'), perm))  4.8 us
  transfers between devices with their start and end apart: 32, of which 20 were waited for; matrix products, arithmetic and copies ran while one was open for 3% of the time, Pallas kernels for 7%

profile of v1, /device:TPU:1, one launch (start us, length us, event | category | flops | bytes accessed | tf_op | source)
XLA Modules:
  0.0 170.3 jit_solution(12537381892113424273)
XLA Ops:
  7.2 4.6 %shard_map.104 = (bf16[4,2,128,768]{3,2,1,0:T(8,128)(2,1)}, bf16[2,128,768]{2,1,0:T(8,128)(2,1)}) custom-call(s32[1]{0:T(128)} %bitcast.y_ref, bf16[128,3072]{1,0:T(8,128)(2,1)} %tok_ref.1, bf16[128,3072]{1,0:T(8,128)(2,1)} %tan_ref.1, f32[1,3072]{1,0:T(1,128)} %bitcast.66, f32[1,3072]{1,0:T(1,128)} %bitcast.67), custom_call_target="tpu_custom_call" | custom-call | flops 7864320 | bytes 3145728 | tf_op jit(solution)/shard_map/pallas_call | solution.py:47
  11.8 3.2 %collective-permute-start = (bf16[4,256,768]{2,1,0:T(8,128)(2,1)}, bf16[4,256,768]{2,1,0:T(8,128)(2,1)}, u32[]{:S(2)}, u32[]{:S(2)}) collective-permute-start(bf16[4,256,768]{2,1,0:T(8,128)(2,1)} %bitcast.43), channel_id=1, source_target_pairs={{0,1},{1,0},{2,3},{3,2},{4,5},{5,4},{6,7},{7,6},{8,9},{9,8},{10,11... | collective-permute-start | bytes 4718600 | tf_op jit(solution)/shard_map/ppermute | solution.py:254
  15.1 1.0 dynamic-slice_reduce_fusion
  16.1 9.9 %collective-permute-done.1 = bf16[256,768]{1,0:T(8,128)(2,1)S(1)} collective-permute-done((bf16[256,768]{1,0:T(8,128)(2,1)}, bf16[256,768]{1,0:T(8,128)(2,1)S(1)}, u32[]{:S(2)}, u32[]{:S(2)}) %collective-permute-start.1) | collective-permute-done | bytes 393248 | tf_op jit(solution)/shard_map/ppermute | solution.py:254
  26.0 0.8 copy-done.5
  26.9 4.4 %collective-permute-start.2 = (bf16[192,384]{1,0:T(8,128)(2,1)S(1)}, bf16[192,384]{1,0:T(8,128)(2,1)S(1)}, u32[]{:S(2)}, u32[]{:S(2)}) collective-permute-start(bf16[192,384]{1,0:T(8,128)(2,1)S(1)} %bitcast.56), channel_id=1, source_target_pairs={{0,192},{64,0},{128,64},{192,128},{1,193},{65,1},{129,65},{193,129... | collective-permute-start | bytes 442376 | tf_op jit(solution)/shard_map/ppermute | solution.py:250
  31.2 1.0 collective-permute-start.3
  32.2 2.3 %collective-permute-start.4 = (bf16[192,384]{1,0:T(8,128)(2,1)S(1)}, bf16[192,384]{1,0:T(8,128)(2,1)S(1)}, u32[]{:S(2)}, u32[]{:S(2)}) collective-permute-start(bf16[192,384]{1,0:T(8,128)(2,1)S(1)} %bitcast.58), channel_id=1, source_target_pairs={{0,64},{64,128},{128,192},{192,0},{1,65},{65,129},{129,193},{193,1... | collective-permute-start | bytes 442376 | tf_op jit(solution)/shard_map/ppermute | solution.py:250
  34.6 3.5 %collective-permute-done.2 = bf16[192,384]{1,0:T(8,128)(2,1)S(1)} collective-permute-done((bf16[192,384]{1,0:T(8,128)(2,1)S(1)}, bf16[192,384]{1,0:T(8,128)(2,1)S(1)}, u32[]{:S(2)}, u32[]{:S(2)}) %collective-permute-start.2) | collective-permute-done | bytes 147488 | tf_op jit(solution)/shard_map/ppermute | solution.py:250
  38.1 5.1 %collective-permute-done.3 = bf16[192,384]{1,0:T(8,128)(2,1)S(1)} collective-permute-done((bf16[192,384]{1,0:T(8,128)(2,1)S(1)}, bf16[192,384]{1,0:T(8,128)(2,1)S(1)}, u32[]{:S(2)}, u32[]{:S(2)}) %collective-permute-start.3) | collective-permute-done | bytes 147488 | tf_op jit(solution)/shard_map/ppermute | solution.py:250
  43.3 1.6 collective-permute-start.5
  44.9 1.4 collective-permute-start.6
  47.1 7.4 %collective-permute-done.5.w1_ref = bf16[768,384]{1,0:T(8,128)(2,1)S(1)} collective-permute-done((bf16[768,384]{1,0:T(8,128)(2,1)S(1)}, bf16[768,384]{1,0:T(8,128)(2,1)S(1)}, u32[]{:S(2)}, u32[]{:S(2)}) %collective-permute-start.5) | collective-permute-done | bytes 589856 | tf_op jit(solution)/shard_map/ppermute | solution.py:259
  54.4 4.3 %collective-permute-done.6.w3_ref = bf16[768,384]{1,0:T(8,128)(2,1)} collective-permute-done((bf16[768,384]{1,0:T(8,128)(2,1)S(1)}, bf16[768,384]{1,0:T(8,128)(2,1)}, u32[]{:S(2)}, u32[]{:S(2)}) %collective-permute-start.6) | collective-permute-done | bytes 589856 | tf_op jit(solution)/shard_map/ppermute | solution.py:259
  58.8 1.9 %collective-permute-start.8 = (bf16[4,256,768]{2,1,0:T(8,128)(2,1)}, bf16[4,256,768]{2,1,0:T(8,128)(2,1)}, u32[]{:S(2)}, u32[]{:S(2)}) collective-permute-start(bf16[4,256,768]{2,1,0:T(8,128)(2,1)} %bitcast.46), channel_id=1, source_target_pairs={{0,1},{1,0},{2,3},{3,2},{4,5},{5,4},{6,7},{7,6},{8,9},{9,8},{10,11... | collective-permute-start | bytes 4718600 | tf_op jit(solution)/shard_map/ppermute | solution.py:254
  60.8 1.2 collective-permute-start.9
  62.2 3.0 %shard_map.105.near_ref = f32[2,256,384]{2,1,0:T(8,128)S(1)} custom-call(s32[2]{0:T(128)S(1)} %pad_add_fusion.2.spot_ref, bf16[4,256,768]{2,1,0:T(8,128)(2,1)S(1)} %bitcast.44, bf16[4,256,768]{2,1,0:T(8,128)(2,1)} %collective-permute-done.n1_ref, bf16[768,384]{1,0:T(8,128)(2,1)S(1)} %bitcast.51, bf16[768,384]{1,0:T(8,128)(2,1)S(1)} %collective-permute-done.5.w1_ref, ...), custom_call_target="tpu_custom_call" | custom-call | flops 905969664 | bytes 6291456 | tf_op jit(solution)/shard_map/pallas_call | solution.py:83
  65.2 2.9 %shard_map.106.far_ref = f32[2,256,384]{2,1,0:T(8,128)S(1)} custom-call(s32[2]{0:T(128)S(1)} %pad_add_fusion.2.spot_ref, bf16[4,256,768]{2,1,0:T(8,128)(2,1)S(1)} %bitcast.47, bf16[4,256,768]{2,1,0:T(8,128)(2,1)} %collective-permute-done.8.n1_ref.n3_ref, bf16[768,384]{1,0:T(8,128)(2,1)S(1)} %bitcast.52, bf16[768,384]{1,0:T(8,128)(2,1)S(1)} %collective-permute-done.5.w1_ref, ...), custom_call_target="tpu_custom_call" | custom-call | flops 905969664 | bytes 6291456 | tf_op jit(solution)/shard_map/pallas_call | solution.py:83
  68.2 2.6 %collective-permute-done.9.w_ref = bf16[768,384]{1,0:T(8,128)(2,1)} collective-permute-done((bf16[768,384]{1,0:T(8,128)(2,1)S(1)}, bf16[768,384]{1,0:T(8,128)(2,1)}, u32[]{:S(2)}, u32[]{:S(2)}) %collective-permute-start.9) | collective-permute-done | bytes 589856 | tf_op jit(solution)/shard_map/ppermute | solution.py:259
  70.8 3.0 %shard_map.107 = (bf16[4,128,128]{2,1,0:T(8,128)(2,1)S(1)}, bf16[6,128,128]{2,1,0:T(8,128)(2,1)S(1)}, bf16[6,128,128]{2,1,0:T(8,128)(2,1)S(1)}, bf16[6,128,128]{2,1,0:T(8,128)(2,1)S(1)}, bf16[2,128,128]{2,1,0:T(8,128)(2,1)S(1)}) custom-call(s32[5]{0:T(128)S(1)} %stack.92.spot_ref, bf16[4,256,768]{2,1,0:T(8,128)(2,1)S(1)} %bitcast.45, ...), custom_call_target="tpu_custom_call" | custom-call | flops 603979776 | bytes 5242880 | tf_op jit(solution)/shard_map/pallas_call | solution.py:121
  73.8 3.6 %collective-permute-start.10 = (bf16[6,128,128]{2,1,0:T(8,128)(2,1)S(1)}, bf16[6,128,128]{2,1,0:T(8,128)(2,1)S(1)}, u32[]{:S(2)}, u32[]{:S(2)}) collective-permute-start(bf16[6,128,128]{2,1,0:T(8,128)(2,1)S(1)} %get-tuple-element.40), channel_id=1, source_target_pairs={{0,64},{64,128},{128,192},{192,0},{1,65},{65,129},{129,193},{193,1... | collective-permute-start | bytes 589832 | tf_op jit(solution)/shard_map/ppermute | solution.py:250
  77.4 0.8 collective-permute-start.11
  78.1 1.2 collective-permute-start.12
  80.2 2.6 %collective-permute-done.12.refs_1_ = bf16[4,128,128]{2,1,0:T(8,128)(2,1)S(1)} collective-permute-done((bf16[4,128,128]{2,1,0:T(8,128)(2,1)S(1)}, bf16[4,128,128]{2,1,0:T(8,128)(2,1)S(1)}, u32[]{:S(2)}, u32[]{:S(2)}) %collective-permute-start.12) | collective-permute-done | bytes 131104 | tf_op jit(solution)/shard_map/ppermute | solution.py:250
  82.8 2.1 %collective-permute-done.13.refs_2_ = bf16[4,128,128]{2,1,0:T(8,128)(2,1)S(1)} collective-permute-done((bf16[4,128,128]{2,1,0:T(8,128)(2,1)S(1)}, bf16[4,128,128]{2,1,0:T(8,128)(2,1)S(1)}, u32[]{:S(2)}, u32[]{:S(2)}) %collective-permute-start.13) | collective-permute-done | bytes 131104 | tf_op jit(solution)/shard_map/ppermute | solution.py:250
  84.9 1.4 collective-permute-done.14.refs_3_
  86.3 8.3 %collective-permute-done.11.refs_12_ = bf16[6,128,128]{2,1,0:T(8,128)(2,1)S(1)} collective-permute-done((bf16[6,128,128]{2,1,0:T(8,128)(2,1)S(1)}, bf16[6,128,128]{2,1,0:T(8,128)(2,1)S(1)}, u32[]{:S(2)}, u32[]{:S(2)}) %collective-permute-start.11) | collective-permute-done | bytes 196640 | tf_op jit(solution)/shard_map/ppermute | solution.py:250
  94.6 1.8 %collective-permute-start.16 = (bf16[8,128,128]{2,1,0:T(8,128)(2,1)S(1)}, bf16[8,128,128]{2,1,0:T(8,128)(2,1)S(1)}, u32[]{:S(2)}, u32[]{:S(2)}) collective-permute-start(bf16[8,128,128]{2,1,0:T(8,128)(2,1)S(1)} %pad_maximum_fusion), channel_id=1, source_target_pairs={{0,48},{16,0},{32,16},{48,32},{1,49},{17,1},{33,17},{49,33},{2,50}... | collective-permute-start | bytes 786440 | tf_op jit(solution)/shard_map/ppermute | solution.py:250
  96.4 2.6 %collective-permute-start.15 = (bf16[6,128,128]{2,1,0:T(8,128)(2,1)S(1)}, bf16[6,128,128]{2,1,0:T(8,128)(2,1)S(1)}, u32[]{:S(2)}, u32[]{:S(2)}) collective-permute-start(bf16[6,128,128]{2,1,0:T(8,128)(2,1)S(1)} %get-tuple-element.48), channel_id=1, source_target_pairs={{0,128},{64,192},{128,0},{192,64},{1,129},{65,193},{129,1},{193,65... | collective-permute-start | bytes 589832 | tf_op jit(solution)/shard_map/ppermute | solution.py:250
  99.7 11.5 %collective-permute-done.15.refs_11_ = bf16[6,128,128]{2,1,0:T(8,128)(2,1)S(1)} collective-permute-done((bf16[6,128,128]{2,1,0:T(8,128)(2,1)S(1)}, bf16[6,128,128]{2,1,0:T(8,128)(2,1)S(1)}, u32[]{:S(2)}, u32[]{:S(2)}) %collective-permute-start.15) | collective-permute-done | bytes 196640 | tf_op jit(solution)/shard_map/ppermute | solution.py:250
  111.4 1.4 collective-permute-start.21
  112.8 3.2 %collective-permute-done.18.refs_6_ = bf16[8,128,128]{2,1,0:T(8,128)(2,1)S(1)} collective-permute-done((bf16[8,128,128]{2,1,0:T(8,128)(2,1)S(1)}, bf16[8,128,128]{2,1,0:T(8,128)(2,1)S(1)}, u32[]{:S(2)}, u32[]{:S(2)}) %collective-permute-start.18) | collective-permute-done | bytes 262176 | tf_op jit(solution)/shard_map/ppermute | solution.py:250
  116.0 2.7 %collective-permute-done.20.refs_8_ = bf16[4,128,128]{2,1,0:T(8,128)(2,1)S(1)} collective-permute-done((bf16[4,128,128]{2,1,0:T(8,128)(2,1)S(1)}, bf16[4,128,128]{2,1,0:T(8,128)(2,1)S(1)}, u32[]{:S(2)}, u32[]{:S(2)}) %collective-permute-start.20) | collective-permute-done | bytes 131104 | tf_op jit(solution)/shard_map/ppermute | solution.py:250
  118.7 5.5 %collective-permute-done.21.refs_9_ = bf16[4,128,128]{2,1,0:T(8,128)(2,1)S(1)} collective-permute-done((bf16[4,128,128]{2,1,0:T(8,128)(2,1)S(1)}, bf16[4,128,128]{2,1,0:T(8,128)(2,1)S(1)}, u32[]{:S(2)}, u32[]{:S(2)}) %collective-permute-start.21) | collective-permute-done | bytes 131104 | tf_op jit(solution)/shard_map/ppermute | solution.py:250
  124.2 3.5 %shard_map.108 = (bf16[256,128]{1,0:T(8,128)(2,1)S(1)}, bf16[256,128]{1,0:T(8,128)(2,1)S(1)}, bf16[256,128]{1,0:T(8,128)(2,1)S(1)}, bf16[256,128]{1,0:T(8,128)(2,1)S(1)}) custom-call(s32[4]{0:T(128)S(1)} %pad_add_fusion.1.spot_ref, bf16[4,128,128]{2,1,0:T(8,128)(2,1)S(1)} %get-tuple-element.39.refs_0_, ...), custom_call_target="tpu_custom_call" | custom-call | flops 1610612736 | bytes 3145728 | tf_op jit(solution)/shard_map/pallas_call | solution.py:190
  127.6 4.0 %collective-permute-start.22 = (bf16[256,128]{1,0:T(8,128)(2,1)S(1)}, bf16[256,128]{1,0:T(8,128)(2,1)S(1)}, u32[]{:S(2)}, u32[]{:S(2)}) collective-permute-start(bf16[256,128]{1,0:T(8,128)(2,1)S(1)} %get-tuple-element.52), channel_id=1, source_target_pairs={{0,0},{1,64},{2,128},{3,192},{64,1},{65,65},{66,129},{67,193},{128... | collective-permute-start | bytes 196616 | tf_op jit(solution)/shard_map/ppermute | solution.py:335
  131.9 3.6 %collective-permute-start.24 = (bf16[256,128]{1,0:T(8,128)(2,1)S(1)}, bf16[256,128]{1,0:T(8,128)(2,1)S(1)}, u32[]{:S(2)}, u32[]{:S(2)}) collective-permute-start(bf16[256,128]{1,0:T(8,128)(2,1)S(1)} %get-tuple-element.54), channel_id=1, source_target_pairs={{0,128},{1,192},{2,0},{3,64},{64,129},{65,193},{66,1},{67,65},{128... | collective-permute-start | bytes 196616 | tf_op jit(solution)/shard_map/ppermute | solution.py:335
  135.5 1.2 collective-permute-done.23
  136.7 1.5 collective-permute-done.24
  138.2 2.1 %collective-permute-done.25 = bf16[256,128]{1,0:T(8,128)(2,1)S(1)} collective-permute-done((bf16[256,128]{1,0:T(8,128)(2,1)S(1)}, bf16[256,128]{1,0:T(8,128)(2,1)S(1)}, u32[]{:S(2)}, u32[]{:S(2)}) %collective-permute-start.25) | collective-permute-done | bytes 65568 | tf_op jit(solution)/shard_map/ppermute | solution.py:335
  140.4 1.7 %collective-permute-start.29 = (bf16[4,4,192,256]{3,2,1,0:T(8,128)(2,1)}, bf16[4,4,192,256]{3,2,1,0:T(8,128)(2,1)S(1)}, u32[]{:S(2)}, u32[]{:S(2)}) collective-permute-start(bf16[4,4,192,256]{3,2,1,0:T(8,128)(2,1)} %bitcast.53), channel_id=1, source_target_pairs={{0,1},{1,0},{2,3},{3,2},{4,5},{5,4},{6,7},{7,6},{8,9},{9,8},{10,11... | collective-permute-start | bytes 4718600 | tf_op jit(solution)/shard_map/ppermute | solution.py:254
  142.4 1.2 collective-permute-start.28
  143.6 0.8 dynamic_slice.20
  145.6 1.8 %constant_dynamic-slice_fusion = (bf16[128,768]{1,0:T(8,128)(2,1)}, bf16[128,768]{1,0:T(8,128)(2,1)}) fusion(bf16[128,3072]{1,0:T(8,128)(2,1)} %tan_ref.1, s32[]{:T(128)S(6)} %select_n.92, bf16[128,3072]{1,0:T(8,128)(2,1)} %tok_ref.1), kind=kLoop, calls=%fused_computation.9 | loop fusion | bytes 786436 | tf_op jit(solution)/shard_map/dynamic_slice | solution.py:343
  147.4 2.6 %collective-permute-done.26.h1 = bf16[4,256,128]{2,1,0:T(8,128)(2,1)S(1)} collective-permute-done((bf16[4,256,128]{2,1,0:T(8,128)(2,1)S(1)}, bf16[4,256,128]{2,1,0:T(8,128)(2,1)S(1)}, u32[]{:S(2)}, u32[]{:S(2)}) %collective-permute-start.26) | collective-permute-done | bytes 262176 | tf_op jit(solution)/shard_map/ppermute | solution.py:250
  150.0 1.4 collective-permute-done.27.h2
  151.4 6.1 %collective-permute-done.28.h3 = bf16[4,256,128]{2,1,0:T(8,128)(2,1)S(1)} collective-permute-done((bf16[4,256,128]{2,1,0:T(8,128)(2,1)S(1)}, bf16[4,256,128]{2,1,0:T(8,128)(2,1)S(1)}, u32[]{:S(2)}, u32[]{:S(2)}) %collective-permute-start.28) | collective-permute-done | bytes 262176 | tf_op jit(solution)/shard_map/ppermute | solution.py:250
  158.7 4.7 %shard_map.109 = (bf16[128,768]{1,0:T(8,128)(2,1)}, bf16[128,768]{1,0:T(8,128)(2,1)}) custom-call(s32[3]{0:T(128)} %pad_add_fusion.place_ref, bf16[4,256,128]{2,1,0:T(8,128)(2,1)} %copy-done.4, bf16[4,256,128]{2,1,0:T(8,128)(2,1)} %copy-done.6, bf16[4,256,128]{2,1,0:T(8,128)(2,1)} %copy-done.7, bf16[4,256,128]{2,1,0:T(8,128)(2,1)} %copy-done.8, ...), custom_call_target="tpu_custom_call" | custom-call | flops 805306368 | bytes 6291456 | tf_op jit(solution)/shard_map/pallas_call | solution.py:232
  (72 shorter events, 6.3 us)
Async XLA Ops:
  7.2 7.9 %copy-start = (bf16[192,4,3,128]{3,1,2,0:T(4,128)(2,1)S(1)}, bf16[192,4,3,128]{3,1,2,0:T(4,128)(2,1)}, u32[]{:S(2)}) copy-start(bf16[192,4,3,128]{3,1,2,0:T(4,128)(2,1)} %param.11) | copy-start | bytes 1769476
  7.2 51.6 %all-gather.5.cloned.1.call-start = ((), (), s32[]{:S(2)}) async-start(), calls=%async_computation | async-start | bytes 1966080 | tf_op jit(solution)/shard_map/all_gather | solution.py:296
  11.8 14.1 %collective-permute-start = (bf16[4,256,768]{2,1,0:T(8,128)(2,1)}, bf16[4,256,768]{2,1,0:T(8,128)(2,1)}, u32[]{:S(2)}, u32[]{:S(2)}) collective-permute-start(bf16[4,256,768]{2,1,0:T(8,128)(2,1)} %bitcast.43), channel_id=1, source_target_pairs={{0,1},{1,0},{2,3},{3,2},{4,5},{5,4},{6,7},{7,6},{8,9},{9,8},{10,11... | collective-permute-start | bytes 4718600 | tf_op jit(solution)/shard_map/ppermute | solution.py:254
  15.1 10.9 %collective-permute-start.1 = (bf16[256,768]{1,0:T(8,128)(2,1)}, bf16[256,768]{1,0:T(8,128)(2,1)S(1)}, u32[]{:S(2)}, u32[]{:S(2)}) collective-permute-start(bf16[256,768]{1,0:T(8,128)(2,1)} %bitcast.70), channel_id=1, source_target_pairs={{0,2},{2,0},{1,3},{3,1},{4,6},{6,4},{5,7},{7,5},{8,10},{10,8},{9,1... | collective-permute-start | bytes 1179656 | tf_op jit(solution)/shard_map/ppermute | solution.py:254
  15.1 31.1 %copy-start.10 = (bf16[192,4,128]{2,1,0:T(4,128)(2,1)S(1)}, bf16[192,4,128]{2,1,0:T(4,128)(2,1)}, u32[]{:S(2)}) copy-start(bf16[192,4,128]{2,1,0:T(4,128)(2,1)} %param.12) | copy-start | bytes 589828
  16.0 46.1 %copy-start.11 = (f32[128]{0:T(128)S(1)}, f32[128]{0:T(128)}, u32[]{:S(2)}) copy-start(f32[128]{0:T(128)} %param.17) | copy-start | bytes 1540
  16.1 46.1 %copy-start.12 = (f32[128]{0:T(128)S(1)}, f32[128]{0:T(128)}, u32[]{:S(2)}) copy-start(f32[128]{0:T(128)} %param.16) | copy-start | bytes 1540
  16.1 46.1 %copy-start.1 = (bf16[4,2,128,768]{3,2,1,0:T(8,128)(2,1)S(1)}, bf16[4,2,128,768]{3,2,1,0:T(8,128)(2,1)}, u32[]{:S(2)}) copy-start(bf16[4,2,128,768]{3,2,1,0:T(8,128)(2,1)} %get-tuple-element.30) | copy-start | bytes 4718596
  26.0 0.8 copy-start.5
  26.8 113.6 %all-gather.7.cloned.1.call-start = ((), (), s32[]{:S(2)}) async-start(), calls=%async_computation.1 | async-start | bytes 1671168 | tf_op jit(solution)/shard_map/all_gather | solution.py:316
  26.9 11.2 %collective-permute-start.2 = (bf16[192,384]{1,0:T(8,128)(2,1)S(1)}, bf16[192,384]{1,0:T(8,128)(2,1)S(1)}, u32[]{:S(2)}, u32[]{:S(2)}) collective-permute-start(bf16[192,384]{1,0:T(8,128)(2,1)S(1)} %bitcast.56), channel_id=1, source_target_pairs={{0,192},{64,0},{128,64},{192,128},{1,193},{65,1},{129,65},{193,129... | collective-permute-start | bytes 442376 | tf_op jit(solution)/shard_map/ppermute | solution.py:250
  31.2 12.0 %collective-permute-start.3 = (bf16[192,384]{1,0:T(8,128)(2,1)S(1)}, bf16[192,384]{1,0:T(8,128)(2,1)S(1)}, u32[]{:S(2)}, u32[]{:S(2)}) collective-permute-start(bf16[192,384]{1,0:T(8,128)(2,1)S(1)} %bitcast.57), channel_id=1, source_target_pairs={{0,128},{64,192},{128,0},{192,64},{1,129},{65,193},{129,1},{193,65... | collective-permute-start | bytes 442376 | tf_op jit(solution)/shard_map/ppermute | solution.py:250
  32.2 11.0 %collective-permute-start.4 = (bf16[192,384]{1,0:T(8,128)(2,1)S(1)}, bf16[192,384]{1,0:T(8,128)(2,1)S(1)}, u32[]{:S(2)}, u32[]{:S(2)}) collective-permute-start(bf16[192,384]{1,0:T(8,128)(2,1)S(1)} %bitcast.58), channel_id=1, source_target_pairs={{0,64},{64,128},{128,192},{192,0},{1,65},{65,129},{129,193},{193,1... | collective-permute-start | bytes 442376 | tf_op jit(solution)/shard_map/ppermute | solution.py:250
  43.3 11.1 %collective-permute-start.5 = (bf16[768,384]{1,0:T(8,128)(2,1)S(1)}, bf16[768,384]{1,0:T(8,128)(2,1)S(1)}, u32[]{:S(2)}, u32[]{:S(2)}) collective-permute-start(bf16[768,384]{1,0:T(8,128)(2,1)S(1)} %bitcast.49), channel_id=1, source_target_pairs={{0,48},{1,17},{16,0},{17,33},{32,16},{33,49},{48,32},{49,1},{2,50}... | collective-permute-start | bytes 1769480 | tf_op jit(solution)/shard_map/ppermute | solution.py:259
  44.9 13.9 %collective-permute-start.6 = (bf16[768,384]{1,0:T(8,128)(2,1)S(1)}, bf16[768,384]{1,0:T(8,128)(2,1)}, u32[]{:S(2)}, u32[]{:S(2)}) collective-permute-start(bf16[768,384]{1,0:T(8,128)(2,1)S(1)} %bitcast.50), channel_id=1, source_target_pairs={{0,16},{1,49},{16,32},{17,1},{32,48},{33,17},{48,0},{49,33},{2,18}... | collective-permute-start | bytes 1769480 | tf_op jit(solution)/shard_map/ppermute | solution.py:259
  46.4 0.7 collective-permute-start.7
  47.0 11.7 %copy-start.9 = (bf16[192,256]{1,0:T(8,128)(2,1)}, bf16[192,256]{1,0:T(8,128)(2,1)S(1)}, u32[]{:S(2)}) copy-start(bf16[192,256]{1,0:T(8,128)(2,1)S(1)} %collective-permute-done.7) | copy-start | bytes 294916
  58.8 6.4 %collective-permute-start.8 = (bf16[4,256,768]{2,1,0:T(8,128)(2,1)}, bf16[4,256,768]{2,1,0:T(8,128)(2,1)}, u32[]{:S(2)}, u32[]{:S(2)}) collective-permute-start(bf16[4,256,768]{2,1,0:T(8,128)(2,1)} %bitcast.46), channel_id=1, source_target_pairs={{0,1},{1,0},{2,3},{3,2},{4,5},{5,4},{6,7},{7,6},{8,9},{9,8},{10,11... | collective-permute-start | bytes 4718600 | tf_op jit(solution)/shard_map/ppermute | solution.py:254
  60.8 10.1 %collective-permute-start.9 = (bf16[768,384]{1,0:T(8,128)(2,1)S(1)}, bf16[768,384]{1,0:T(8,128)(2,1)}, u32[]{:S(2)}, u32[]{:S(2)}) collective-permute-start(bf16[768,384]{1,0:T(8,128)(2,1)S(1)} %collective-permute-done.5.w1_ref), channel_id=1, source_target_pairs={{0,48},{1,17},{16,0},{17,33},{32,16},{33,49},{48,32},{49,1},{2,50}... | collective-permute-start | bytes 1769480 | tf_op jit(solution)/shard_map/ppermute | solution.py:259
  62.1 3.1 %copy-start.2 = (bf16[1024,768]{1,0:T(8,128)(2,1)S(1)}, bf16[1024,768]{1,0:T(8,128)(2,1)}, u32[]{:S(2)}) copy-start(bf16[1024,768]{1,0:T(8,128)(2,1)} %all-gather.5.cloned.1.call-done) | copy-start | bytes 4718596
  73.8 12.5 %collective-permute-start.10 = (bf16[6,128,128]{2,1,0:T(8,128)(2,1)S(1)}, bf16[6,128,128]{2,1,0:T(8,128)(2,1)S(1)}, u32[]{:S(2)}, u32[]{:S(2)}) collective-permute-start(bf16[6,128,128]{2,1,0:T(8,128)(2,1)S(1)} %get-tuple-element.40), channel_id=1, source_target_pairs={{0,64},{64,128},{128,192},{192,0},{1,65},{65,129},{129,193},{193,1... | collective-permute-start | bytes 589832 | tf_op jit(solution)/shard_map/ppermute | solution.py:250
  77.4 17.2 %collective-permute-start.11 = (bf16[6,128,128]{2,1,0:T(8,128)(2,1)S(1)}, bf16[6,128,128]{2,1,0:T(8,128)(2,1)S(1)}, u32[]{:S(2)}, u32[]{:S(2)}) collective-permute-start(bf16[6,128,128]{2,1,0:T(8,128)(2,1)S(1)} %get-tuple-element.41), channel_id=1, source_target_pairs={{0,192},{64,0},{128,64},{192,128},{1,193},{65,1},{129,65},{193,129... | collective-permute-start | bytes 589832 | tf_op jit(solution)/shard_map/ppermute | solution.py:250
  78.1 4.6 %collective-permute-start.12 = (bf16[4,128,128]{2,1,0:T(8,128)(2,1)S(1)}, bf16[4,128,128]{2,1,0:T(8,128)(2,1)S(1)}, u32[]{:S(2)}, u32[]{:S(2)}) collective-permute-start(bf16[4,128,128]{2,1,0:T(8,128)(2,1)S(1)} %get-tuple-element.39.refs_0_), channel_id=1, source_target_pairs={{0,48},{16,0},{32,16},{48,32},{1,49},{17,1},{33,17},{49,33},{2,50}... | collective-permute-start | bytes 393224 | tf_op jit(solution)/shard_map/ppermute | solution.py:250
  79.3 5.6 %collective-permute-start.13 = (bf16[4,128,128]{2,1,0:T(8,128)(2,1)S(1)}, bf16[4,128,128]{2,1,0:T(8,128)(2,1)S(1)}, u32[]{:S(2)}, u32[]{:S(2)}) collective-permute-start(bf16[4,128,128]{2,1,0:T(8,128)(2,1)S(1)} %get-tuple-element.39.refs_0_), channel_id=1, source_target_pairs={{0,32},{16,48},{32,0},{48,16},{1,33},{17,49},{33,1},{49,17},{2,34}... | collective-permute-start | bytes 393224 | tf_op jit(solution)/shard_map/ppermute | solution.py:250
  79.7 6.5 %collective-permute-start.14 = (bf16[4,128,128]{2,1,0:T(8,128)(2,1)S(1)}, bf16[4,128,128]{2,1,0:T(8,128)(2,1)S(1)}, u32[]{:S(2)}, u32[]{:S(2)}) collective-permute-start(bf16[4,128,128]{2,1,0:T(8,128)(2,1)S(1)} %get-tuple-element.39.refs_0_), channel_id=1, source_target_pairs={{0,16},{16,32},{32,48},{48,0},{1,17},{17,33},{33,49},{49,1},{2,18}... | collective-permute-start | bytes 393224 | tf_op jit(solution)/shard_map/ppermute | solution.py:250
  94.6 16.6 %collective-permute-start.16 = (bf16[8,128,128]{2,1,0:T(8,128)(2,1)S(1)}, bf16[8,128,128]{2,1,0:T(8,128)(2,1)S(1)}, u32[]{:S(2)}, u32[]{:S(2)}) collective-permute-start(bf16[8,128,128]{2,1,0:T(8,128)(2,1)S(1)} %pad_maximum_fusion), channel_id=1, source_target_pairs={{0,48},{16,0},{32,16},{48,32},{1,49},{17,1},{33,17},{49,33},{2,50}... | collective-permute-start | bytes 786440 | tf_op jit(solution)/shard_map/ppermute | solution.py:250
  96.4 14.8 %collective-permute-start.15 = (bf16[6,128,128]{2,1,0:T(8,128)(2,1)S(1)}, bf16[6,128,128]{2,1,0:T(8,128)(2,1)S(1)}, u32[]{:S(2)}, u32[]{:S(2)}) collective-permute-start(bf16[6,128,128]{2,1,0:T(8,128)(2,1)S(1)} %get-tuple-element.48), channel_id=1, source_target_pairs={{0,128},{64,192},{128,0},{192,64},{1,129},{65,193},{129,1},{193,65... | collective-permute-start | bytes 589832 | tf_op jit(solution)/shard_map/ppermute | solution.py:250
  99.0 13.8 %collective-permute-start.17 = (bf16[8,128,128]{2,1,0:T(8,128)(2,1)S(1)}, bf16[8,128,128]{2,1,0:T(8,128)(2,1)S(1)}, u32[]{:S(2)}, u32[]{:S(2)}) collective-permute-start(bf16[8,128,128]{2,1,0:T(8,128)(2,1)S(1)} %pad_maximum_fusion), channel_id=1, source_target_pairs={{0,32},{16,48},{32,0},{48,16},{1,33},{17,49},{33,1},{49,17},{2,34}... | collective-permute-start | bytes 786440 | tf_op jit(solution)/shard_map/ppermute | solution.py:250
  99.0 17.0 %collective-permute-start.18 = (bf16[8,128,128]{2,1,0:T(8,128)(2,1)S(1)}, bf16[8,128,128]{2,1,0:T(8,128)(2,1)S(1)}, u32[]{:S(2)}, u32[]{:S(2)}) collective-permute-start(bf16[8,128,128]{2,1,0:T(8,128)(2,1)S(1)} %pad_maximum_fusion), channel_id=1, source_target_pairs={{0,16},{16,32},{32,48},{48,0},{1,17},{17,33},{33,49},{49,1},{2,18}... | collective-permute-start | bytes 786440 | tf_op jit(solution)/shard_map/ppermute | solution.py:250
  111.2 4.8 %collective-permute-start.19 = (bf16[4,128,128]{2,1,0:T(8,128)(2,1)S(1)}, bf16[4,128,128]{2,1,0:T(8,128)(2,1)S(1)}, u32[]{:S(2)}, u32[]{:S(2)}) collective-permute-start(bf16[4,128,128]{2,1,0:T(8,128)(2,1)S(1)} %slice.11), channel_id=1, source_target_pairs={{0,48},{16,0},{32,16},{48,32},{1,49},{17,1},{33,17},{49,33},{2,50}... | collective-permute-start | bytes 393224 | tf_op jit(solution)/shard_map/ppermute | solution.py:250
  111.4 7.3 %collective-permute-start.20 = (bf16[4,128,128]{2,1,0:T(8,128)(2,1)S(1)}, bf16[4,128,128]{2,1,0:T(8,128)(2,1)S(1)}, u32[]{:S(2)}, u32[]{:S(2)}) collective-permute-start(bf16[4,128,128]{2,1,0:T(8,128)(2,1)S(1)} %slice.11), channel_id=1, source_target_pairs={{0,32},{16,48},{32,0},{48,16},{1,33},{17,49},{33,1},{49,17},{2,34}... | collective-permute-start | bytes 393224 | tf_op jit(solution)/shard_map/ppermute | solution.py:250
  111.4 12.8 %collective-permute-start.21 = (bf16[4,128,128]{2,1,0:T(8,128)(2,1)S(1)}, bf16[4,128,128]{2,1,0:T(8,128)(2,1)S(1)}, u32[]{:S(2)}, u32[]{:S(2)}) collective-permute-start(bf16[4,128,128]{2,1,0:T(8,128)(2,1)S(1)} %slice.11), channel_id=1, source_target_pairs={{0,16},{16,32},{32,48},{48,0},{1,17},{17,33},{33,49},{49,1},{2,18}... | collective-permute-start | bytes 393224 | tf_op jit(solution)/shard_map/ppermute | solution.py:250
  127.6 7.8 %collective-permute-start.22 = (bf16[256,128]{1,0:T(8,128)(2,1)S(1)}, bf16[256,128]{1,0:T(8,128)(2,1)S(1)}, u32[]{:S(2)}, u32[]{:S(2)}) collective-permute-start(bf16[256,128]{1,0:T(8,128)(2,1)S(1)} %get-tuple-element.52), channel_id=1, source_target_pairs={{0,0},{1,64},{2,128},{3,192},{64,1},{65,65},{66,129},{67,193},{128... | collective-permute-start | bytes 196616 | tf_op jit(solution)/shard_map/ppermute | solution.py:335
  131.7 5.0 %collective-permute-start.23 = (bf16[256,128]{1,0:T(8,128)(2,1)S(1)}, bf16[256,128]{1,0:T(8,128)(2,1)S(1)}, u32[]{:S(2)}, u32[]{:S(2)}) collective-permute-start(bf16[256,128]{1,0:T(8,128)(2,1)S(1)} %get-tuple-element.53), channel_id=1, source_target_pairs={{0,64},{1,128},{2,192},{3,0},{64,65},{65,129},{66,193},{67,1},{128... | collective-permute-start | bytes 196616 | tf_op jit(solution)/shard_map/ppermute | solution.py:335
  131.9 6.2 %collective-permute-start.24 = (bf16[256,128]{1,0:T(8,128)(2,1)S(1)}, bf16[256,128]{1,0:T(8,128)(2,1)S(1)}, u32[]{:S(2)}, u32[]{:S(2)}) collective-permute-start(bf16[256,128]{1,0:T(8,128)(2,1)S(1)} %get-tuple-element.54), channel_id=1, source_target_pairs={{0,128},{1,192},{2,0},{3,64},{64,129},{65,193},{66,1},{67,65},{128... | collective-permute-start | bytes 196616 | tf_op jit(solution)/shard_map/ppermute | solution.py:335
  135.5 4.8 %collective-permute-start.25 = (bf16[256,128]{1,0:T(8,128)(2,1)S(1)}, bf16[256,128]{1,0:T(8,128)(2,1)S(1)}, u32[]{:S(2)}, u32[]{:S(2)}) collective-permute-start(bf16[256,128]{1,0:T(8,128)(2,1)S(1)} %get-tuple-element.55), channel_id=1, source_target_pairs={{0,192},{1,0},{2,64},{3,128},{64,193},{65,1},{66,65},{67,129},{128... | collective-permute-start | bytes 196616 | tf_op jit(solution)/shard_map/ppermute | solution.py:335
  140.3 17.2 %copy-start.4 = (bf16[4,256,128]{2,1,0:T(8,128)(2,1)}, bf16[4,256,128]{2,1,0:T(8,128)(2,1)S(1)}, u32[]{:S(2)}) copy-start(bf16[4,256,128]{2,1,0:T(8,128)(2,1)S(1)} %pad_maximum_fusion.1.h0) | copy-start | bytes 786436
  140.4 17.1 %collective-permute-start.29 = (bf16[4,4,192,256]{3,2,1,0:T(8,128)(2,1)}, bf16[4,4,192,256]{3,2,1,0:T(8,128)(2,1)S(1)}, u32[]{:S(2)}, u32[]{:S(2)}) collective-permute-start(bf16[4,4,192,256]{3,2,1,0:T(8,128)(2,1)} %bitcast.53), channel_id=1, source_target_pairs={{0,1},{1,0},{2,3},{3,2},{4,5},{5,4},{6,7},{7,6},{8,9},{9,8},{10,11... | collective-permute-start | bytes 4718600 | tf_op jit(solution)/shard_map/ppermute | solution.py:254
  142.1 7.9 %collective-permute-start.26 = (bf16[4,256,128]{2,1,0:T(8,128)(2,1)S(1)}, bf16[4,256,128]{2,1,0:T(8,128)(2,1)S(1)}, u32[]{:S(2)}, u32[]{:S(2)}) collective-permute-start(bf16[4,256,128]{2,1,0:T(8,128)(2,1)S(1)} %pad_maximum_fusion.1.h0), channel_id=1, source_target_pairs={{0,12},{4,0},{8,4},{12,8},{1,13},{5,1},{9,5},{13,9},{2,14},{6,2},{... | collective-permute-start | bytes 786440 | tf_op jit(solution)/shard_map/ppermute | solution.py:250
  142.1 9.3 %collective-permute-start.27 = (bf16[4,256,128]{2,1,0:T(8,128)(2,1)S(1)}, bf16[4,256,128]{2,1,0:T(8,128)(2,1)S(1)}, u32[]{:S(2)}, u32[]{:S(2)}) collective-permute-start(bf16[4,256,128]{2,1,0:T(8,128)(2,1)S(1)} %pad_maximum_fusion.1.h0), channel_id=1, source_target_pairs={{0,8},{4,12},{8,0},{12,4},{1,9},{5,13},{9,1},{13,5},{2,10},{6,14},... | collective-permute-start | bytes 786440 | tf_op jit(solution)/shard_map/ppermute | solution.py:250
  142.4 15.0 %collective-permute-start.28 = (bf16[4,256,128]{2,1,0:T(8,128)(2,1)S(1)}, bf16[4,256,128]{2,1,0:T(8,128)(2,1)S(1)}, u32[]{:S(2)}, u32[]{:S(2)}) collective-permute-start(bf16[4,256,128]{2,1,0:T(8,128)(2,1)S(1)} %pad_maximum_fusion.1.h0), channel_id=1, source_target_pairs={{0,4},{4,8},{8,12},{12,0},{1,5},{5,9},{9,13},{13,1},{2,6},{6,10},{... | collective-permute-start | bytes 786440 | tf_op jit(solution)/shard_map/ppermute | solution.py:250
  150.0 7.5 %copy-start.6 = (bf16[4,256,128]{2,1,0:T(8,128)(2,1)}, bf16[4,256,128]{2,1,0:T(8,128)(2,1)S(1)}, u32[]{:S(2)}) copy-start(bf16[4,256,128]{2,1,0:T(8,128)(2,1)S(1)} %collective-permute-done.26.h1) | copy-start | bytes 786436
  151.4 6.1 %copy-start.7 = (bf16[4,256,128]{2,1,0:T(8,128)(2,1)}, bf16[4,256,128]{2,1,0:T(8,128)(2,1)S(1)}, u32[]{:S(2)}) copy-start(bf16[4,256,128]{2,1,0:T(8,128)(2,1)S(1)} %collective-permute-done.27.h2) | copy-start | bytes 786436
  157.5 0.7 copy-start.8
  157.5 1.2 copy-start.3
Sparse Core Ops, SparseCore 0:
  26.9 30.5 all-gather.4
  60.4 67.2 all-gather.6

commit v2 on v1

--- a/solution.py
+++ b/solution.py
@@ -41,7 +41,7 @@
 
 def modulate(y, tokens, tangents, shift, scale):
     rows, width = tokens.shape
-    step = 32
+    step = 64
     token_spec = pl.BlockSpec((step, width), lambda i, s: (i, 0))
     whole_spec = pl.BlockSpec((1, width), lambda i, s: (0, 0))
     return pl.pallas_call(
@@ -210,14 +210,12 @@
 def finish_kernel(place_ref, h0, h1, h2, h3, own_ref, other_ref, tok_ref, tan_ref, gate_ref, out_ref, out_dot_ref):
     rows = tok_ref.shape[0]
     y, zh, c = (place_ref[i] for i in range(3))
-    totals = [None] * own_ref.shape[1]
+    total = None
     for m, ref in enumerate((h0, h1, h2, h3)):
         for first, w_ref in ((2 * c, own_ref), (2 - 2 * c, other_ref)):
             left = jnp.concatenate([ref[(zh - first + 4) % 4], ref[(zh - first + 3) % 4]], axis=1)
-            for b in range(len(totals)):
-                term = dot_nt(left, w_ref[(y + m) % 4, b])
-                totals[b] = term if totals[b] is None else totals[b] + term
-    total = jnp.concatenate(totals, axis=1)
+            term = dot_nt(left, w_ref[(y + m) % 4].reshape(-1, left.shape[1]))
+            total = term if total is None else total + term
     gate = gate_ref[...]
     out_ref[...] = (tok_ref[...].astype(f32) + gate * total[:rows]).astype(bf16)
     out_dot_ref[...] = (tan_ref[...].astype(f32) + gate * total[rows:]).astype(bf16)
@@ -225,21 +223,12 @@
 
 def finish(place, parts, own, other, tokens, tangents, gate):
     rows, cols = tokens.shape
-    step = cols // 2
-    part_spec = pl.BlockSpec(parts[0].shape, lambda n, s: (0, 0, 0))
-    col_spec = pl.BlockSpec((rows, step), lambda n, s: (0, n))
-    weight_spec = pl.BlockSpec((4, 2) + own.shape[2:], lambda n, s: (0, n, 0, 0))
     return pl.pallas_call(
         finish_kernel,
-        grid_spec=pltpu.PrefetchScalarGridSpec(
-            num_scalar_prefetch=1,
-            grid=(2,),
-            in_specs=[part_spec] * 4
-            + [weight_spec, weight_spec, col_spec, col_spec, pl.BlockSpec((1, step), lambda n, s: (0, n))],
-            out_specs=[col_spec, col_spec],
-        ),
+        in_specs=[smem] + [vmem] * 9,
+        out_specs=[vmem] * 2,
         out_shape=[jax.ShapeDtypeStruct((rows, cols), bf16)] * 2,
-        compiler_params=pltpu.CompilerParams(vmem_limit_bytes=56 * MIB),
+        compiler_params=pltpu.CompilerParams(vmem_limit_bytes=24 * MIB),
         cost_estimate=pl.CostEstimate(flops=4 * rows * cols * 2048, bytes_accessed=6 * MIB, transcendentals=0),
     )(place, *parts, own, other, tokens, tangents, gate)
 
@@ -320,9 +309,10 @@
 
     got = {k: from_ahead(blocks[k - 1], "zh", -k) for k in (1, 3)}
     second = along_x(first)
+    got[1], middle_block, *second = lax.optimization_barrier((got[1], blocks[1], *second))
     wave = lax.optimization_barrier((got[1], got[3], *second))
     got[1], got[3], second = wave[0], wave[1], wave[2:]
-    got[2] = from_ahead(after(blocks[1], *wave), "zh", -2)
+    got[2] = from_ahead(middle_block, "zh", -2)
     third = along_x(jnp.concatenate([got[1][:4], got[3][:4]]))
     got[2], third[0] = lax.optimization_barrier((got[2], third[0]))
     fourth = along_x(got[2][:4])

time: 171 us -> 167 us (0.977)
  Pallas kernels: 21.7 us -> 18.3 us
    pallas_call x1, Pallas kernels: 4.69 us -> 2.29 us  [finish(): pl.pallas_call(finish_kernel, in_specs=[smem] + [vmem] * 9, out_specs=[vm...]
    ppermute x18, starting transfers between devices: 22.1 us -> 24.3 us  [from_ahead(): return lax.ppermute(array, axis, [(i, (i - k) % 4) for i in range(4)])]
  transfers between devices with their start and end apart: 32 -> 32, of which waited for: 20 -> 22; matrix products, arithmetic and copies ran while one was open for 3% -> 2% of each run, Pallas kernels for 7% -> 7%
where the time goes in v2:
time: 167 us; the launch traced here: 166 us
  waiting for transfers between devices  84.4 us (51%)
  starting transfers between devices  43.2 us (26%)
  Pallas kernels  18.3 us (11%)
  between operations  14.4 us (9%)
  local copies, waits for them, and re-layouts  5.41 us (3%)
    ppermute x18, waiting for transfers between devices, from_ahead(): return lax.ppermute(array, axis, [(i, (i - k) % 4) for i in range(4)])  55.4 us
    ppermute x18, starting transfers between devices, from_ahead(): return lax.ppermute(array, axis, [(i, (i - k) % 4) for i in range(4)])  24.3 us
    ppermute x3, waiting for transfers between devices, beside(): return lax.ppermute(array, (axis, 'c'), perm)  14.3 us
    ppermute x4, waiting for transfers between devices, swap(): return lax.ppermute(array, axis, [(0, 1), (1, 0)])  9.86 us
    ppermute x4, starting transfers between devices, swap(): return lax.ppermute(array, axis, [(0, 1), (1, 0)])  7.38 us
    ppermute x4, starting transfers between devices, per_device(): heads.append(lax.ppermute(attended[i], ('zh', 'zl', 'c'), perm))  6.57 us
    pallas_call x2, Pallas kernels, project_three(): pl.pallas_call(three_kernel, in_specs=[smem] + [vmem] * 5, out_specs=vmem...  5.99 us
    ppermute x4, waiting for transfers between devices, per_device(): heads.append(lax.ppermute(attended[i], ('zh', 'zl', 'c'), perm))  4.72 us
  transfers between devices with their start and end apart: 32, of which 22 were waited for; matrix products, arithmetic and copies ran while one was open for 2% of the time, Pallas kernels for 7%

profile of v2, /device:TPU:1, one launch (start us, length us, event | category | flops | bytes accessed | tf_op | source)
XLA Modules:
  0.0 166.0 jit_solution(15228519499523852325)
XLA Ops:
  7.2 3.6 %shard_map.104 = (bf16[4,2,128,768]{3,2,1,0:T(8,128)(2,1)}, bf16[2,128,768]{2,1,0:T(8,128)(2,1)}) custom-call(s32[1]{0:T(128)} %bitcast.y_ref, bf16[128,3072]{1,0:T(8,128)(2,1)} %tok_ref.1, bf16[128,3072]{1,0:T(8,128)(2,1)} %tan_ref.1, f32[1,3072]{1,0:T(1,128)} %bitcast.66, f32[1,3072]{1,0:T(1,128)} %bitcast.67), custom_call_target="tpu_custom_call" | custom-call | flops 7864320 | bytes 3145728 | tf_op jit(solution)/shard_map/pallas_call | solution.py:47
  10.8 3.2 %collective-permute-start = (bf16[4,256,768]{2,1,0:T(8,128)(2,1)}, bf16[4,256,768]{2,1,0:T(8,128)(2,1)}, u32[]{:S(2)}, u32[]{:S(2)}) collective-permute-start(bf16[4,256,768]{2,1,0:T(8,128)(2,1)} %bitcast.43), channel_id=1, source_target_pairs={{0,1},{1,0},{2,3},{3,2},{4,5},{5,4},{6,7},{7,6},{8,9},{9,8},{10,11... | collective-permute-start | bytes 4718600 | tf_op jit(solution)/shard_map/ppermute | solution.py:243
  14.0 1.0 dynamic-slice_reduce_fusion
  15.1 9.9 %collective-permute-done.1 = bf16[256,768]{1,0:T(8,128)(2,1)S(1)} collective-permute-done((bf16[256,768]{1,0:T(8,128)(2,1)}, bf16[256,768]{1,0:T(8,128)(2,1)S(1)}, u32[]{:S(2)}, u32[]{:S(2)}) %collective-permute-start.1) | collective-permute-done | bytes 393248 | tf_op jit(solution)/shard_map/ppermute | solution.py:243
  25.8 4.4 %collective-permute-start.2 = (bf16[192,384]{1,0:T(8,128)(2,1)S(1)}, bf16[192,384]{1,0:T(8,128)(2,1)S(1)}, u32[]{:S(2)}, u32[]{:S(2)}) collective-permute-start(bf16[192,384]{1,0:T(8,128)(2,1)S(1)} %bitcast.56), channel_id=1, source_target_pairs={{0,192},{64,0},{128,64},{192,128},{1,193},{65,1},{129,65},{193,129... | collective-permute-start | bytes 442376 | tf_op jit(solution)/shard_map/ppermute | solution.py:239
  30.2 1.0 collective-permute-start.3
  31.2 2.3 %collective-permute-start.4 = (bf16[192,384]{1,0:T(8,128)(2,1)S(1)}, bf16[192,384]{1,0:T(8,128)(2,1)S(1)}, u32[]{:S(2)}, u32[]{:S(2)}) collective-permute-start(bf16[192,384]{1,0:T(8,128)(2,1)S(1)} %bitcast.58), channel_id=1, source_target_pairs={{0,64},{64,128},{128,192},{192,0},{1,65},{65,129},{129,193},{193,1... | collective-permute-start | bytes 442376 | tf_op jit(solution)/shard_map/ppermute | solution.py:239
  33.5 3.5 %collective-permute-done.2 = bf16[192,384]{1,0:T(8,128)(2,1)S(1)} collective-permute-done((bf16[192,384]{1,0:T(8,128)(2,1)S(1)}, bf16[192,384]{1,0:T(8,128)(2,1)S(1)}, u32[]{:S(2)}, u32[]{:S(2)}) %collective-permute-start.2) | collective-permute-done | bytes 147488 | tf_op jit(solution)/shard_map/ppermute | solution.py:239
  37.1 5.1 %collective-permute-done.3 = bf16[192,384]{1,0:T(8,128)(2,1)S(1)} collective-permute-done((bf16[192,384]{1,0:T(8,128)(2,1)S(1)}, bf16[192,384]{1,0:T(8,128)(2,1)S(1)}, u32[]{:S(2)}, u32[]{:S(2)}) %collective-permute-start.3) | collective-permute-done | bytes 147488 | tf_op jit(solution)/shard_map/ppermute | solution.py:239
  42.2 1.6 collective-permute-start.5
  43.8 1.4 collective-permute-start.6
  46.0 7.4 %collective-permute-done.5.w1_ref = bf16[768,384]{1,0:T(8,128)(2,1)S(1)} collective-permute-done((bf16[768,384]{1,0:T(8,128)(2,1)S(1)}, bf16[768,384]{1,0:T(8,128)(2,1)S(1)}, u32[]{:S(2)}, u32[]{:S(2)}) %collective-permute-start.5) | collective-permute-done | bytes 589856 | tf_op jit(solution)/shard_map/ppermute | solution.py:248
  53.4 4.3 %collective-permute-done.6.w3_ref = bf16[768,384]{1,0:T(8,128)(2,1)} collective-permute-done((bf16[768,384]{1,0:T(8,128)(2,1)S(1)}, bf16[768,384]{1,0:T(8,128)(2,1)}, u32[]{:S(2)}, u32[]{:S(2)}) %collective-permute-start.6) | collective-permute-done | bytes 589856 | tf_op jit(solution)/shard_map/ppermute | solution.py:248
  57.8 1.9 %collective-permute-start.8 = (bf16[4,256,768]{2,1,0:T(8,128)(2,1)}, bf16[4,256,768]{2,1,0:T(8,128)(2,1)}, u32[]{:S(2)}, u32[]{:S(2)}) collective-permute-start(bf16[4,256,768]{2,1,0:T(8,128)(2,1)} %bitcast.46), channel_id=1, source_target_pairs={{0,1},{1,0},{2,3},{3,2},{4,5},{5,4},{6,7},{7,6},{8,9},{9,8},{10,11... | collective-permute-start | bytes 4718600 | tf_op jit(solution)/shard_map/ppermute | solution.py:243
  59.7 1.2 collective-permute-start.9
  61.1 3.0 %shard_map.105.near_ref = f32[2,256,384]{2,1,0:T(8,128)S(1)} custom-call(s32[2]{0:T(128)S(1)} %pad_add_fusion.2.spot_ref, bf16[4,256,768]{2,1,0:T(8,128)(2,1)S(1)} %bitcast.44, bf16[4,256,768]{2,1,0:T(8,128)(2,1)} %collective-permute-done.n1_ref, bf16[768,384]{1,0:T(8,128)(2,1)S(1)} %bitcast.51, bf16[768,384]{1,0:T(8,128)(2,1)S(1)} %collective-permute-done.5.w1_ref, ...), custom_call_target="tpu_custom_call" | custom-call | flops 905969664 | bytes 6291456 | tf_op jit(solution)/shard_map/pallas_call | solution.py:83
  64.2 2.9 %shard_map.106.far_ref = f32[2,256,384]{2,1,0:T(8,128)S(1)} custom-call(s32[2]{0:T(128)S(1)} %pad_add_fusion.2.spot_ref, bf16[4,256,768]{2,1,0:T(8,128)(2,1)S(1)} %bitcast.47, bf16[4,256,768]{2,1,0:T(8,128)(2,1)} %collective-permute-done.8.n1_ref.n3_ref, bf16[768,384]{1,0:T(8,128)(2,1)S(1)} %bitcast.52, bf16[768,384]{1,0:T(8,128)(2,1)S(1)} %collective-permute-done.5.w1_ref, ...), custom_call_target="tpu_custom_call" | custom-call | flops 905969664 | bytes 6291456 | tf_op jit(solution)/shard_map/pallas_call | solution.py:83
  67.1 2.6 %collective-permute-done.9.w_ref = bf16[768,384]{1,0:T(8,128)(2,1)} collective-permute-done((bf16[768,384]{1,0:T(8,128)(2,1)S(1)}, bf16[768,384]{1,0:T(8,128)(2,1)}, u32[]{:S(2)}, u32[]{:S(2)}) %collective-permute-start.9) | collective-permute-done | bytes 589856 | tf_op jit(solution)/shard_map/ppermute | solution.py:248
  69.8 3.0 %shard_map.107 = (bf16[4,128,128]{2,1,0:T(8,128)(2,1)S(1)}, bf16[6,128,128]{2,1,0:T(8,128)(2,1)S(1)}, bf16[6,128,128]{2,1,0:T(8,128)(2,1)S(1)}, bf16[6,128,128]{2,1,0:T(8,128)(2,1)S(1)}, bf16[2,128,128]{2,1,0:T(8,128)(2,1)S(1)}) custom-call(s32[5]{0:T(128)S(1)} %stack.92.spot_ref, bf16[4,256,768]{2,1,0:T(8,128)(2,1)S(1)} %bitcast.45, ...), custom_call_target="tpu_custom_call" | custom-call | flops 603979776 | bytes 5242880 | tf_op jit(solution)/shard_map/pallas_call | solution.py:121
  72.8 3.6 %collective-permute-start.10 = (bf16[6,128,128]{2,1,0:T(8,128)(2,1)S(1)}, bf16[6,128,128]{2,1,0:T(8,128)(2,1)S(1)}, u32[]{:S(2)}, u32[]{:S(2)}) collective-permute-start(bf16[6,128,128]{2,1,0:T(8,128)(2,1)S(1)} %get-tuple-element.44), channel_id=1, source_target_pairs={{0,64},{64,128},{128,192},{192,0},{1,65},{65,129},{129,193},{193,1... | collective-permute-start | bytes 589832 | tf_op jit(solution)/shard_map/ppermute | solution.py:239
  77.1 1.2 collective-permute-start.11
  79.1 2.6 %collective-permute-done.11.refs_1_ = bf16[4,128,128]{2,1,0:T(8,128)(2,1)S(1)} collective-permute-done((bf16[4,128,128]{2,1,0:T(8,128)(2,1)S(1)}, bf16[4,128,128]{2,1,0:T(8,128)(2,1)S(1)}, u32[]{:S(2)}, u32[]{:S(2)}) %collective-permute-start.11) | collective-permute-done | bytes 131104 | tf_op jit(solution)/shard_map/ppermute | solution.py:239
  81.8 2.1 %collective-permute-done.12.refs_2_ = bf16[4,128,128]{2,1,0:T(8,128)(2,1)S(1)} collective-permute-done((bf16[4,128,128]{2,1,0:T(8,128)(2,1)S(1)}, bf16[4,128,128]{2,1,0:T(8,128)(2,1)S(1)}, u32[]{:S(2)}, u32[]{:S(2)}) %collective-permute-start.12) | collective-permute-done | bytes 131104 | tf_op jit(solution)/shard_map/ppermute | solution.py:239
  83.9 1.4 collective-permute-done.13.refs_3_
  85.2 8.3 %collective-permute-done.14.refs_12_ = bf16[6,128,128]{2,1,0:T(8,128)(2,1)S(1)} collective-permute-done((bf16[6,128,128]{2,1,0:T(8,128)(2,1)S(1)}, bf16[6,128,128]{2,1,0:T(8,128)(2,1)S(1)}, u32[]{:S(2)}, u32[]{:S(2)}) %collective-permute-start.14) | collective-permute-done | bytes 196640 | tf_op jit(solution)/shard_map/ppermute | solution.py:239
  93.6 1.8 %collective-permute-start.16 = (bf16[8,128,128]{2,1,0:T(8,128)(2,1)S(1)}, bf16[8,128,128]{2,1,0:T(8,128)(2,1)S(1)}, u32[]{:S(2)}, u32[]{:S(2)}) collective-permute-start(bf16[8,128,128]{2,1,0:T(8,128)(2,1)S(1)} %pad_maximum_fusion), channel_id=1, source_target_pairs={{0,48},{16,0},{32,16},{48,32},{1,49},{17,1},{33,17},{49,33},{2,50}... | collective-permute-start | bytes 786440 | tf_op jit(solution)/shard_map/ppermute | solution.py:239
  95.4 2.6 %collective-permute-start.15 = (bf16[6,128,128]{2,1,0:T(8,128)(2,1)S(1)}, bf16[6,128,128]{2,1,0:T(8,128)(2,1)S(1)}, u32[]{:S(2)}, u32[]{:S(2)}) collective-permute-start(bf16[6,128,128]{2,1,0:T(8,128)(2,1)S(1)} %get-tuple-element.54), channel_id=1, source_target_pairs={{0,128},{64,192},{128,0},{192,64},{1,129},{65,193},{129,1},{193,65... | collective-permute-start | bytes 589832 | tf_op jit(solution)/shard_map/ppermute | solution.py:239
  98.7 11.5 %collective-permute-done.15.refs_11_ = bf16[6,128,128]{2,1,0:T(8,128)(2,1)S(1)} collective-permute-done((bf16[6,128,128]{2,1,0:T(8,128)(2,1)S(1)}, bf16[6,128,128]{2,1,0:T(8,128)(2,1)S(1)}, u32[]{:S(2)}, u32[]{:S(2)}) %collective-permute-start.15) | collective-permute-done | bytes 196640 | tf_op jit(solution)/shard_map/ppermute | solution.py:239
  110.4 1.4 collective-permute-start.21
  111.8 1.2 collective-permute-done.18.refs_6_
  113.0 4.0 %collective-permute-done.19.refs_7_ = bf16[4,128,128]{2,1,0:T(8,128)(2,1)S(1)} collective-permute-done((bf16[4,128,128]{2,1,0:T(8,128)(2,1)S(1)}, bf16[4,128,128]{2,1,0:T(8,128)(2,1)S(1)}, u32[]{:S(2)}, u32[]{:S(2)}) %collective-permute-start.19) | collective-permute-done | bytes 131104 | tf_op jit(solution)/shard_map/ppermute | solution.py:239
  117.0 1.3 collective-permute-done.20.refs_8_
  118.3 4.0 %collective-permute-done.21.refs_9_ = bf16[4,128,128]{2,1,0:T(8,128)(2,1)S(1)} collective-permute-done((bf16[4,128,128]{2,1,0:T(8,128)(2,1)S(1)}, bf16[4,128,128]{2,1,0:T(8,128)(2,1)S(1)}, u32[]{:S(2)}, u32[]{:S(2)}) %collective-permute-start.21) | collective-permute-done | bytes 131104 | tf_op jit(solution)/shard_map/ppermute | solution.py:239
  122.3 3.5 %shard_map.108 = (bf16[256,128]{1,0:T(8,128)(2,1)S(1)}, bf16[256,128]{1,0:T(8,128)(2,1)S(1)}, bf16[256,128]{1,0:T(8,128)(2,1)S(1)}, bf16[256,128]{1,0:T(8,128)(2,1)S(1)}) custom-call(s32[4]{0:T(128)S(1)} %pad_add_fusion.1.spot_ref, bf16[4,128,128]{2,1,0:T(8,128)(2,1)S(1)} %get-tuple-element.43.refs_0_, ...), custom_call_target="tpu_custom_call" | custom-call | flops 1610612736 | bytes 3145728 | tf_op jit(solution)/shard_map/pallas_call | solution.py:190
  125.8 2.9 %collective-permute-start.22 = (bf16[256,128]{1,0:T(8,128)(2,1)S(1)}, bf16[256,128]{1,0:T(8,128)(2,1)S(1)}, u32[]{:S(2)}, u32[]{:S(2)}) collective-permute-start(bf16[256,128]{1,0:T(8,128)(2,1)S(1)} %get-tuple-element.60), channel_id=1, source_target_pairs={{0,0},{1,64},{2,128},{3,192},{64,1},{65,65},{66,129},{67,193},{128... | collective-permute-start | bytes 196616 | tf_op jit(solution)/shard_map/ppermute | solution.py:325
  128.7 1.0 collective-permute-start.23
  129.7 2.7 %collective-permute-start.24 = (bf16[256,128]{1,0:T(8,128)(2,1)S(1)}, bf16[256,128]{1,0:T(8,128)(2,1)S(1)}, u32[]{:S(2)}, u32[]{:S(2)}) collective-permute-start(bf16[256,128]{1,0:T(8,128)(2,1)S(1)} %get-tuple-element.62), channel_id=1, source_target_pairs={{0,128},{1,192},{2,0},{3,64},{64,129},{65,193},{66,1},{67,65},{128... | collective-permute-start | bytes 196616 | tf_op jit(solution)/shard_map/ppermute | solution.py:325
  132.6 1.1 collective-permute-done.23
  133.7 1.6 collective-permute-done.24
  135.2 1.8 %collective-permute-done.25 = bf16[256,128]{1,0:T(8,128)(2,1)S(1)} collective-permute-done((bf16[256,128]{1,0:T(8,128)(2,1)S(1)}, bf16[256,128]{1,0:T(8,128)(2,1)S(1)}, u32[]{:S(2)}, u32[]{:S(2)}) %collective-permute-start.25) | collective-permute-done | bytes 65568 | tf_op jit(solution)/shard_map/ppermute | solution.py:325
  137.1 2.2 %collective-permute-start.29 = (bf16[4,4,192,256]{3,2,1,0:T(8,128)(2,1)}, bf16[4,4,192,256]{3,2,1,0:T(8,128)(2,1)S(1)}, u32[]{:S(2)}, u32[]{:S(2)}) collective-permute-start(bf16[4,4,192,256]{3,2,1,0:T(8,128)(2,1)} %bitcast.53), channel_id=1, source_target_pairs={{0,1},{1,0},{2,3},{3,2},{4,5},{5,4},{6,7},{7,6},{8,9},{9,8},{10,11... | collective-permute-start | bytes 4718600 | tf_op jit(solution)/shard_map/ppermute | solution.py:243
  139.3 3.8 %collective-permute-start.27 = (bf16[4,256,128]{2,1,0:T(8,128)(2,1)S(1)}, bf16[4,256,128]{2,1,0:T(8,128)(2,1)S(1)}, u32[]{:S(2)}, u32[]{:S(2)}) collective-permute-start(bf16[4,256,128]{2,1,0:T(8,128)(2,1)S(1)} %pad_maximum_fusion.1.h0), channel_id=1, source_target_pairs={{0,8},{4,12},{8,0},{12,4},{1,9},{5,13},{9,1},{13,5},{2,10},{6,14},... | collective-permute-start | bytes 786440 | tf_op jit(solution)/shard_map/ppermute | solution.py:239
  143.9 1.0 constant_dynamic-slice_fusion
  145.0 2.6 %collective-permute-done.26.h1 = bf16[4,256,128]{2,1,0:T(8,128)(2,1)S(1)} collective-permute-done((bf16[4,256,128]{2,1,0:T(8,128)(2,1)S(1)}, bf16[4,256,128]{2,1,0:T(8,128)(2,1)S(1)}, u32[]{:S(2)}, u32[]{:S(2)}) %collective-permute-start.26) | collective-permute-done | bytes 262176 | tf_op jit(solution)/shard_map/ppermute | solution.py:239
  147.6 1.5 collective-permute-done.27.h2
  149.1 6.3 %collective-permute-done.28.h3 = bf16[4,256,128]{2,1,0:T(8,128)(2,1)S(1)} collective-permute-done((bf16[4,256,128]{2,1,0:T(8,128)(2,1)S(1)}, bf16[4,256,128]{2,1,0:T(8,128)(2,1)S(1)}, u32[]{:S(2)}, u32[]{:S(2)}) %collective-permute-start.28) | collective-permute-done | bytes 262176 | tf_op jit(solution)/shard_map/ppermute | solution.py:239
  155.5 1.4 copy-done.3
  156.9 2.3 %shard_map.109 = (bf16[128,768]{1,0:T(8,128)(2,1)}, bf16[128,768]{1,0:T(8,128)(2,1)}) custom-call(s32[3]{0:T(128)S(1)} %pad_add_fusion.place_ref, bf16[4,256,128]{2,1,0:T(8,128)(2,1)S(1)} %pad_maximum_fusion.1.h0, bf16[4,256,128]{2,1,0:T(8,128)(2,1)S(1)} %collective-permute-done.26.h1, bf16[4,256,128]{2,1,0:T(8,128)(2,1)S(1)} %collective-permute-done.27.h2, ...), custom_call_target="tpu_custom_call" | custom-call | flops 805306368 | bytes 6291456 | tf_op jit(solution)/shard_map/pallas_call | solution.py:226
  (64 shorter events, 5.8 us)
Async XLA Ops:
  7.2 6.9 %copy-start = (bf16[192,4,3,128]{3,1,2,0:T(4,128)(2,1)S(1)}, bf16[192,4,3,128]{3,1,2,0:T(4,128)(2,1)}, u32[]{:S(2)}) copy-start(bf16[192,4,3,128]{3,1,2,0:T(4,128)(2,1)} %param.11) | copy-start | bytes 1769476
  7.2 50.6 %all-gather.5.cloned.1.call-start = ((), (), s32[]{:S(2)}) async-start(), calls=%async_computation | async-start | bytes 1966080 | tf_op jit(solution)/shard_map/all_gather | solution.py:285
  10.8 14.1 %collective-permute-start = (bf16[4,256,768]{2,1,0:T(8,128)(2,1)}, bf16[4,256,768]{2,1,0:T(8,128)(2,1)}, u32[]{:S(2)}, u32[]{:S(2)}) collective-permute-start(bf16[4,256,768]{2,1,0:T(8,128)(2,1)} %bitcast.43), channel_id=1, source_target_pairs={{0,1},{1,0},{2,3},{3,2},{4,5},{5,4},{6,7},{7,6},{8,9},{9,8},{10,11... | collective-permute-start | bytes 4718600 | tf_op jit(solution)/shard_map/ppermute | solution.py:243
  14.0 10.9 %collective-permute-start.1 = (bf16[256,768]{1,0:T(8,128)(2,1)}, bf16[256,768]{1,0:T(8,128)(2,1)S(1)}, u32[]{:S(2)}, u32[]{:S(2)}) collective-permute-start(bf16[256,768]{1,0:T(8,128)(2,1)} %bitcast.70), channel_id=1, source_target_pairs={{0,2},{2,0},{1,3},{3,1},{4,6},{6,4},{5,7},{7,5},{8,10},{10,8},{9,1... | collective-permute-start | bytes 1179656 | tf_op jit(solution)/shard_map/ppermute | solution.py:243
  14.0 31.1 %copy-start.6 = (bf16[192,4,128]{2,1,0:T(4,128)(2,1)S(1)}, bf16[192,4,128]{2,1,0:T(4,128)(2,1)}, u32[]{:S(2)}) copy-start(bf16[192,4,128]{2,1,0:T(4,128)(2,1)} %param.12) | copy-start | bytes 589828
  15.0 46.1 %copy-start.7 = (f32[128]{0:T(128)S(1)}, f32[128]{0:T(128)}, u32[]{:S(2)}) copy-start(f32[128]{0:T(128)} %param.17) | copy-start | bytes 1540
  15.0 46.1 %copy-start.8 = (f32[128]{0:T(128)S(1)}, f32[128]{0:T(128)}, u32[]{:S(2)}) copy-start(f32[128]{0:T(128)} %param.16) | copy-start | bytes 1540
  15.0 46.1 %copy-start.1 = (bf16[4,2,128,768]{3,2,1,0:T(8,128)(2,1)S(1)}, bf16[4,2,128,768]{3,2,1,0:T(8,128)(2,1)}, u32[]{:S(2)}) copy-start(bf16[4,2,128,768]{3,2,1,0:T(8,128)(2,1)} %get-tuple-element.34) | copy-start | bytes 4718596
  24.9 0.8 copy-start.4
  25.7 111.4 %all-gather.7.cloned.1.call-start = ((), (), s32[]{:S(2)}) async-start(), calls=%async_computation.1 | async-start | bytes 1671168 | tf_op jit(solution)/shard_map/all_gather | solution.py:305
  25.8 11.2 %collective-permute-start.2 = (bf16[192,384]{1,0:T(8,128)(2,1)S(1)}, bf16[192,384]{1,0:T(8,128)(2,1)S(1)}, u32[]{:S(2)}, u32[]{:S(2)}) collective-permute-start(bf16[192,384]{1,0:T(8,128)(2,1)S(1)} %bitcast.56), channel_id=1, source_target_pairs={{0,192},{64,0},{128,64},{192,128},{1,193},{65,1},{129,65},{193,129... | collective-permute-start | bytes 442376 | tf_op jit(solution)/shard_map/ppermute | solution.py:239
  30.2 12.0 %collective-permute-start.3 = (bf16[192,384]{1,0:T(8,128)(2,1)S(1)}, bf16[192,384]{1,0:T(8,128)(2,1)S(1)}, u32[]{:S(2)}, u32[]{:S(2)}) collective-permute-start(bf16[192,384]{1,0:T(8,128)(2,1)S(1)} %bitcast.57), channel_id=1, source_target_pairs={{0,128},{64,192},{128,0},{192,64},{1,129},{65,193},{129,1},{193,65... | collective-permute-start | bytes 442376 | tf_op jit(solution)/shard_map/ppermute | solution.py:239
  31.2 11.0 %collective-permute-start.4 = (bf16[192,384]{1,0:T(8,128)(2,1)S(1)}, bf16[192,384]{1,0:T(8,128)(2,1)S(1)}, u32[]{:S(2)}, u32[]{:S(2)}) collective-permute-start(bf16[192,384]{1,0:T(8,128)(2,1)S(1)} %bitcast.58), channel_id=1, source_target_pairs={{0,64},{64,128},{128,192},{192,0},{1,65},{65,129},{129,193},{193,1... | collective-permute-start | bytes 442376 | tf_op jit(solution)/shard_map/ppermute | solution.py:239
  42.2 11.1 %collective-permute-start.5 = (bf16[768,384]{1,0:T(8,128)(2,1)S(1)}, bf16[768,384]{1,0:T(8,128)(2,1)S(1)}, u32[]{:S(2)}, u32[]{:S(2)}) collective-permute-start(bf16[768,384]{1,0:T(8,128)(2,1)S(1)} %bitcast.49), channel_id=1, source_target_pairs={{0,48},{1,17},{16,0},{17,33},{32,16},{33,49},{48,32},{49,1},{2,50}... | collective-permute-start | bytes 1769480 | tf_op jit(solution)/shard_map/ppermute | solution.py:248
  43.8 13.9 %collective-permute-start.6 = (bf16[768,384]{1,0:T(8,128)(2,1)S(1)}, bf16[768,384]{1,0:T(8,128)(2,1)}, u32[]{:S(2)}, u32[]{:S(2)}) collective-permute-start(bf16[768,384]{1,0:T(8,128)(2,1)S(1)} %bitcast.50), channel_id=1, source_target_pairs={{0,16},{1,49},{16,32},{17,1},{32,48},{33,17},{48,0},{49,33},{2,18}... | collective-permute-start | bytes 1769480 | tf_op jit(solution)/shard_map/ppermute | solution.py:248
  45.3 0.7 collective-permute-start.7
  46.0 11.7 %copy-start.5 = (bf16[192,256]{1,0:T(8,128)(2,1)}, bf16[192,256]{1,0:T(8,128)(2,1)S(1)}, u32[]{:S(2)}) copy-start(bf16[192,256]{1,0:T(8,128)(2,1)S(1)} %collective-permute-done.7) | copy-start | bytes 294916
  57.8 6.4 %collective-permute-start.8 = (bf16[4,256,768]{2,1,0:T(8,128)(2,1)}, bf16[4,256,768]{2,1,0:T(8,128)(2,1)}, u32[]{:S(2)}, u32[]{:S(2)}) collective-permute-start(bf16[4,256,768]{2,1,0:T(8,128)(2,1)} %bitcast.46), channel_id=1, source_target_pairs={{0,1},{1,0},{2,3},{3,2},{4,5},{5,4},{6,7},{7,6},{8,9},{9,8},{10,11... | collective-permute-start | bytes 4718600 | tf_op jit(solution)/shard_map/ppermute | solution.py:243
  59.7 10.1 %collective-permute-start.9 = (bf16[768,384]{1,0:T(8,128)(2,1)S(1)}, bf16[768,384]{1,0:T(8,128)(2,1)}, u32[]{:S(2)}, u32[]{:S(2)}) collective-permute-start(bf16[768,384]{1,0:T(8,128)(2,1)S(1)} %collective-permute-done.5.w1_ref), channel_id=1, source_target_pairs={{0,48},{1,17},{16,0},{17,33},{32,16},{33,49},{48,32},{49,1},{2,50}... | collective-permute-start | bytes 1769480 | tf_op jit(solution)/shard_map/ppermute | solution.py:248
  61.1 3.1 %copy-start.2 = (bf16[1024,768]{1,0:T(8,128)(2,1)S(1)}, bf16[1024,768]{1,0:T(8,128)(2,1)}, u32[]{:S(2)}) copy-start(bf16[1024,768]{1,0:T(8,128)(2,1)} %all-gather.5.cloned.1.call-done) | copy-start | bytes 4718596
  72.8 12.5 %collective-permute-start.10 = (bf16[6,128,128]{2,1,0:T(8,128)(2,1)S(1)}, bf16[6,128,128]{2,1,0:T(8,128)(2,1)S(1)}, u32[]{:S(2)}, u32[]{:S(2)}) collective-permute-start(bf16[6,128,128]{2,1,0:T(8,128)(2,1)S(1)} %get-tuple-element.44), channel_id=1, source_target_pairs={{0,64},{64,128},{128,192},{192,0},{1,65},{65,129},{129,193},{193,1... | collective-permute-start | bytes 589832 | tf_op jit(solution)/shard_map/ppermute | solution.py:239
  76.3 17.2 %collective-permute-start.14 = (bf16[6,128,128]{2,1,0:T(8,128)(2,1)S(1)}, bf16[6,128,128]{2,1,0:T(8,128)(2,1)S(1)}, u32[]{:S(2)}, u32[]{:S(2)}) collective-permute-start(bf16[6,128,128]{2,1,0:T(8,128)(2,1)S(1)} %get-tuple-element.47), channel_id=1, source_target_pairs={{0,192},{64,0},{128,64},{192,128},{1,193},{65,1},{129,65},{193,129... | collective-permute-start | bytes 589832 | tf_op jit(solution)/shard_map/ppermute | solution.py:239
  77.1 4.6 %collective-permute-start.11 = (bf16[4,128,128]{2,1,0:T(8,128)(2,1)S(1)}, bf16[4,128,128]{2,1,0:T(8,128)(2,1)S(1)}, u32[]{:S(2)}, u32[]{:S(2)}) collective-permute-start(bf16[4,128,128]{2,1,0:T(8,128)(2,1)S(1)} %get-tuple-element.43.refs_0_), channel_id=1, source_target_pairs={{0,48},{16,0},{32,16},{48,32},{1,49},{17,1},{33,17},{49,33},{2,50}... | collective-permute-start | bytes 393224 | tf_op jit(solution)/shard_map/ppermute | solution.py:239
  78.3 5.6 %collective-permute-start.12 = (bf16[4,128,128]{2,1,0:T(8,128)(2,1)S(1)}, bf16[4,128,128]{2,1,0:T(8,128)(2,1)S(1)}, u32[]{:S(2)}, u32[]{:S(2)}) collective-permute-start(bf16[4,128,128]{2,1,0:T(8,128)(2,1)S(1)} %get-tuple-element.43.refs_0_), channel_id=1, source_target_pairs={{0,32},{16,48},{32,0},{48,16},{1,33},{17,49},{33,1},{49,17},{2,34}... | collective-permute-start | bytes 393224 | tf_op jit(solution)/shard_map/ppermute | solution.py:239
  78.7 6.5 %collective-permute-start.13 = (bf16[4,128,128]{2,1,0:T(8,128)(2,1)S(1)}, bf16[4,128,128]{2,1,0:T(8,128)(2,1)S(1)}, u32[]{:S(2)}, u32[]{:S(2)}) collective-permute-start(bf16[4,128,128]{2,1,0:T(8,128)(2,1)S(1)} %get-tuple-element.43.refs_0_), channel_id=1, source_target_pairs={{0,16},{16,32},{32,48},{48,0},{1,17},{17,33},{33,49},{49,1},{2,18}... | collective-permute-start | bytes 393224 | tf_op jit(solution)/shard_map/ppermute | solution.py:239
  93.6 16.6 %collective-permute-start.16 = (bf16[8,128,128]{2,1,0:T(8,128)(2,1)S(1)}, bf16[8,128,128]{2,1,0:T(8,128)(2,1)S(1)}, u32[]{:S(2)}, u32[]{:S(2)}) collective-permute-start(bf16[8,128,128]{2,1,0:T(8,128)(2,1)S(1)} %pad_maximum_fusion), channel_id=1, source_target_pairs={{0,48},{16,0},{32,16},{48,32},{1,49},{17,1},{33,17},{49,33},{2,50}... | collective-permute-start | bytes 786440 | tf_op jit(solution)/shard_map/ppermute | solution.py:239
  95.4 14.8 %collective-permute-start.15 = (bf16[6,128,128]{2,1,0:T(8,128)(2,1)S(1)}, bf16[6,128,128]{2,1,0:T(8,128)(2,1)S(1)}, u32[]{:S(2)}, u32[]{:S(2)}) collective-permute-start(bf16[6,128,128]{2,1,0:T(8,128)(2,1)S(1)} %get-tuple-element.54), channel_id=1, source_target_pairs={{0,128},{64,192},{128,0},{192,64},{1,129},{65,193},{129,1},{193,65... | collective-permute-start | bytes 589832 | tf_op jit(solution)/shard_map/ppermute | solution.py:239
  98.0 13.8 %collective-permute-start.17 = (bf16[8,128,128]{2,1,0:T(8,128)(2,1)S(1)}, bf16[8,128,128]{2,1,0:T(8,128)(2,1)S(1)}, u32[]{:S(2)}, u32[]{:S(2)}) collective-permute-start(bf16[8,128,128]{2,1,0:T(8,128)(2,1)S(1)} %pad_maximum_fusion), channel_id=1, source_target_pairs={{0,32},{16,48},{32,0},{48,16},{1,33},{17,49},{33,1},{49,17},{2,34}... | collective-permute-start | bytes 786440 | tf_op jit(solution)/shard_map/ppermute | solution.py:239
  98.0 15.0 %collective-permute-start.18 = (bf16[8,128,128]{2,1,0:T(8,128)(2,1)S(1)}, bf16[8,128,128]{2,1,0:T(8,128)(2,1)S(1)}, u32[]{:S(2)}, u32[]{:S(2)}) collective-permute-start(bf16[8,128,128]{2,1,0:T(8,128)(2,1)S(1)} %pad_maximum_fusion), channel_id=1, source_target_pairs={{0,16},{16,32},{32,48},{48,0},{1,17},{17,33},{33,49},{49,1},{2,18}... | collective-permute-start | bytes 786440 | tf_op jit(solution)/shard_map/ppermute | solution.py:239
  110.2 6.8 %collective-permute-start.19 = (bf16[4,128,128]{2,1,0:T(8,128)(2,1)S(1)}, bf16[4,128,128]{2,1,0:T(8,128)(2,1)S(1)}, u32[]{:S(2)}, u32[]{:S(2)}) collective-permute-start(bf16[4,128,128]{2,1,0:T(8,128)(2,1)S(1)} %slice.11), channel_id=1, source_target_pairs={{0,48},{16,0},{32,16},{48,32},{1,49},{17,1},{33,17},{49,33},{2,50}... | collective-permute-start | bytes 393224 | tf_op jit(solution)/shard_map/ppermute | solution.py:239
  110.3 8.0 %collective-permute-start.20 = (bf16[4,128,128]{2,1,0:T(8,128)(2,1)S(1)}, bf16[4,128,128]{2,1,0:T(8,128)(2,1)S(1)}, u32[]{:S(2)}, u32[]{:S(2)}) collective-permute-start(bf16[4,128,128]{2,1,0:T(8,128)(2,1)S(1)} %slice.11), channel_id=1, source_target_pairs={{0,32},{16,48},{32,0},{48,16},{1,33},{17,49},{33,1},{49,17},{2,34}... | collective-permute-start | bytes 393224 | tf_op jit(solution)/shard_map/ppermute | solution.py:239
  110.4 11.9 %collective-permute-start.21 = (bf16[4,128,128]{2,1,0:T(8,128)(2,1)S(1)}, bf16[4,128,128]{2,1,0:T(8,128)(2,1)S(1)}, u32[]{:S(2)}, u32[]{:S(2)}) collective-permute-start(bf16[4,128,128]{2,1,0:T(8,128)(2,1)S(1)} %slice.11), channel_id=1, source_target_pairs={{0,16},{16,32},{32,48},{48,0},{1,17},{17,33},{33,49},{49,1},{2,18}... | collective-permute-start | bytes 393224 | tf_op jit(solution)/shard_map/ppermute | solution.py:239
  125.8 6.8 %collective-permute-start.22 = (bf16[256,128]{1,0:T(8,128)(2,1)S(1)}, bf16[256,128]{1,0:T(8,128)(2,1)S(1)}, u32[]{:S(2)}, u32[]{:S(2)}) collective-permute-start(bf16[256,128]{1,0:T(8,128)(2,1)S(1)} %get-tuple-element.60), channel_id=1, source_target_pairs={{0,0},{1,64},{2,128},{3,192},{64,1},{65,65},{66,129},{67,193},{128... | collective-permute-start | bytes 196616 | tf_op jit(solution)/shard_map/ppermute | solution.py:325
  128.7 5.0 %collective-permute-start.23 = (bf16[256,128]{1,0:T(8,128)(2,1)S(1)}, bf16[256,128]{1,0:T(8,128)(2,1)S(1)}, u32[]{:S(2)}, u32[]{:S(2)}) collective-permute-start(bf16[256,128]{1,0:T(8,128)(2,1)S(1)} %get-tuple-element.61), channel_id=1, source_target_pairs={{0,64},{1,128},{2,192},{3,0},{64,65},{65,129},{66,193},{67,1},{128... | collective-permute-start | bytes 196616 | tf_op jit(solution)/shard_map/ppermute | solution.py:325
  129.7 5.6 %collective-permute-start.24 = (bf16[256,128]{1,0:T(8,128)(2,1)S(1)}, bf16[256,128]{1,0:T(8,128)(2,1)S(1)}, u32[]{:S(2)}, u32[]{:S(2)}) collective-permute-start(bf16[256,128]{1,0:T(8,128)(2,1)S(1)} %get-tuple-element.62), channel_id=1, source_target_pairs={{0,128},{1,192},{2,0},{3,64},{64,129},{65,193},{66,1},{67,65},{128... | collective-permute-start | bytes 196616 | tf_op jit(solution)/shard_map/ppermute | solution.py:325
  132.3 4.7 %collective-permute-start.25 = (bf16[256,128]{1,0:T(8,128)(2,1)S(1)}, bf16[256,128]{1,0:T(8,128)(2,1)S(1)}, u32[]{:S(2)}, u32[]{:S(2)}) collective-permute-start(bf16[256,128]{1,0:T(8,128)(2,1)S(1)} %get-tuple-element.63), channel_id=1, source_target_pairs={{0,192},{1,0},{2,64},{3,128},{64,193},{65,1},{66,65},{67,129},{128... | collective-permute-start | bytes 196616 | tf_op jit(solution)/shard_map/ppermute | solution.py:325
  137.1 18.3 %collective-permute-start.29 = (bf16[4,4,192,256]{3,2,1,0:T(8,128)(2,1)}, bf16[4,4,192,256]{3,2,1,0:T(8,128)(2,1)S(1)}, u32[]{:S(2)}, u32[]{:S(2)}) collective-permute-start(bf16[4,4,192,256]{3,2,1,0:T(8,128)(2,1)} %bitcast.53), channel_id=1, source_target_pairs={{0,1},{1,0},{2,3},{3,2},{4,5},{5,4},{6,7},{7,6},{8,9},{9,8},{10,11... | collective-permute-start | bytes 4718600 | tf_op jit(solution)/shard_map/ppermute | solution.py:243
  139.3 8.3 %collective-permute-start.26 = (bf16[4,256,128]{2,1,0:T(8,128)(2,1)S(1)}, bf16[4,256,128]{2,1,0:T(8,128)(2,1)S(1)}, u32[]{:S(2)}, u32[]{:S(2)}) collective-permute-start(bf16[4,256,128]{2,1,0:T(8,128)(2,1)S(1)} %pad_maximum_fusion.1.h0), channel_id=1, source_target_pairs={{0,12},{4,0},{8,4},{12,8},{1,13},{5,1},{9,5},{13,9},{2,14},{6,2},{... | collective-permute-start | bytes 786440 | tf_op jit(solution)/shard_map/ppermute | solution.py:239
  139.3 9.8 %collective-permute-start.27 = (bf16[4,256,128]{2,1,0:T(8,128)(2,1)S(1)}, bf16[4,256,128]{2,1,0:T(8,128)(2,1)S(1)}, u32[]{:S(2)}, u32[]{:S(2)}) collective-permute-start(bf16[4,256,128]{2,1,0:T(8,128)(2,1)S(1)} %pad_maximum_fusion.1.h0), channel_id=1, source_target_pairs={{0,8},{4,12},{8,0},{12,4},{1,9},{5,13},{9,1},{13,5},{2,10},{6,14},... | collective-permute-start | bytes 786440 | tf_op jit(solution)/shard_map/ppermute | solution.py:239
  143.1 12.4 %collective-permute-start.28 = (bf16[4,256,128]{2,1,0:T(8,128)(2,1)S(1)}, bf16[4,256,128]{2,1,0:T(8,128)(2,1)S(1)}, u32[]{:S(2)}, u32[]{:S(2)}) collective-permute-start(bf16[4,256,128]{2,1,0:T(8,128)(2,1)S(1)} %pad_maximum_fusion.1.h0), channel_id=1, source_target_pairs={{0,4},{4,8},{8,12},{12,0},{1,5},{5,9},{9,13},{13,1},{2,6},{6,10},{... | collective-permute-start | bytes 786440 | tf_op jit(solution)/shard_map/ppermute | solution.py:239
  155.5 1.4 copy-start.3
Sparse Core Ops, SparseCore 0:
  25.8 30.5 all-gather.4
  59.4 70.5 all-gather.6

commit v3 on v2

--- a/solution.py
+++ b/solution.py
@@ -91,7 +91,7 @@
 
 
 def last_kernel(spot_ref, n0_ref, n1_ref, n2_ref, n3_ref, w_ref, near_ref, far_ref, gain_ref, *refs):
-    *out_refs, own_ref, held_ref = refs
+    *out_refs, held_ref = refs
     rows = n0_ref.shape[1] // 2
     for r, ref in enumerate((n0_ref, n1_ref, n2_ref, n3_ref)):
         before = near_ref[r] if r < 2 else far_ref[r - 2]
@@ -107,9 +107,9 @@
             at = (4, 0, 2)[kind]
             held_ref[r, at] = part.astype(bf16)
             held_ref[r, at + 1] = part_dot.astype(bf16)
-    for k, ref in enumerate(out_refs):
-        ref[...] = held_ref[spot_ref[1 + k], : ref.shape[0]]
-    own_ref[...] = held_ref[spot_ref[1], 4:]
+    for k in range(4):
+        out_refs[k][...] = held_ref[spot_ref[1 + k], :4]
+        out_refs[4 + k][...] = held_ref[spot_ref[1 + k], 4:]
 
 
 def project_last(spot, parts, weight, near, far, gains):
@@ -117,7 +117,7 @@
     whole = lambda shape: pl.BlockSpec(shape, lambda n, s: (0,) * len(shape))
     part_spec = pl.BlockSpec((1, rows, depth), lambda n, s: (s[0], 0, 0))
     extra = [weight, near, far, gains]
-    shapes = [(4, rows // 2, 128)] + [(6, rows // 2, 128)] * 3 + [(2, rows // 2, 128)]
+    shapes = [(4, rows // 2, 128)] * 4 + [(2, rows // 2, 128)] * 4
     return pl.pallas_call(
         last_kernel,
         grid_spec=pltpu.PrefetchScalarGridSpec(
@@ -134,16 +134,14 @@
 
 
 def attend_kernel(counts, spot_ref, *refs):
-    kv_refs = refs[: len(counts)]
-    own_refs = refs[len(counts) : len(counts) + 3]
-    first_ref, *out_refs, q_cat, k_cat, v_cat, e_ref, sd_ref, held_ref = refs[len(counts) + 3 :]
+    kv_refs, q_refs = refs[: len(counts)], refs[len(counts) : len(counts) + 4]
+    *out_refs, q_cat, k_cat, v_cat, e_ref, sd_ref, held_ref = refs[len(counts) + 4 :]
     rows = 128
-    for i, ref in enumerate((first_ref,) + own_refs):
-        at = 0 if i == 0 else 4
-        q_cat[i * rows : (i + 1) * rows, :128] = ref[at + 1]
-        q_cat[i * rows : (i + 1) * rows, 128:] = ref[at]
+    for i, ref in enumerate(q_refs):
+        q_cat[i * rows : (i + 1) * rows, :128] = ref[1]
+        q_cat[i * rows : (i + 1) * rows, 128:] = ref[0]
     at = 0
-    for count, ref in zip(counts + (1,) * 3, kv_refs + own_refs):
+    for count, ref in zip(counts, kv_refs):
         for n in range(count):
             k_cat[at : at + rows, :128] = ref[4 * n]
             k_cat[at : at + rows, 128:] = ref[4 * n + 1]
@@ -184,9 +182,9 @@
         ref[...] = held_ref[spot_ref[i]]
 
 
-def attend(spot, key_parts, own_parts, first_queries):
+def attend(spot, key_parts, query_parts):
     counts = tuple(part.shape[0] // 4 for part in key_parts)
-    keys = 128 * (sum(counts) + 3)
+    keys = 128 * sum(counts)
     return pl.pallas_call(
         functools.partial(attend_kernel, counts),
         in_specs=[smem] + [vmem] * (len(counts) + 4),
@@ -204,7 +202,7 @@
         cost_estimate=pl.CostEstimate(
             flops=2 * 512 * keys * 128 * 6, bytes_accessed=3 * MIB, transcendentals=512 * keys
         ),
-    )(spot, *key_parts, *own_parts, first_queries)
+    )(spot, *key_parts, *query_parts)
 
 
 def finish_kernel(place_ref, h0, h1, h2, h3, own_ref, other_ref, tok_ref, tan_ref, gate_ref, out_ref, out_dot_ref):
@@ -298,7 +296,7 @@
     far_total = project_three(spot, [far_own, far_other], three)
     gains = jnp.stack([query_gain, key_gain])
     spot = jnp.stack([ahead(x, 2)] + [ahead(zh, k) ^ clip for k in range(4)]).astype(jnp.int32)
-    first, *blocks, first_queries = project_last(
+    first, *blocks = project_last(
         spot, [normed, near, far_own, far_other], opposite, near_total, far_total, gains
     )
 
@@ -307,17 +305,20 @@
     def along_x(group):
         return [from_ahead(group, "x", m) for m in range(1, 4)]
 
+    queries = {k: blocks[3 + k] for k in range(4)}
     got = {k: from_ahead(blocks[k - 1], "zh", -k) for k in (1, 3)}
     second = along_x(first)
-    got[1], middle_block, *second = lax.optimization_barrier((got[1], blocks[1], *second))
-    wave = lax.optimization_barrier((got[1], got[3], *second))
-    got[1], got[3], second = wave[0], wave[1], wave[2:]
-    got[2] = from_ahead(middle_block, "zh", -2)
-    third = along_x(jnp.concatenate([got[1][:4], got[3][:4]]))
+    got[1], got[3], *second = lax.optimization_barrier((got[1], got[3], *second))
+    got[2] = from_ahead(after(blocks[1], got[1], got[3], *second), "zh", -2)
+    third = along_x(jnp.concatenate([got[1], got[3]]))
+    queries[1] = from_ahead(after(queries[1], got[1], got[3]), "zh", -1)
     got[2], third[0] = lax.optimization_barrier((got[2], third[0]))
-    fourth = along_x(got[2][:4])
+    fourth = along_x(got[2])
+    queries[2] = from_ahead(after(queries[2], got[2]), "zh", -2)
+    queries[3] = from_ahead(after(queries[3], got[2]), "zh", -3)
     spot = jnp.stack([ahead(zh, -clip - i) for i in range(4)]).astype(jnp.int32)
-    attended = attend(spot, [first, *second, *third, *fourth], [got[k] for k in (1, 2, 3)], first_queries)
+    key_parts = [first, got[1], got[2], got[3], *second, *third, *fourth]
+    attended = attend(spot, key_parts, [queries[k] for k in range(4)])
 
     heads = []
     for i in range(4):

time: 167 us -> 172 us (1.030)
  starting transfers between devices: 43.2 us -> 57.8 us
  waiting for transfers between devices: 84.4 us -> 75.9 us
    ppermute x4, starting transfers between devices: 6.57 us -> 16.3 us  [per_device(): heads.append(lax.ppermute(attended[i], ('zh', 'zl', 'c'), perm))]
    ppermute x18 -> x21, waiting for transfers between devices: 55.4 us -> 46.6 us  [from_ahead(): return lax.ppermute(array, axis, [(i, (i - k) % 4) for i in range(4)])]
    ppermute x18 -> x21, starting transfers between devices: 24.3 us -> 31.3 us  [from_ahead(): return lax.ppermute(array, axis, [(i, (i - k) % 4) for i in range(4)])]
    ppermute x4, starting transfers between devices: 7.38 us -> 5.28 us  [swap(): return lax.ppermute(array, axis, [(0, 1), (1, 0)])]
  transfers between devices with their start and end apart: 32 -> 35, of which waited for: 22 -> 16; matrix products, arithmetic and copies ran while one was open for 2% -> 2% of each run, Pallas kernels for 7% -> 7%
where the time goes in v3:
time: 172 us
  waiting for transfers between devices  75.9 us (44%)
  starting transfers between devices  57.8 us (34%)
  Pallas kernels  18.4 us (11%)
  between operations  14.4 us (8%)
  local copies, waits for them, and re-layouts  5.41 us (3%)
    ppermute x21, waiting for transfers between devices, from_ahead(): return lax.ppermute(array, axis, [(i, (i - k) % 4) for i in range(4)])  46.6 us
    ppermute x21, starting transfers between devices, from_ahead(): return lax.ppermute(array, axis, [(i, (i - k) % 4) for i in range(4)])  31.3 us
    ppermute x4, starting transfers between devices, per_device(): heads.append(lax.ppermute(attended[i], ('zh', 'zl', 'c'), perm))  16.3 us
    ppermute x3, waiting for transfers between devices, beside(): return lax.ppermute(array, (axis, 'c'), perm)  14.3 us
    ppermute x4, waiting for transfers between devices, swap(): return lax.ppermute(array, axis, [(0, 1), (1, 0)])  9.86 us
    pallas_call x2, Pallas kernels, project_three(): pl.pallas_call(three_kernel, in_specs=[smem] + [vmem] * 5, out_specs=vmem...  5.99 us
    ppermute x4, starting transfers between devices, swap(): return lax.ppermute(array, axis, [(0, 1), (1, 0)])  5.28 us
    ppermute x4, waiting for transfers between devices, per_device(): heads.append(lax.ppermute(attended[i], ('zh', 'zl', 'c'), perm))  5.03 us
  transfers between devices with their start and end apart: 35, of which 16 were waited for; matrix products, arithmetic and copies ran while one was open for 2% of the time, Pallas kernels for 7%

profile of v3, /device:TPU:1, one launch (start us, length us, event | category | flops | bytes accessed | tf_op | source)
XLA Modules:
  0.0 172.1 jit_solution(1475358195639692805)
XLA Ops:
  7.2 3.6 %shard_map.104 = (bf16[4,2,128,768]{3,2,1,0:T(8,128)(2,1)}, bf16[2,128,768]{2,1,0:T(8,128)(2,1)}) custom-call(s32[1]{0:T(128)} %bitcast.y_ref, bf16[128,3072]{1,0:T(8,128)(2,1)} %tok_ref.1, bf16[128,3072]{1,0:T(8,128)(2,1)} %tan_ref.1, f32[1,3072]{1,0:T(1,128)} %bitcast.66, f32[1,3072]{1,0:T(1,128)} %bitcast.67), custom_call_target="tpu_custom_call" | custom-call | flops 7864320 | bytes 3145728 | tf_op jit(solution)/shard_map/pallas_call | solution.py:47
  10.8 3.2 %collective-permute-start = (bf16[4,256,768]{2,1,0:T(8,128)(2,1)}, bf16[4,256,768]{2,1,0:T(8,128)(2,1)}, u32[]{:S(2)}, u32[]{:S(2)}) collective-permute-start(bf16[4,256,768]{2,1,0:T(8,128)(2,1)} %bitcast.43), channel_id=1, source_target_pairs={{0,1},{1,0},{2,3},{3,2},{4,5},{5,4},{6,7},{7,6},{8,9},{9,8},{10,11... | collective-permute-start | bytes 4718600 | tf_op jit(solution)/shard_map/ppermute | solution.py:241
  14.1 1.0 dynamic-slice_reduce_fusion
  15.1 9.9 %collective-permute-done.1 = bf16[256,768]{1,0:T(8,128)(2,1)S(1)} collective-permute-done((bf16[256,768]{1,0:T(8,128)(2,1)}, bf16[256,768]{1,0:T(8,128)(2,1)S(1)}, u32[]{:S(2)}, u32[]{:S(2)}) %collective-permute-start.1) | collective-permute-done | bytes 393248 | tf_op jit(solution)/shard_map/ppermute | solution.py:241
  25.0 0.8 copy-done.4
  25.9 4.4 %collective-permute-start.2 = (bf16[192,384]{1,0:T(8,128)(2,1)S(1)}, bf16[192,384]{1,0:T(8,128)(2,1)S(1)}, u32[]{:S(2)}, u32[]{:S(2)}) collective-permute-start(bf16[192,384]{1,0:T(8,128)(2,1)S(1)} %bitcast.56), channel_id=1, source_target_pairs={{0,192},{64,0},{128,64},{192,128},{1,193},{65,1},{129,65},{193,129... | collective-permute-start | bytes 442376 | tf_op jit(solution)/shard_map/ppermute | solution.py:237
  30.2 1.0 collective-permute-start.3
  31.2 2.3 %collective-permute-start.4 = (bf16[192,384]{1,0:T(8,128)(2,1)S(1)}, bf16[192,384]{1,0:T(8,128)(2,1)S(1)}, u32[]{:S(2)}, u32[]{:S(2)}) collective-permute-start(bf16[192,384]{1,0:T(8,128)(2,1)S(1)} %bitcast.58), channel_id=1, source_target_pairs={{0,64},{64,128},{128,192},{192,0},{1,65},{65,129},{129,193},{193,1... | collective-permute-start | bytes 442376 | tf_op jit(solution)/shard_map/ppermute | solution.py:237
  33.6 3.5 %collective-permute-done.2 = bf16[192,384]{1,0:T(8,128)(2,1)S(1)} collective-permute-done((bf16[192,384]{1,0:T(8,128)(2,1)S(1)}, bf16[192,384]{1,0:T(8,128)(2,1)S(1)}, u32[]{:S(2)}, u32[]{:S(2)}) %collective-permute-start.2) | collective-permute-done | bytes 147488 | tf_op jit(solution)/shard_map/ppermute | solution.py:237
  37.1 5.1 %collective-permute-done.3 = bf16[192,384]{1,0:T(8,128)(2,1)S(1)} collective-permute-done((bf16[192,384]{1,0:T(8,128)(2,1)S(1)}, bf16[192,384]{1,0:T(8,128)(2,1)S(1)}, u32[]{:S(2)}, u32[]{:S(2)}) %collective-permute-start.3) | collective-permute-done | bytes 147488 | tf_op jit(solution)/shard_map/ppermute | solution.py:237
  42.3 1.6 collective-permute-start.5
  43.9 1.4 collective-permute-start.6
  45.4 0.7 collective-permute-start.7
  46.1 7.4 %collective-permute-done.5.w1_ref = bf16[768,384]{1,0:T(8,128)(2,1)S(1)} collective-permute-done((bf16[768,384]{1,0:T(8,128)(2,1)S(1)}, bf16[768,384]{1,0:T(8,128)(2,1)S(1)}, u32[]{:S(2)}, u32[]{:S(2)}) %collective-permute-start.5) | collective-permute-done | bytes 589856 | tf_op jit(solution)/shard_map/ppermute | solution.py:246
  53.4 4.3 %collective-permute-done.6.w3_ref = bf16[768,384]{1,0:T(8,128)(2,1)} collective-permute-done((bf16[768,384]{1,0:T(8,128)(2,1)S(1)}, bf16[768,384]{1,0:T(8,128)(2,1)}, u32[]{:S(2)}, u32[]{:S(2)}) %collective-permute-start.6) | collective-permute-done | bytes 589856 | tf_op jit(solution)/shard_map/ppermute | solution.py:246
  57.8 1.9 %collective-permute-start.8 = (bf16[4,256,768]{2,1,0:T(8,128)(2,1)}, bf16[4,256,768]{2,1,0:T(8,128)(2,1)}, u32[]{:S(2)}, u32[]{:S(2)}) collective-permute-start(bf16[4,256,768]{2,1,0:T(8,128)(2,1)} %bitcast.46), channel_id=1, source_target_pairs={{0,1},{1,0},{2,3},{3,2},{4,5},{5,4},{6,7},{7,6},{8,9},{9,8},{10,11... | collective-permute-start | bytes 4718600 | tf_op jit(solution)/shard_map/ppermute | solution.py:241
  59.8 1.2 collective-permute-start.9
  61.2 3.0 %shard_map.105.near_ref = f32[2,256,384]{2,1,0:T(8,128)S(1)} custom-call(s32[2]{0:T(128)S(1)} %pad_add_fusion.2.spot_ref, bf16[4,256,768]{2,1,0:T(8,128)(2,1)S(1)} %bitcast.44, bf16[4,256,768]{2,1,0:T(8,128)(2,1)} %collective-permute-done.n1_ref, bf16[768,384]{1,0:T(8,128)(2,1)S(1)} %bitcast.51, bf16[768,384]{1,0:T(8,128)(2,1)S(1)} %collective-permute-done.5.w1_ref, ...), custom_call_target="tpu_custom_call" | custom-call | flops 905969664 | bytes 6291456 | tf_op jit(solution)/shard_map/pallas_call | solution.py:83
  64.2 2.9 %shard_map.106.far_ref = f32[2,256,384]{2,1,0:T(8,128)S(1)} custom-call(s32[2]{0:T(128)S(1)} %pad_add_fusion.2.spot_ref, bf16[4,256,768]{2,1,0:T(8,128)(2,1)S(1)} %bitcast.47, bf16[4,256,768]{2,1,0:T(8,128)(2,1)} %collective-permute-done.8.n1_ref.n3_ref, bf16[768,384]{1,0:T(8,128)(2,1)S(1)} %bitcast.52, bf16[768,384]{1,0:T(8,128)(2,1)S(1)} %collective-permute-done.5.w1_ref, ...), custom_call_target="tpu_custom_call" | custom-call | flops 905969664 | bytes 6291456 | tf_op jit(solution)/shard_map/pallas_call | solution.py:83
  67.2 2.6 %collective-permute-done.9.w_ref = bf16[768,384]{1,0:T(8,128)(2,1)} collective-permute-done((bf16[768,384]{1,0:T(8,128)(2,1)S(1)}, bf16[768,384]{1,0:T(8,128)(2,1)}, u32[]{:S(2)}, u32[]{:S(2)}) %collective-permute-start.9) | collective-permute-done | bytes 589856 | tf_op jit(solution)/shard_map/ppermute | solution.py:246
  69.8 3.0 %shard_map.107 = (bf16[4,128,128]{2,1,0:T(8,128)(2,1)S(1)}, bf16[4,128,128]{2,1,0:T(8,128)(2,1)S(1)}, bf16[4,128,128]{2,1,0:T(8,128)(2,1)S(1)}, bf16[4,128,128]{...) custom-call(s32[5]{0:T(128)S(1)} %stack.92.spot_ref, ...), custom_call_target="tpu_custom_call" | custom-call | flops 603979776 | bytes 5242880 | tf_op jit(solution)/shard_map/pallas_call | solution.py:121
  72.8 3.6 %collective-permute-start.10 = (bf16[4,128,128]{2,1,0:T(8,128)(2,1)S(1)}, bf16[4,128,128]{2,1,0:T(8,128)(2,1)S(1)}, u32[]{:S(2)}, u32[]{:S(2)}) collective-permute-start(bf16[4,128,128]{2,1,0:T(8,128)(2,1)S(1)} %get-tuple-element.46), channel_id=1, source_target_pairs={{0,64},{64,128},{128,192},{192,0},{1,65},{65,129},{129,193},{193,1... | collective-permute-start | bytes 393224 | tf_op jit(solution)/shard_map/ppermute | solution.py:237
  76.4 0.8 collective-permute-start.11
  77.2 1.2 collective-permute-start.12
  79.2 1.6 collective-permute-done.10.refs_1_
  80.8 9.9 %collective-permute-done.11.refs_3_ = bf16[4,128,128]{2,1,0:T(8,128)(2,1)S(1)} collective-permute-done((bf16[4,128,128]{2,1,0:T(8,128)(2,1)S(1)}, bf16[4,128,128]{2,1,0:T(8,128)(2,1)S(1)}, u32[]{:S(2)}, u32[]{:S(2)}) %collective-permute-start.11) | collective-permute-done | bytes 131104 | tf_op jit(solution)/shard_map/ppermute | solution.py:237
  90.8 0.7 collective-permute-start.16
  91.5 0.9 collective-permute-start.18
  92.3 3.5 %collective-permute-start.15 = (bf16[4,128,128]{2,1,0:T(8,128)(2,1)S(1)}, bf16[4,128,128]{2,1,0:T(8,128)(2,1)S(1)}, u32[]{:S(2)}, u32[]{:S(2)}) collective-permute-start(bf16[4,128,128]{2,1,0:T(8,128)(2,1)S(1)} %get-tuple-element.54), channel_id=1, source_target_pairs={{0,128},{64,192},{128,0},{192,64},{1,129},{65,193},{129,1},{193,65... | collective-permute-start | bytes 393224 | tf_op jit(solution)/shard_map/ppermute | solution.py:237
  96.0 5.7 %collective-permute-done.15.refs_2_ = bf16[4,128,128]{2,1,0:T(8,128)(2,1)S(1)} collective-permute-done((bf16[4,128,128]{2,1,0:T(8,128)(2,1)S(1)}, bf16[4,128,128]{2,1,0:T(8,128)(2,1)S(1)}, u32[]{:S(2)}, u32[]{:S(2)}) %collective-permute-start.15) | collective-permute-done | bytes 131104 | tf_op jit(solution)/shard_map/ppermute | solution.py:237
  101.7 2.4 %collective-permute-start.19 = (bf16[4,128,128]{2,1,0:T(8,128)(2,1)S(1)}, bf16[4,128,128]{2,1,0:T(8,128)(2,1)S(1)}, u32[]{:S(2)}, u32[]{:S(2)}) collective-permute-start(bf16[4,128,128]{2,1,0:T(8,128)(2,1)S(1)} %collective-permute-done.15.refs_2_), channel_id=1, source_target_pairs={{0,48},{16,0},{32,16},{48,32},{1,49},{17,1},{33,17},{49,33},{2,50}... | collective-permute-start | bytes 393224 | tf_op jit(solution)/shard_map/ppermute | solution.py:237
  104.1 1.2 collective-permute-start.20
  105.5 1.0 collective-permute-start.21
  106.5 2.0 %collective-permute-done.18.refs_9_ = bf16[8,128,128]{2,1,0:T(8,128)(2,1)S(1)} collective-permute-done((bf16[8,128,128]{2,1,0:T(8,128)(2,1)S(1)}, bf16[8,128,128]{2,1,0:T(8,128)(2,1)S(1)}, u32[]{:S(2)}, u32[]{:S(2)}) %collective-permute-start.18) | collective-permute-done | bytes 262176 | tf_op jit(solution)/shard_map/ppermute | solution.py:237
  108.5 3.0 %collective-permute-start.23 = (bf16[2,128,128]{2,1,0:T(8,128)(2,1)S(1)}, bf16[2,128,128]{2,1,0:T(8,128)(2,1)S(1)}, u32[]{:S(2)}, u32[]{:S(2)}) collective-permute-start(bf16[2,128,128]{2,1,0:T(8,128)(2,1)S(1)} %get-tuple-element.61), channel_id=1, source_target_pairs={{0,128},{64,192},{128,0},{192,64},{1,129},{65,193},{129,1},{193,65... | collective-permute-start | bytes 196616 | tf_op jit(solution)/shard_map/ppermute | solution.py:237
  111.6 6.1 %collective-permute-done.23.refs_15_ = bf16[2,128,128]{2,1,0:T(8,128)(2,1)S(1)} collective-permute-done((bf16[2,128,128]{2,1,0:T(8,128)(2,1)S(1)}, bf16[2,128,128]{2,1,0:T(8,128)(2,1)S(1)}, u32[]{:S(2)}, u32[]{:S(2)}) %collective-permute-start.23) | collective-permute-done | bytes 65568 | tf_op jit(solution)/shard_map/ppermute | solution.py:237
  117.7 3.5 %shard_map.108 = (bf16[256,128]{1,0:T(8,128)(2,1)S(1)}, bf16[256,128]{1,0:T(8,128)(2,1)S(1)}, bf16[256,128]{1,0:T(8,128)(2,1)S(1)}, bf16[256,128]{1,0:T(8,128)(2,1)S(1)}) custom-call(s32[4]{0:T(128)S(1)} %pad_add_fusion.1.spot_ref, bf16[4,128,128]{2,1,0:T(8,128)(2,1)S(1)} %get-tuple-element.45.refs_0_, ...), custom_call_target="tpu_custom_call" | custom-call | flops 1610612736 | bytes 3145728 | tf_op jit(solution)/shard_map/pallas_call | solution.py:188
  121.2 10.6 %collective-permute-start.25 = (bf16[256,128]{1,0:T(8,128)(2,1)S(1)}, bf16[256,128]{1,0:T(8,128)(2,1)S(1)}, u32[]{:S(2)}, u32[]{:S(2)}) collective-permute-start(bf16[256,128]{1,0:T(8,128)(2,1)S(1)} %get-tuple-element.64), channel_id=1, source_target_pairs={{0,0},{1,64},{2,128},{3,192},{64,1},{65,65},{66,129},{67,193},{128... | collective-permute-start | bytes 196616 | tf_op jit(solution)/shard_map/ppermute | solution.py:326
  131.8 5.3 %collective-permute-start.26 = (bf16[256,128]{1,0:T(8,128)(2,1)S(1)}, bf16[256,128]{1,0:T(8,128)(2,1)S(1)}, u32[]{:S(2)}, u32[]{:S(2)}) collective-permute-start(bf16[256,128]{1,0:T(8,128)(2,1)S(1)} %get-tuple-element.65), channel_id=1, source_target_pairs={{0,64},{1,128},{2,192},{3,0},{64,65},{65,129},{66,193},{67,1},{128... | collective-permute-start | bytes 196616 | tf_op jit(solution)/shard_map/ppermute | solution.py:326
  137.6 0.8 collective-permute-done.26
  138.4 4.2 %collective-permute-done.27 = bf16[256,128]{1,0:T(8,128)(2,1)S(1)} collective-permute-done((bf16[256,128]{1,0:T(8,128)(2,1)S(1)}, bf16[256,128]{1,0:T(8,128)(2,1)S(1)}, u32[]{:S(2)}, u32[]{:S(2)}) %collective-permute-start.27) | collective-permute-done | bytes 65568 | tf_op jit(solution)/shard_map/ppermute | solution.py:326
  142.8 3.8 %collective-permute-start.29 = (bf16[4,256,128]{2,1,0:T(8,128)(2,1)S(1)}, bf16[4,256,128]{2,1,0:T(8,128)(2,1)S(1)}, u32[]{:S(2)}, u32[]{:S(2)}) collective-permute-start(bf16[4,256,128]{2,1,0:T(8,128)(2,1)S(1)} %pad_maximum_fusion.h0), channel_id=1, source_target_pairs={{0,12},{4,0},{8,4},{12,8},{1,13},{5,1},{9,5},{13,9},{2,14},{6,2},{... | collective-permute-start | bytes 786440 | tf_op jit(solution)/shard_map/ppermute | solution.py:237
  147.2 0.8 dynamic_slice.20
  148.1 1.0 constant_dynamic-slice_fusion
  149.1 8.2 %collective-permute-done.29.h1 = bf16[4,256,128]{2,1,0:T(8,128)(2,1)S(1)} collective-permute-done((bf16[4,256,128]{2,1,0:T(8,128)(2,1)S(1)}, bf16[4,256,128]{2,1,0:T(8,128)(2,1)S(1)}, u32[]{:S(2)}, u32[]{:S(2)}) %collective-permute-start.29) | collective-permute-done | bytes 262176 | tf_op jit(solution)/shard_map/ppermute | solution.py:237
  157.3 4.2 %collective-permute-done.31.h3 = bf16[4,256,128]{2,1,0:T(8,128)(2,1)S(1)} collective-permute-done((bf16[4,256,128]{2,1,0:T(8,128)(2,1)S(1)}, bf16[4,256,128]{2,1,0:T(8,128)(2,1)S(1)}, u32[]{:S(2)}, u32[]{:S(2)}) %collective-permute-start.31) | collective-permute-done | bytes 262176 | tf_op jit(solution)/shard_map/ppermute | solution.py:237
  161.5 1.4 copy-done.3
  162.9 2.3 %shard_map.109 = (bf16[128,768]{1,0:T(8,128)(2,1)}, bf16[128,768]{1,0:T(8,128)(2,1)}) custom-call(s32[3]{0:T(128)S(1)} %pad_add_fusion.place_ref, bf16[4,256,128]{2,1,0:T(8,128)(2,1)S(1)} %pad_maximum_fusion.h0, bf16[4,256,128]{2,1,0:T(8,128)(2,1)S(1)} %collective-permute-done.29.h1, bf16[4,256,128]{2,1,0:T(8,128)(2,1)S(1)} %collective-permute-done.30.h2, ...), custom_call_target="tpu_custom_call" | custom-call | flops 805306368 | bytes 6291456 | tf_op jit(solution)/shard_map/pallas_call | solution.py:224
  (68 shorter events, 3.4 us)
Async XLA Ops:
  7.2 6.9 %copy-start = (bf16[192,4,3,128]{3,1,2,0:T(4,128)(2,1)S(1)}, bf16[192,4,3,128]{3,1,2,0:T(4,128)(2,1)}, u32[]{:S(2)}) copy-start(bf16[192,4,3,128]{3,1,2,0:T(4,128)(2,1)} %param.11) | copy-start | bytes 1769476
  7.2 50.6 %all-gather.5.cloned.1.call-start = ((), (), s32[]{:S(2)}) async-start(), calls=%async_computation | async-start | bytes 1966080 | tf_op jit(solution)/shard_map/all_gather | solution.py:283
  10.8 14.1 %collective-permute-start = (bf16[4,256,768]{2,1,0:T(8,128)(2,1)}, bf16[4,256,768]{2,1,0:T(8,128)(2,1)}, u32[]{:S(2)}, u32[]{:S(2)}) collective-permute-start(bf16[4,256,768]{2,1,0:T(8,128)(2,1)} %bitcast.43), channel_id=1, source_target_pairs={{0,1},{1,0},{2,3},{3,2},{4,5},{5,4},{6,7},{7,6},{8,9},{9,8},{10,11... | collective-permute-start | bytes 4718600 | tf_op jit(solution)/shard_map/ppermute | solution.py:241
  14.1 10.9 %collective-permute-start.1 = (bf16[256,768]{1,0:T(8,128)(2,1)}, bf16[256,768]{1,0:T(8,128)(2,1)S(1)}, u32[]{:S(2)}, u32[]{:S(2)}) collective-permute-start(bf16[256,768]{1,0:T(8,128)(2,1)} %bitcast.70), channel_id=1, source_target_pairs={{0,2},{2,0},{1,3},{3,1},{4,6},{6,4},{5,7},{7,5},{8,10},{10,8},{9,1... | collective-permute-start | bytes 1179656 | tf_op jit(solution)/shard_map/ppermute | solution.py:241
  14.1 31.1 %copy-start.6 = (bf16[192,4,128]{2,1,0:T(4,128)(2,1)S(1)}, bf16[192,4,128]{2,1,0:T(4,128)(2,1)}, u32[]{:S(2)}) copy-start(bf16[192,4,128]{2,1,0:T(4,128)(2,1)} %param.12) | copy-start | bytes 589828
  15.1 46.1 %copy-start.7 = (f32[128]{0:T(128)S(1)}, f32[128]{0:T(128)}, u32[]{:S(2)}) copy-start(f32[128]{0:T(128)} %param.17) | copy-start | bytes 1540
  15.1 46.1 %copy-start.8 = (f32[128]{0:T(128)S(1)}, f32[128]{0:T(128)}, u32[]{:S(2)}) copy-start(f32[128]{0:T(128)} %param.16) | copy-start | bytes 1540
  15.1 46.1 %copy-start.1 = (bf16[4,2,128,768]{3,2,1,0:T(8,128)(2,1)S(1)}, bf16[4,2,128,768]{3,2,1,0:T(8,128)(2,1)}, u32[]{:S(2)}) copy-start(bf16[4,2,128,768]{3,2,1,0:T(8,128)(2,1)} %get-tuple-element.36) | copy-start | bytes 4718596
  25.0 0.8 copy-start.4
  25.8 116.9 %all-gather.7.cloned.1.call-start = ((), (), s32[]{:S(2)}) async-start(), calls=%async_computation.1 | async-start | bytes 1671168 | tf_op jit(solution)/shard_map/all_gather | solution.py:303
  25.9 11.2 %collective-permute-start.2 = (bf16[192,384]{1,0:T(8,128)(2,1)S(1)}, bf16[192,384]{1,0:T(8,128)(2,1)S(1)}, u32[]{:S(2)}, u32[]{:S(2)}) collective-permute-start(bf16[192,384]{1,0:T(8,128)(2,1)S(1)} %bitcast.56), channel_id=1, source_target_pairs={{0,192},{64,0},{128,64},{192,128},{1,193},{65,1},{129,65},{193,129... | collective-permute-start | bytes 442376 | tf_op jit(solution)/shard_map/ppermute | solution.py:237
  30.2 12.0 %collective-permute-start.3 = (bf16[192,384]{1,0:T(8,128)(2,1)S(1)}, bf16[192,384]{1,0:T(8,128)(2,1)S(1)}, u32[]{:S(2)}, u32[]{:S(2)}) collective-permute-start(bf16[192,384]{1,0:T(8,128)(2,1)S(1)} %bitcast.57), channel_id=1, source_target_pairs={{0,128},{64,192},{128,0},{192,64},{1,129},{65,193},{129,1},{193,65... | collective-permute-start | bytes 442376 | tf_op jit(solution)/shard_map/ppermute | solution.py:237
  31.2 11.0 %collective-permute-start.4 = (bf16[192,384]{1,0:T(8,128)(2,1)S(1)}, bf16[192,384]{1,0:T(8,128)(2,1)S(1)}, u32[]{:S(2)}, u32[]{:S(2)}) collective-permute-start(bf16[192,384]{1,0:T(8,128)(2,1)S(1)} %bitcast.58), channel_id=1, source_target_pairs={{0,64},{64,128},{128,192},{192,0},{1,65},{65,129},{129,193},{193,1... | collective-permute-start | bytes 442376 | tf_op jit(solution)/shard_map/ppermute | solution.py:237
  42.3 11.1 %collective-permute-start.5 = (bf16[768,384]{1,0:T(8,128)(2,1)S(1)}, bf16[768,384]{1,0:T(8,128)(2,1)S(1)}, u32[]{:S(2)}, u32[]{:S(2)}) collective-permute-start(bf16[768,384]{1,0:T(8,128)(2,1)S(1)} %bitcast.49), channel_id=1, source_target_pairs={{0,48},{1,17},{16,0},{17,33},{32,16},{33,49},{48,32},{49,1},{2,50}... | collective-permute-start | bytes 1769480 | tf_op jit(solution)/shard_map/ppermute | solution.py:246
  43.9 13.9 %collective-permute-start.6 = (bf16[768,384]{1,0:T(8,128)(2,1)S(1)}, bf16[768,384]{1,0:T(8,128)(2,1)}, u32[]{:S(2)}, u32[]{:S(2)}) collective-permute-start(bf16[768,384]{1,0:T(8,128)(2,1)S(1)} %bitcast.50), channel_id=1, source_target_pairs={{0,16},{1,49},{16,32},{17,1},{32,48},{33,17},{48,0},{49,33},{2,18}... | collective-permute-start | bytes 1769480 | tf_op jit(solution)/shard_map/ppermute | solution.py:246
  45.4 0.7 collective-permute-start.7
  46.0 11.7 %copy-start.5 = (bf16[192,256]{1,0:T(8,128)(2,1)}, bf16[192,256]{1,0:T(8,128)(2,1)S(1)}, u32[]{:S(2)}) copy-start(bf16[192,256]{1,0:T(8,128)(2,1)S(1)} %collective-permute-done.7) | copy-start | bytes 294916
  57.8 6.4 %collective-permute-start.8 = (bf16[4,256,768]{2,1,0:T(8,128)(2,1)}, bf16[4,256,768]{2,1,0:T(8,128)(2,1)}, u32[]{:S(2)}, u32[]{:S(2)}) collective-permute-start(bf16[4,256,768]{2,1,0:T(8,128)(2,1)} %bitcast.46), channel_id=1, source_target_pairs={{0,1},{1,0},{2,3},{3,2},{4,5},{5,4},{6,7},{7,6},{8,9},{9,8},{10,11... | collective-permute-start | bytes 4718600 | tf_op jit(solution)/shard_map/ppermute | solution.py:241
  59.8 10.1 %collective-permute-start.9 = (bf16[768,384]{1,0:T(8,128)(2,1)S(1)}, bf16[768,384]{1,0:T(8,128)(2,1)}, u32[]{:S(2)}, u32[]{:S(2)}) collective-permute-start(bf16[768,384]{1,0:T(8,128)(2,1)S(1)} %collective-permute-done.5.w1_ref), channel_id=1, source_target_pairs={{0,48},{1,17},{16,0},{17,33},{32,16},{33,49},{48,32},{49,1},{2,50}... | collective-permute-start | bytes 1769480 | tf_op jit(solution)/shard_map/ppermute | solution.py:246
  61.2 3.1 %copy-start.2 = (bf16[1024,768]{1,0:T(8,128)(2,1)S(1)}, bf16[1024,768]{1,0:T(8,128)(2,1)}, u32[]{:S(2)}) copy-start(bf16[1024,768]{1,0:T(8,128)(2,1)} %all-gather.5.cloned.1.call-done) | copy-start | bytes 4718596
  72.8 8.0 %collective-permute-start.10 = (bf16[4,128,128]{2,1,0:T(8,128)(2,1)S(1)}, bf16[4,128,128]{2,1,0:T(8,128)(2,1)S(1)}, u32[]{:S(2)}, u32[]{:S(2)}) collective-permute-start(bf16[4,128,128]{2,1,0:T(8,128)(2,1)S(1)} %get-tuple-element.46), channel_id=1, source_target_pairs={{0,64},{64,128},{128,192},{192,0},{1,65},{65,129},{129,193},{193,1... | collective-permute-start | bytes 393224 | tf_op jit(solution)/shard_map/ppermute | solution.py:237
  76.4 14.4 %collective-permute-start.11 = (bf16[4,128,128]{2,1,0:T(8,128)(2,1)S(1)}, bf16[4,128,128]{2,1,0:T(8,128)(2,1)S(1)}, u32[]{:S(2)}, u32[]{:S(2)}) collective-permute-start(bf16[4,128,128]{2,1,0:T(8,128)(2,1)S(1)} %get-tuple-element.47), channel_id=1, source_target_pairs={{0,192},{64,0},{128,64},{192,128},{1,193},{65,1},{129,65},{193,129... | collective-permute-start | bytes 393224 | tf_op jit(solution)/shard_map/ppermute | solution.py:237
  77.2 13.6 %collective-permute-start.12 = (bf16[4,128,128]{2,1,0:T(8,128)(2,1)S(1)}, bf16[4,128,128]{2,1,0:T(8,128)(2,1)S(1)}, u32[]{:S(2)}, u32[]{:S(2)}) collective-permute-start(bf16[4,128,128]{2,1,0:T(8,128)(2,1)S(1)} %get-tuple-element.45.refs_0_), channel_id=1, source_target_pairs={{0,48},{16,0},{32,16},{48,32},{1,49},{17,1},{33,17},{49,33},{2,50}... | collective-permute-start | bytes 393224 | tf_op jit(solution)/shard_map/ppermute | solution.py:237
  78.3 12.4 %collective-permute-start.13 = (bf16[4,128,128]{2,1,0:T(8,128)(2,1)S(1)}, bf16[4,128,128]{2,1,0:T(8,128)(2,1)S(1)}, u32[]{:S(2)}, u32[]{:S(2)}) collective-permute-start(bf16[4,128,128]{2,1,0:T(8,128)(2,1)S(1)} %get-tuple-element.45.refs_0_), channel_id=1, source_target_pairs={{0,32},{16,48},{32,0},{48,16},{1,33},{17,49},{33,1},{49,17},{2,34}... | collective-permute-start | bytes 393224 | tf_op jit(solution)/shard_map/ppermute | solution.py:237
  78.7 12.0 %collective-permute-start.14 = (bf16[4,128,128]{2,1,0:T(8,128)(2,1)S(1)}, bf16[4,128,128]{2,1,0:T(8,128)(2,1)S(1)}, u32[]{:S(2)}, u32[]{:S(2)}) collective-permute-start(bf16[4,128,128]{2,1,0:T(8,128)(2,1)S(1)} %get-tuple-element.45.refs_0_), channel_id=1, source_target_pairs={{0,16},{16,32},{32,48},{48,0},{1,17},{17,33},{33,49},{49,1},{2,18}... | collective-permute-start | bytes 393224 | tf_op jit(solution)/shard_map/ppermute | solution.py:237
  90.8 10.9 %collective-permute-start.16 = (bf16[8,128,128]{2,1,0:T(8,128)(2,1)S(1)}, bf16[8,128,128]{2,1,0:T(8,128)(2,1)S(1)}, u32[]{:S(2)}, u32[]{:S(2)}) collective-permute-start(bf16[8,128,128]{2,1,0:T(8,128)(2,1)S(1)} %constant_dynamic-update-slice_fusion), channel_id=1, source_target_pairs={{0,48},{16,0},{32,16},{48,32},{1,49},{17,1},{33,17},{49,33},{2,50}... | collective-permute-start | bytes 786440 | tf_op jit(solution)/shard_map/ppermute | solution.py:237
  91.5 15.1 %collective-permute-start.17 = (bf16[8,128,128]{2,1,0:T(8,128)(2,1)S(1)}, bf16[8,128,128]{2,1,0:T(8,128)(2,1)S(1)}, u32[]{:S(2)}, u32[]{:S(2)}) collective-permute-start(bf16[8,128,128]{2,1,0:T(8,128)(2,1)S(1)} %constant_dynamic-update-slice_fusion), channel_id=1, source_target_pairs={{0,32},{16,48},{32,0},{48,16},{1,33},{17,49},{33,1},{49,17},{2,34}... | collective-permute-start | bytes 786440 | tf_op jit(solution)/shard_map/ppermute | solution.py:237
  91.5 17.0 %collective-permute-start.18 = (bf16[8,128,128]{2,1,0:T(8,128)(2,1)S(1)}, bf16[8,128,128]{2,1,0:T(8,128)(2,1)S(1)}, u32[]{:S(2)}, u32[]{:S(2)}) collective-permute-start(bf16[8,128,128]{2,1,0:T(8,128)(2,1)S(1)} %constant_dynamic-update-slice_fusion), channel_id=1, source_target_pairs={{0,16},{16,32},{32,48},{48,0},{1,17},{17,33},{33,49},{49,1},{2,18}... | collective-permute-start | bytes 786440 | tf_op jit(solution)/shard_map/ppermute | solution.py:237
  92.3 9.3 %collective-permute-start.15 = (bf16[4,128,128]{2,1,0:T(8,128)(2,1)S(1)}, bf16[4,128,128]{2,1,0:T(8,128)(2,1)S(1)}, u32[]{:S(2)}, u32[]{:S(2)}) collective-permute-start(bf16[4,128,128]{2,1,0:T(8,128)(2,1)S(1)} %get-tuple-element.54), channel_id=1, source_target_pairs={{0,128},{64,192},{128,0},{192,64},{1,129},{65,193},{129,1},{193,65... | collective-permute-start | bytes 393224 | tf_op jit(solution)/shard_map/ppermute | solution.py:237
  95.8 9.7 %collective-permute-start.22 = (bf16[2,128,128]{2,1,0:T(8,128)(2,1)S(1)}, bf16[2,128,128]{2,1,0:T(8,128)(2,1)S(1)}, u32[]{:S(2)}, u32[]{:S(2)}) collective-permute-start(bf16[2,128,128]{2,1,0:T(8,128)(2,1)S(1)} %get-tuple-element.59), channel_id=1, source_target_pairs={{0,64},{64,128},{128,192},{192,0},{1,65},{65,129},{129,193},{193,1... | collective-permute-start | bytes 196616 | tf_op jit(solution)/shard_map/ppermute | solution.py:237
  101.7 16.0 %collective-permute-start.19 = (bf16[4,128,128]{2,1,0:T(8,128)(2,1)S(1)}, bf16[4,128,128]{2,1,0:T(8,128)(2,1)S(1)}, u32[]{:S(2)}, u32[]{:S(2)}) collective-permute-start(bf16[4,128,128]{2,1,0:T(8,128)(2,1)S(1)} %collective-permute-done.15.refs_2_), channel_id=1, source_target_pairs={{0,48},{16,0},{32,16},{48,32},{1,49},{17,1},{33,17},{49,33},{2,50}... | collective-permute-start | bytes 393224 | tf_op jit(solution)/shard_map/ppermute | solution.py:237
  104.1 13.7 %collective-permute-start.20 = (bf16[4,128,128]{2,1,0:T(8,128)(2,1)S(1)}, bf16[4,128,128]{2,1,0:T(8,128)(2,1)S(1)}, u32[]{:S(2)}, u32[]{:S(2)}) collective-permute-start(bf16[4,128,128]{2,1,0:T(8,128)(2,1)S(1)} %collective-permute-done.15.refs_2_), channel_id=1, source_target_pairs={{0,32},{16,48},{32,0},{48,16},{1,33},{17,49},{33,1},{49,17},{2,34}... | collective-permute-start | bytes 393224 | tf_op jit(solution)/shard_map/ppermute | solution.py:237
  105.5 12.2 %collective-permute-start.21 = (bf16[4,128,128]{2,1,0:T(8,128)(2,1)S(1)}, bf16[4,128,128]{2,1,0:T(8,128)(2,1)S(1)}, u32[]{:S(2)}, u32[]{:S(2)}) collective-permute-start(bf16[4,128,128]{2,1,0:T(8,128)(2,1)S(1)} %collective-permute-done.15.refs_2_), channel_id=1, source_target_pairs={{0,16},{16,32},{32,48},{48,0},{1,17},{17,33},{33,49},{49,1},{2,18}... | collective-permute-start | bytes 393224 | tf_op jit(solution)/shard_map/ppermute | solution.py:237
  106.5 5.1 %collective-permute-start.24 = (bf16[2,128,128]{2,1,0:T(8,128)(2,1)S(1)}, bf16[2,128,128]{2,1,0:T(8,128)(2,1)S(1)}, u32[]{:S(2)}, u32[]{:S(2)}) collective-permute-start(bf16[2,128,128]{2,1,0:T(8,128)(2,1)S(1)} %get-tuple-element.63), channel_id=1, source_target_pairs={{0,192},{64,0},{128,64},{192,128},{1,193},{65,1},{129,65},{193,129... | collective-permute-start | bytes 196616 | tf_op jit(solution)/shard_map/ppermute | solution.py:237
  108.5 9.2 %collective-permute-start.23 = (bf16[2,128,128]{2,1,0:T(8,128)(2,1)S(1)}, bf16[2,128,128]{2,1,0:T(8,128)(2,1)S(1)}, u32[]{:S(2)}, u32[]{:S(2)}) collective-permute-start(bf16[2,128,128]{2,1,0:T(8,128)(2,1)S(1)} %get-tuple-element.61), channel_id=1, source_target_pairs={{0,128},{64,192},{128,0},{192,64},{1,129},{65,193},{129,1},{193,65... | collective-permute-start | bytes 196616 | tf_op jit(solution)/shard_map/ppermute | solution.py:237
  121.2 16.3 %collective-permute-start.25 = (bf16[256,128]{1,0:T(8,128)(2,1)S(1)}, bf16[256,128]{1,0:T(8,128)(2,1)S(1)}, u32[]{:S(2)}, u32[]{:S(2)}) collective-permute-start(bf16[256,128]{1,0:T(8,128)(2,1)S(1)} %get-tuple-element.64), channel_id=1, source_target_pairs={{0,0},{1,64},{2,128},{3,192},{64,1},{65,65},{66,129},{67,193},{128... | collective-permute-start | bytes 196616 | tf_op jit(solution)/shard_map/ppermute | solution.py:326
  131.8 6.6 %collective-permute-start.26 = (bf16[256,128]{1,0:T(8,128)(2,1)S(1)}, bf16[256,128]{1,0:T(8,128)(2,1)S(1)}, u32[]{:S(2)}, u32[]{:S(2)}) collective-permute-start(bf16[256,128]{1,0:T(8,128)(2,1)S(1)} %get-tuple-element.65), channel_id=1, source_target_pairs={{0,64},{1,128},{2,192},{3,0},{64,65},{65,129},{66,193},{67,1},{128... | collective-permute-start | bytes 196616 | tf_op jit(solution)/shard_map/ppermute | solution.py:326
  137.1 5.5 %collective-permute-start.27 = (bf16[256,128]{1,0:T(8,128)(2,1)S(1)}, bf16[256,128]{1,0:T(8,128)(2,1)S(1)}, u32[]{:S(2)}, u32[]{:S(2)}) collective-permute-start(bf16[256,128]{1,0:T(8,128)(2,1)S(1)} %get-tuple-element.66), channel_id=1, source_target_pairs={{0,128},{1,192},{2,0},{3,64},{64,129},{65,193},{66,1},{67,65},{128... | collective-permute-start | bytes 196616 | tf_op jit(solution)/shard_map/ppermute | solution.py:326
  137.1 5.5 %collective-permute-start.28 = (bf16[256,128]{1,0:T(8,128)(2,1)S(1)}, bf16[256,128]{1,0:T(8,128)(2,1)S(1)}, u32[]{:S(2)}, u32[]{:S(2)}) collective-permute-start(bf16[256,128]{1,0:T(8,128)(2,1)S(1)} %get-tuple-element.67), channel_id=1, source_target_pairs={{0,192},{1,0},{2,64},{3,128},{64,193},{65,1},{66,65},{67,129},{128... | collective-permute-start | bytes 196616 | tf_op jit(solution)/shard_map/ppermute | solution.py:326
  142.7 18.9 %collective-permute-start.32 = (bf16[4,4,192,256]{3,2,1,0:T(8,128)(2,1)}, bf16[4,4,192,256]{3,2,1,0:T(8,128)(2,1)S(1)}, u32[]{:S(2)}, u32[]{:S(2)}) collective-permute-start(bf16[4,4,192,256]{3,2,1,0:T(8,128)(2,1)} %bitcast.53), channel_id=1, source_target_pairs={{0,1},{1,0},{2,3},{3,2},{4,5},{5,4},{6,7},{7,6},{8,9},{9,8},{10,11... | collective-permute-start | bytes 4718600 | tf_op jit(solution)/shard_map/ppermute | solution.py:241
  142.8 14.5 %collective-permute-start.29 = (bf16[4,256,128]{2,1,0:T(8,128)(2,1)S(1)}, bf16[4,256,128]{2,1,0:T(8,128)(2,1)S(1)}, u32[]{:S(2)}, u32[]{:S(2)}) collective-permute-start(bf16[4,256,128]{2,1,0:T(8,128)(2,1)S(1)} %pad_maximum_fusion.h0), channel_id=1, source_target_pairs={{0,12},{4,0},{8,4},{12,8},{1,13},{5,1},{9,5},{13,9},{2,14},{6,2},{... | collective-permute-start | bytes 786440 | tf_op jit(solution)/shard_map/ppermute | solution.py:237
  146.6 10.7 %collective-permute-start.30 = (bf16[4,256,128]{2,1,0:T(8,128)(2,1)S(1)}, bf16[4,256,128]{2,1,0:T(8,128)(2,1)S(1)}, u32[]{:S(2)}, u32[]{:S(2)}) collective-permute-start(bf16[4,256,128]{2,1,0:T(8,128)(2,1)S(1)} %pad_maximum_fusion.h0), channel_id=1, source_target_pairs={{0,8},{4,12},{8,0},{12,4},{1,9},{5,13},{9,1},{13,5},{2,10},{6,14},... | collective-permute-start | bytes 786440 | tf_op jit(solution)/shard_map/ppermute | solution.py:237
  146.7 14.9 %collective-permute-start.31 = (bf16[4,256,128]{2,1,0:T(8,128)(2,1)S(1)}, bf16[4,256,128]{2,1,0:T(8,128)(2,1)S(1)}, u32[]{:S(2)}, u32[]{:S(2)}) collective-permute-start(bf16[4,256,128]{2,1,0:T(8,128)(2,1)S(1)} %pad_maximum_fusion.h0), channel_id=1, source_target_pairs={{0,4},{4,8},{8,12},{12,0},{1,5},{5,9},{9,13},{13,1},{2,6},{6,10},{... | collective-permute-start | bytes 786440 | tf_op jit(solution)/shard_map/ppermute | solution.py:237
  161.5 1.4 copy-start.3
Sparse Core Ops, SparseCore 0:
  25.9 30.5 all-gather.4
  59.4 63.2 all-gather.6
